TPU v7x, 256 devices: a whole 4x4x8 slice. The times are simulated.
256 devices in a mesh: section: 2 (over x_lo), dp: 4 (over y), mp: 32 (over z, x_hi, core).
Axes of the slice: x: 4 (x_hi: 2, x_lo: 2; x = x_hi * 2 + x_lo), y: 4, z: 8, core: 2. Of those that a mesh axis runs over, the one named last changes fastest.
Arguments:
- section_input: bfloat16 [2, 256, 8192], P('section', 'mp', 'dp')
- saved_input: bfloat16 [2, 256, 8192], P('section', 'mp', 'dp')
- cotangent: bfloat16 [2, 256, 8192], P('section', 'mp', 'dp'), may hold values from -6 to 6
- norm_gain: float32 [2, 8192], P('section', 'dp'), may hold values from 0.3 to 2.5
- norm_shift: float32 [2, 8192], P('section', 'dp'), may hold values from -3 to 3
- up_weight: bfloat16 [2, 8192, 16384], P('section', 'dp', 'mp'), may hold values from -0.0625 to 0.0625
- up_bias: float32 [2, 16384], P('section', 'mp'), may hold values from -3 to 3
- down_weight: bfloat16 [2, 16384, 8192], P('section', 'mp', 'dp'), may hold values from -0.046875 to 0.046875
- down_bias: float32 [2, 8192], P('section', 'dp'), may hold values from -3 to 3
Outputs:
- sent_forward: bfloat16 [2, 256, 8192], P('section', None, ('dp', 'mp'))
- sent_backward: bfloat16 [2, 256, 8192], P('section', None, ('dp', 'mp'))
- up_weight_grad: bfloat16 [2, 8192, 16384], P('section', 'dp', 'mp')
- up_bias_grad: float32 [2, 16384], P('section', 'mp')
- down_weight_grad: bfloat16 [2, 16384, 8192], P('section', 'mp', 'dp')
- down_bias_grad: float32 [2, 8192], P('section', 'dp')
- gain_grad: float32 [2, 8192], P('section', 'dp')
- shift_grad: float32 [2, 8192], P('section', 'dp')
All inputs are finite; a program needn't handle non-finite values.
Results may differ from a plain program's by a relative error of at most 0.007.
Values may be sent and summed in bfloat16 or wider, within the bound.
No kernel may reach another device: no remote copies, remote signals or barrier semaphores. Data moves between devices by JAX's collectives and lax.ppermute only.
A program may use at most 64 MiB of HBM per device.

v0:
```python
import jax
import jax.numpy as jnp
from jax import lax
from jax.sharding import PartitionSpec as P

D = 8192


EPS = 1e-05
COEF_A = 0.7978845608028654
COEF_B = 0.044715


def passed_along(value, axis, steps):
    count = lax.axis_size(axis)
    pairs = [(source, (source + steps) % count) for source in range(count)]
    return lax.ppermute(value, axis, pairs)


def gelu_value(value):
    inner = jnp.tanh(COEF_A * (value + COEF_B * value * value * value))
    return 0.5 * value * (1.0 + inner)


def gelu_slope(value):
    inner = jnp.tanh(COEF_A * (value + COEF_B * value * value * value))
    return 0.5 * (1.0 + inner) + 0.5 * value * (1.0 - inner * inner) * COEF_A * (
        1.0 + 3.0 * COEF_B * value * value
    )


def normalize(gathered, gain, shift):
    values = gathered.astype(jnp.float32)
    sums = lax.psum((jnp.sum(values, 1), jnp.sum(values * values, 1)), "dp")
    mean_row = sums[0] / D
    square_row = sums[1] / D
    rstd_row = lax.rsqrt(square_row - mean_row * mean_row + EPS)
    centered = (values - mean_row[:, None]) * rstd_row[:, None]
    normed = (centered * gain + shift).astype(jnp.bfloat16)
    return (normed, centered, rstd_row)


def local(
    section_input,
    saved_input,
    cotangent,
    norm_gain,
    norm_shift,
    up_weight,
    up_bias,
    down_weight,
    down_bias,
):
    gain, shift = (norm_gain[0], norm_shift[0])
    w_up, w_down = (up_weight[0], down_weight[0])
    bias_up, bias_down = (up_bias[0], down_bias[0])
    shard_rows = section_input.shape[1]
    start_row = lax.axis_index("mp") * shard_rows
    width_piece = section_input.shape[2] // lax.axis_size("mp")
    start_column = lax.axis_index("mp") * width_piece
    gathered = lax.all_gather(section_input[0], "mp", axis=0, tiled=True)
    normed, _, _ = normalize(gathered, gain, shift)
    partial_up = jnp.dot(normed, w_up, preferred_element_type=jnp.float32)
    pre = lax.psum(partial_up, "dp") + bias_up
    activated = gelu_value(pre).astype(jnp.bfloat16)
    full_branch = lax.psum(jnp.dot(activated, w_down, preferred_element_type=jnp.float32), "mp")
    branch = lax.dynamic_slice_in_dim(full_branch, start_row, shard_rows, 0)
    result = (section_input[0].astype(jnp.float32) + branch + bias_down).astype(jnp.bfloat16)
    whole_out = lax.all_gather(result, "mp", axis=0, tiled=True)
    out_columns = lax.dynamic_slice_in_dim(whole_out, start_column, width_piece, 1)
    forward_arrived = passed_along(out_columns, "section", 1)
    saved_full, grad_full = (
        lax.all_gather(saved_input[0], "mp", axis=0, tiled=True),
        lax.all_gather(cotangent[0], "mp", axis=0, tiled=True),
    )
    normed_saved, centered, rstd_row = normalize(saved_full, gain, shift)
    partial_pre = jnp.dot(normed_saved, w_up, preferred_element_type=jnp.float32)
    partial_back = lax.dot_general(
        grad_full, w_down, (((1,), (1,)), ((), ())), preferred_element_type=jnp.float32
    )
    summed = lax.psum((partial_pre, partial_back), "dp")
    pre_saved = summed[0] + bias_up
    grad_pre = (summed[1] * gelu_slope(pre_saved)).astype(jnp.bfloat16)
    act_saved = gelu_value(pre_saved).astype(jnp.bfloat16)
    down_weight_grad = lax.dot_general(
        act_saved, grad_full, (((0,), (0,)), ((), ())), preferred_element_type=jnp.float32
    ).astype(jnp.bfloat16)
    down_bias_grad = jnp.sum(grad_full.astype(jnp.float32), 0)
    up_weight_grad = lax.dot_general(
        normed_saved, grad_pre, (((0,), (0,)), ((), ())), preferred_element_type=jnp.float32
    ).astype(jnp.bfloat16)
    up_bias_grad = jnp.sum(grad_pre.astype(jnp.float32), 0)
    full_normed = lax.dot_general(
        grad_pre, w_up, (((1,), (1,)), ((), ())), preferred_element_type=jnp.float32
    )
    full_normed = lax.psum(full_normed, "mp")
    grad_normed = lax.dynamic_slice_in_dim(full_normed, start_row, shard_rows, 0)
    centered_rows = lax.dynamic_slice_in_dim(centered, start_row, shard_rows, 0)
    rstd_rows = lax.dynamic_slice_in_dim(rstd_row, start_row, shard_rows, 0)
    scaled = grad_normed * gain
    moments = lax.psum((jnp.sum(scaled, 1), jnp.sum(scaled * centered_rows, 1)), "dp")
    first = moments[0][:, None] / D
    second = moments[1][:, None] / D
    grad_in = cotangent[0].astype(jnp.float32) + rstd_rows[:, None] * (
        scaled - first - centered_rows * second
    )
    grad_in = grad_in.astype(jnp.bfloat16)
    gain_grad, shift_grad = lax.psum(
        (jnp.sum(grad_normed * centered_rows, 0), jnp.sum(grad_normed, 0)), "mp"
    )
    whole_grad = lax.all_gather(grad_in, "mp", axis=0, tiled=True)
    grad_columns = lax.dynamic_slice_in_dim(whole_grad, start_column, width_piece, 1)
    backward_arrived = passed_along(grad_columns, "section", -1)
    return (
        forward_arrived[None],
        backward_arrived[None],
        up_weight_grad[None],
        up_bias_grad[None],
        down_weight_grad[None],
        down_bias_grad[None],
        gain_grad[None],
        shift_grad[None],
    )


def solution(mesh):
    placed = (
        P("section", "mp", "dp"),
        P("section", "mp", "dp"),
        P("section", "mp", "dp"),
        P("section", "dp"),
        P("section", "dp"),
        P("section", "dp", "mp"),
        P("section", "mp"),
        P("section", "mp", "dp"),
        P("section", "dp"),
    )
    return jax.shard_map(
        local,
        mesh=mesh,
        in_specs=placed,
        out_specs=(
            P("section", None, ("dp", "mp")),
            P("section", None, ("dp", "mp")),
            P("section", "dp", "mp"),
            P("section", "mp"),
            P("section", "mp", "dp"),
            P("section", "dp"),
            P("section", "dp"),
            P("section", "dp"),
        ),
        check_vma=False,
    )
```

profile of v0, /device:TPU:1, one launch (start us, length us, event | category | flops | bytes accessed | tf_op | source)
XLA Modules:
  0.0 896.2 jit_solution(9905936853502147587)
XLA Ops:
  7.2 0.7 all-gather.15.cloned.1.call-update
  8.0 0.7 all-gather.13.cloned.1.call-update
  8.7 0.7 all-gather.17.cloned.1.call-update
  9.5 83.1 %all-gather.15.cloned.1.call-done = bf16[1,256,2048]{2,1,0:T(8,128)(2,1)} async-done(((bf16[1,8,2048]{2,1,0:T(8,128)(2,1)}), bf16[1,256,2048]{2,1,0:T(8,128)(2,1)}) %all-gather.15.cloned.1.call-update) | async-done | bytes 1048592 | tf_op jit(solution)/shard_map/all_gather | solution.py:73
  92.6 1.5 convert_reduce_fusion
  94.1 75.7 %all-gather.13.cloned.1.call-done = bf16[1,256,2048]{2,1,0:T(8,128)(2,1)} async-done(((bf16[1,8,2048]{2,1,0:T(8,128)(2,1)}), bf16[1,256,2048]{2,1,0:T(8,128)(2,1)}) %all-gather.13.cloned.1.call-update) | async-done | bytes 1048592 | tf_op jit(solution)/shard_map/all_gather | solution.py:61
  169.8 1.5 convert_reduce_fusion.1
  171.9 8.5 all-reduce.3
  180.4 1.6 fusion.19
  182.0 1.6 fusion.21
  183.6 63.5 %all-gather.17.cloned.1.call-done = bf16[1,256,2048]{2,1,0:T(8,128)(2,1)} async-done(((bf16[1,8,2048]{2,1,0:T(8,128)(2,1)}), bf16[1,256,2048]{2,1,0:T(8,128)(2,1)}) %all-gather.17.cloned.1.call-update) | async-done | bytes 1048592 | tf_op jit(solution)/shard_map/all_gather | solution.py:74
  247.0 3.5 fusion.13
  250.6 52.4 %all-reduce.10.cloned.1.call-done = (f32[256,512]{1,0:T(8,128)}, f32[256,512]{1,0:T(8,128)}, f32[256,512]{1,0:T(8,128)}) async-done(((f32[256,512]{1,0:T(8,128)}, f32[256,512]{1,0:T(8,128)}, f32[256,512]{1,0:T(8,128)}), (f32[256,512]{1,0:T(8,128)}, f32[256,512]{1,0:T(8,128)}, f32[256,512]{1,0:T(8,128)})) %all-reduce.10.cloned.1.call-update) | async-done | bytes 1572880 | tf_op jit(solution)/shard_map/psum | solution.py:64
  303.0 2.2 convert_reduce_fusion.3
  305.2 2.1 fusion.17
  307.2 2.1 fusion.15
  309.6 1.6 fusion.12
  311.2 281.1 %all-reduce.8.cloned.1.call-done = (f32[256,2048]{1,0:T(8,128)}, f32[256,2048]{1,0:T(8,128)}) async-done(((f32[256,2048]{1,0:T(8,128)}, f32[256,2048]{1,0:T(8,128)}), (f32[256,2048]{1,0:T(8,128)}, f32[256,2048]{1,0:T(8,128)})) %all-reduce.8.cloned.1.call-update) | async-done | bytes 4194320 | tf_op jit(solution)/shard_map/psum | solution.py:66
  592.3 1.1 multiply_reduce_fusion
  593.4 7.4 all-reduce.2
  600.8 1.6 fusion.53
  602.5 1.5 fusion.55
  604.0 2.0 convert_reduce_fusion.2
  606.0 2.3 fusion
  608.2 71.2 %all-gather.11.cloned.1.call-done = bf16[256,2048]{1,0:T(8,128)(2,1)} async-done(((bf16[8,2048]{1,0:T(8,128)(2,1)}), bf16[256,2048]{1,0:T(8,128)(2,1)}) %all-gather.11.cloned.1.call-update) | async-done | bytes 1048592 | tf_op jit(solution)/shard_map/all_gather | solution.py:111
  679.4 0.9 constant_dynamic-slice_fusion
  680.7 76.5 %all-gather.9.cloned.1.call-done = bf16[256,2048]{1,0:T(8,128)(2,1)} async-done(((bf16[8,2048]{1,0:T(8,128)(2,1)}), bf16[256,2048]{1,0:T(8,128)(2,1)}) %all-gather.9.cloned.1.call-update) | async-done | bytes 1048592 | tf_op jit(solution)/shard_map/all_gather | solution.py:69
  757.2 0.9 constant_dynamic-slice_fusion.1
  758.5 3.6 fusion.1
  762.1 125.9 %all-reduce = (f32[1,2048]{1,0:T(1,128)}, f32[1,2048]{1,0:T(1,128)}) all-reduce(f32[1,2048]{1,0:T(1,128)S(1)} %bitcast.80, f32[1,2048]{1,0:T(1,128)S(1)} %bitcast.81), channel_id=1, replica_groups=mesh['section'=2,'dp'=4,'mp'=32] {'mp'}, use_global_device_ids=true, to_apply=%region_20.0 | all-reduce | flops 4096 | bytes 32768 | tf_op jit(solution)/shard_map/psum | solution.py:108
  888.0 0.7 copy.18
  888.7 0.7 copy.17
  (45 shorter events, 1.8 us)
Async XLA Ops:
  7.2 173.2 %copy-start = (bf16[1,2048,512]{2,1,0:T(8,128)(2,1)S(1)}, bf16[1,2048,512]{2,1,0:T(8,128)(2,1)}, u32[]{:S(2)}) copy-start(bf16[1,2048,512]{2,1,0:T(8,128)(2,1)} %param.14) | copy-start | bytes 6291460
  7.2 85.4 %all-gather.15.cloned.1.call-start = ((), (), s32[]{:S(2)}) async-start(), calls=%async_computation.3 | async-start | bytes 1081344 | tf_op jit(solution)/shard_map/all_gather | solution.py:73
  7.9 161.9 %all-gather.13.cloned.1.call-start = ((), (), s32[]{:S(2)}) async-start(), calls=%async_computation.2 | async-start | bytes 1081344 | tf_op jit(solution)/shard_map/all_gather | solution.py:61
  8.7 238.4 %all-gather.17.cloned.1.call-start = ((), (), s32[]{:S(2)}) async-start(), calls=%async_computation.4 | async-start | bytes 1081344 | tf_op jit(solution)/shard_map/all_gather | solution.py:74
  9.4 171.0 %copy-start.8 = (f32[1,2048]{1,0:T(1,128)S(1)}, f32[1,2048]{1,0:T(1,128)}, u32[]{:S(2)}) copy-start(f32[1,2048]{1,0:T(1,128)} %param.12) | copy-start | bytes 24580
  9.4 171.0 %copy-start.11 = (f32[1,2048]{1,0:T(1,128)S(1)}, f32[1,2048]{1,0:T(1,128)}, u32[]{:S(2)}) copy-start(f32[1,2048]{1,0:T(1,128)} %param.13) | copy-start | bytes 24580
  9.4 293.6 %all-reduce.10.cloned.1.call-start = ((), (), s32[]{:S(2)}) async-start(), calls=%async_computation.6 | async-start | bytes 3145728 | tf_op jit(solution)/shard_map/psum | solution.py:64
  92.6 78.8 %copy-start.1 = (bf16[1,256,2048]{2,1,0:T(8,128)(2,1)S(1)}, bf16[1,256,2048]{2,1,0:T(8,128)(2,1)}, u32[]{:S(2)}) copy-start(bf16[1,256,2048]{2,1,0:T(8,128)(2,1)} %all-gather.15.cloned.1.call-done) | copy-start | bytes 3145732
  169.8 1.8 copy-start.2
  180.4 1.6 copy-start.3
  183.6 119.4 %copy-start.9 = (f32[1,512]{1,0:T(1,128)S(1)}, f32[1,512]{1,0:T(1,128)}, u32[]{:S(2)}) copy-start(f32[1,512]{1,0:T(1,128)} %param.15) | copy-start | bytes 6148
  250.5 341.8 %all-reduce.8.cloned.1.call-start = ((), (), s32[]{:S(2)}) async-start(), calls=%async_computation.5 | async-start | bytes 8388608 | tf_op jit(solution)/shard_map/psum | solution.py:66
  305.2 2.1 copy-start.4
  305.2 2.1 copy-start.5
  309.4 291.4 %copy-start.6 = (bf16[1,8,2048]{2,1,0:T(8,128)(2,1)S(1)}, bf16[1,8,2048]{2,1,0:T(8,128)(2,1)}, u32[]{:S(2)}) copy-start(bf16[1,8,2048]{2,1,0:T(8,128)(2,1)} %param.11) | copy-start | bytes 98308
  309.4 293.0 %copy-start.7 = (bf16[1,8,2048]{2,1,0:T(8,128)(2,1)S(1)}, bf16[1,8,2048]{2,1,0:T(8,128)(2,1)}, u32[]{:S(2)}) copy-start(bf16[1,8,2048]{2,1,0:T(8,128)(2,1)} %param.9) | copy-start | bytes 98308
  309.4 293.0 %copy-start.10 = (f32[1,2048]{1,0:T(1,128)S(1)}, f32[1,2048]{1,0:T(1,128)}, u32[]{:S(2)}) copy-start(f32[1,2048]{1,0:T(1,128)} %param.17) | copy-start | bytes 24580
  309.4 369.9 %all-gather.11.cloned.1.call-start = ((), (), s32[]{:S(2)}) async-start(), calls=%async_computation.1 | async-start | bytes 1081344 | tf_op jit(solution)/shard_map/all_gather | solution.py:111
  602.4 154.8 %all-gather.9.cloned.1.call-start = ((), (), s32[]{:S(2)}) async-start(), calls=%async_computation | async-start | bytes 1081344 | tf_op jit(solution)/shard_map/all_gather | solution.py:69
  680.3 207.7 %collective-permute-start.1 = (bf16[256,64]{1,0:T(8,128)(2,1)S(1)}, bf16[256,64]{1,0:T(8,128)(2,1)S(1)}, u32[]{:S(2)}, u32[]{:S(2)}) collective-permute-start(bf16[256,64]{1,0:T(8,128)(2,1)S(1)} %constant_dynamic-slice_fusion), channel_id=1, source_target_pairs={{0,128},{128,0},{1,129},{129,1},{2,130},{130,2},{3,131},{131,3},{4... | collective-permute-start | bytes 98312 | tf_op jit(solution)/shard_map/ppermute | solution.py:17
  758.1 130.6 %collective-permute-start = (bf16[256,64]{1,0:T(8,128)(2,1)S(1)}, bf16[256,64]{1,0:T(8,128)(2,1)S(1)}, u32[]{:S(2)}, u32[]{:S(2)}) collective-permute-start(bf16[256,64]{1,0:T(8,128)(2,1)S(1)} %constant_dynamic-slice_fusion.1), channel_id=1, source_target_pairs={{0,128},{128,0},{1,129},{129,1},{2,130},{130,2},{3,131},{131,3},{4... | collective-permute-start | bytes 98312 | tf_op jit(solution)/shard_map/ppermute | solution.py:17
Sparse Core Ops, SparseCore 0:
  10.8 81.7 all-gather.14
  95.4 74.3 all-gather.12
  172.6 74.3 all-gather.16
  250.6 52.3 all-reduce.9
  309.5 282.7 all-reduce.7
  602.5 76.8 all-gather.10
  682.7 74.3 all-gather.8
where the time goes:
time: 901 us; the launch traced here: 896 us
  waiting for transfers between devices  706 us (78%)
  blocking collectives  142 us (16%)
  matrix products  16.7 us (2%)
  between operations  14.3 us (2%)
  other arithmetic  13.5 us (1%)
    psum x1, waiting for transfers between devices, local(): lax.psum(jnp.dot(activated, w_down, preferred_element_type=jnp.float32),...  281 us
    psum x1, blocking collectives, local(): lax.psum((jnp.sum(grad_normed * centered_rows, 0), jnp.sum(grad_normed, 0...  126 us
    all_gather x1, waiting for transfers between devices, local(): lax.all_gather(saved_input[0], 'mp', axis=0, tiled=True)  83.1 us
    all_gather x1, waiting for transfers between devices, local(): whole_out = lax.all_gather(result, 'mp', axis=0, tiled=True)  76.5 us
    all_gather x1, waiting for transfers between devices, local(): gathered = lax.all_gather(section_input[0], 'mp', axis=0, tiled=True)  75.7 us
    all_gather x1, waiting for transfers between devices, local(): whole_grad = lax.all_gather(grad_in, 'mp', axis=0, tiled=True)  71.2 us
    all_gather x1, waiting for transfers between devices, local(): lax.all_gather(cotangent[0], 'mp', axis=0, tiled=True)  63.5 us
    psum x1, waiting for transfers between devices, local(): pre = lax.psum(partial_up, 'dp') + bias_up  52.4 us
  transfers between devices with their start and end apart: 9, of which 7 were waited for; matrix products, arithmetic and copies ran while one was open for 2% of the time, Pallas kernels for 0%

commit v1 on v0

v1 whole, which is shorter than its diff:
```python
import jax
import jax.numpy as jnp
from jax import lax
from jax.sharding import Mesh, PartitionSpec as P

D = 8192


EPS = 1e-05
COEF_A = 0.7978845608028654
COEF_B = 0.044715
F32 = jnp.float32
BF = jnp.bfloat16


def shifted(value, axis, steps):
    count = lax.axis_size(axis)
    return lax.ppermute(value, axis, [(i, (i + steps) % count) for i in range(count)])


def swapped(value, axis, bit):
    count = lax.axis_size(axis)
    return lax.ppermute(value, axis, [(i, i ^ bit) for i in range(count)])


def gelu_value(value):
    inner = jnp.tanh(COEF_A * (value + COEF_B * value * value * value))
    return 0.5 * value * (1.0 + inner)


def gelu_slope(value):
    inner = jnp.tanh(COEF_A * (value + COEF_B * value * value * value))
    return 0.5 * (1.0 + inner) + 0.5 * value * (1.0 - inner * inner) * COEF_A * (
        1.0 + 3.0 * COEF_B * value * value
    )


def paired(mine, axis, place):
    other = swapped(mine, axis, 1)
    first = lax.axis_index(axis) == 0
    return jnp.where(
        first, jnp.stack([mine, other], place), jnp.stack([other, mine], place)
    )


def gather_tokens(own):
    ahead, behind = [own], [own]
    for _ in range(4):
        ahead.append(shifted(ahead[-1], "z", 1))
    for _ in range(3):
        behind.append(shifted(behind[-1], "z", -1))
    around = jnp.stack([own] + behind[1:] + [ahead[4], ahead[3], ahead[2], ahead[1]], 1)
    column = jnp.roll(around, lax.axis_index("z"), axis=1)
    plane = paired(column, "xh", 2)
    whole = paired(plane, "core", 3)
    return whole.reshape(own.shape[0], -1, own.shape[2])


def take(value, index, axis):
    return lax.dynamic_index_in_dim(value, index, axis, keepdims=False)


def local(
    section_input,
    saved_input,
    cotangent,
    norm_gain,
    norm_shift,
    up_weight,
    up_bias,
    down_weight,
    down_bias,
):
    gain, shift = (norm_gain[0], norm_shift[0])
    w_up, w_down = (up_weight[0], down_weight[0])
    bias_up, bias_down = (up_bias[0], down_bias[0])
    at_z, at_h, at_c = (lax.axis_index("z"), lax.axis_index("xh"), lax.axis_index("core"))
    piece = 64
    start_column = (at_z * 4 + at_h * 2 + at_c) * piece

    own = jnp.stack([section_input[0], saved_input[0], cotangent[0]])
    gathered = gather_tokens(own)
    grad_full = gathered[2]

    partial_back = lax.dot_general(
        grad_full, w_down, (((1,), (1,)), ((), ())), preferred_element_type=F32
    )
    values = gathered[:2].astype(F32)
    sums = jnp.stack([jnp.sum(values, 2), jnp.sum(values * values, 2)])
    sums = sums + shifted(sums, "dp", 1) + shifted(sums, "dp", 2) + shifted(sums, "dp", 3)
    mean = sums[0] / D
    rstd = lax.rsqrt(sums[1] / D - mean * mean + EPS)
    centered = (values - mean[:, :, None]) * rstd[:, :, None]
    normed = (centered * gain + shift).astype(BF)
    partial_pre = jnp.dot(normed.reshape(-1, normed.shape[2]), w_up, preferred_element_type=F32)

    parts = jnp.concatenate([partial_pre.astype(BF), partial_back.astype(BF)])
    parts = parts.reshape(3, 4, 64, 512).transpose(1, 0, 2, 3)
    parts = lax.all_to_all(parts, "dp", 0, 0, tiled=False)
    total = jnp.sum(parts.astype(F32), 0)
    pre = total[:2] + bias_up
    act = gelu_value(pre).astype(BF)
    grad_pre = (total[2] * gelu_slope(pre[1])).astype(BF)
    quarter = jnp.concatenate([act, grad_pre[None]])
    hops = [shifted(quarter, "dp", -k) for k in (1, 2, 3)]
    hidden = jnp.roll(jnp.stack([quarter] + hops, 1), lax.axis_index("dp"), axis=1)
    hidden = hidden.reshape(3, 256, 512)
    act_forward, act_saved, grad_pre = hidden[0], hidden[1], hidden[2]

    forward_t = lax.dot_general(
        w_down, act_forward, (((0,), (1,)), ((), ())), preferred_element_type=F32
    )
    normed_t = lax.dot_general(
        w_up, grad_pre, (((1,), (1,)), ((), ())), preferred_element_type=F32
    )
    forward_t = forward_t.reshape(8, 2, 2, piece, 256)
    normed_t = normed_t.reshape(8, 2, 2, piece, 256)

    def both(index, axis, a, b):
        return jnp.stack([take(a, index, axis), take(b, index, axis)], axis)

    kept = both(at_c, 2, forward_t, normed_t)
    given = both(1 - at_c, 2, forward_t, normed_t).astype(BF)
    kept = kept + swapped(given, "core", 1).astype(F32)
    given = take(kept, 1 - at_h, 1).astype(BF)
    kept = take(kept, at_h, 1) + swapped(given, "xh", 1).astype(F32)
    blocks = lax.all_to_all(kept.astype(BF), "z", 0, 0, tiled=False)
    columns = jnp.sum(blocks.astype(F32), 0)

    grad_normed = lax.dot_general(
        grad_pre, w_up, (((1,), (1,)), ((), ())), preferred_element_type=F32
    )
    scaled = grad_normed * gain
    moments = jnp.stack([jnp.sum(scaled, 1), jnp.sum(scaled * centered[1], 1)])
    params = jnp.stack([jnp.sum(grad_normed * centered[1], 0), jnp.sum(grad_normed, 0)])
    moments = (
        moments
        + shifted(moments, "dp", 1)
        + shifted(moments, "dp", 2)
        + shifted(moments, "dp", 3)
    )
    small = jnp.concatenate([moments, params], 1)
    for axis, bit in (("core", 1), ("xh", 1), ("z", 1), ("z", 2), ("z", 4)):
        small = small + swapped(small, axis, bit)
    moments, params = small[:, :256], small[:, 256:]

    def own_columns(value):
        return lax.dynamic_slice_in_dim(value, start_column, piece, 1).astype(F32).T

    def own_piece(vector):
        return lax.dynamic_slice_in_dim(vector, start_column, piece, 0)[:, None]

    out = (own_columns(gathered[0]) + columns[0] + own_piece(bias_down)).astype(BF)
    forward_arrived = shifted(out.T, "section", 1)

    centered_columns = (own_columns(gathered[1]) - mean[1]) * rstd[1]
    grad_in = own_columns(grad_full) + rstd[1] * (
        columns[1] * own_piece(gain) - moments[0] / D - centered_columns * (moments[1] / D)
    )
    backward_arrived = shifted(grad_in.astype(BF).T, "section", -1)

    down_weight_grad = lax.dot_general(
        act_saved, grad_full, (((0,), (0,)), ((), ())), preferred_element_type=F32
    ).astype(BF)
    down_bias_grad = jnp.sum(grad_full.astype(F32), 0)
    up_weight_grad = lax.dot_general(
        normed[1], grad_pre, (((0,), (0,)), ((), ())), preferred_element_type=F32
    ).astype(BF)
    up_bias_grad = jnp.sum(grad_pre.astype(F32), 0)
    return (
        forward_arrived[None],
        backward_arrived[None],
        up_weight_grad[None],
        up_bias_grad[None],
        down_weight_grad[None],
        down_bias_grad[None],
        params[0][None],
        params[1][None],
    )


def solution(mesh):
    names = ("section", "dp", "z", "xh", "core")
    split = Mesh(mesh.devices.reshape(2, 4, 8, 2, 2), names)
    mp = ("z", "xh", "core")
    placed = (
        P("section", mp, "dp"),
        P("section", mp, "dp"),
        P("section", mp, "dp"),
        P("section", "dp"),
        P("section", "dp"),
        P("section", "dp", mp),
        P("section", mp),
        P("section", mp, "dp"),
        P("section", "dp"),
    )
    return jax.shard_map(
        local,
        mesh=split,
        in_specs=placed,
        out_specs=(
            P("section", None, ("dp",) + mp),
            P("section", None, ("dp",) + mp),
            P("section", "dp", mp),
            P("section", mp),
            P("section", mp, "dp"),
            P("section", "dp"),
            P("section", "dp"),
            P("section", "dp"),
        ),
        check_vma=False,
    )
```

time: 901 us -> 198 us (0.22)
  the two profiles are of different devices: /device:TPU:1 before, /device:TPU:4 now
where the time goes in v1:
time: 198 us; the launch traced here: 197 us
  waiting for transfers between devices  72.5 us (37%)
  starting transfers between devices  44 us (22%)
  local copies, waits for them, and re-layouts  43.4 us (22%)
  other arithmetic  22.4 us (11%)
  matrix products  13.6 us (7%)
    ppermute x9, waiting for transfers between devices, swapped(): return lax.ppermute(value, axis, [(i, i ^ bit) for i in range(count)])  37.4 us
    ppermute x18, starting transfers between devices, shifted(): lax.ppermute(value, axis, [(i, (i + steps) % count) for i in range(count)])  25 us
    ppermute x18, waiting for transfers between devices, shifted(): lax.ppermute(value, axis, [(i, (i + steps) % count) for i in range(count)])  23.1 us
    unnamed x54, local copies, waits for them, and re-layouts  17.4 us
    all_to_all x1, waiting for transfers between devices, local(): parts = lax.all_to_all(parts, 'dp', 0, 0, tiled=False)  12 us
    ppermute x9, starting transfers between devices, swapped(): return lax.ppermute(value, axis, [(i, i ^ bit) for i in range(count)])  9.69 us
    all_to_all x1, starting transfers between devices, local(): blocks = lax.all_to_all(kept.astype(BF), 'z', 0, 0, tiled=False)  5.06 us
    all_to_all x1, starting transfers between devices, local(): parts = lax.all_to_all(parts, 'dp', 0, 0, tiled=False)  4.32 us
  transfers between devices with their start and end apart: 29, of which 15 were waited for; matrix products, arithmetic and copies ran while one was open for 18% of the time, Pallas kernels for 0%

profile of v1, /device:TPU:4, one launch (start us, length us, event | category | flops | bytes accessed | tf_op | source)
XLA Modules:
  0.0 197.2 jit_solution(551356419971333776)
XLA Ops:
  5.0 3.9 %collective-permute-start = (bf16[3,8,2048]{2,1,0:T(8,128)(2,1)S(1)}, bf16[3,8,2048]{2,1,0:T(8,128)(2,1)S(1)}, u32[]{:S(2)}, u32[]{:S(2)}) collective-permute-start(bf16[3,8,2048]{2,1,0:T(8,128)(2,1)S(1)} %constant_dynamic-update-slice_fusion), channel_id=1, source_target_pairs={{0,28},{4,0},{8,4},{12,8},{16,12},{20,16},{24,20},{28,24},{1,29},{... | collective-permute-start | bytes 294920 | tf_op jit(solution)/shard_map/ppermute | solution.py:18
  9.6 2.1 %collective-permute-done.3 = bf16[3,8,2048]{2,1,0:T(8,128)(2,1)S(1)} collective-permute-done((bf16[3,8,2048]{2,1,0:T(8,128)(2,1)S(1)}, bf16[3,8,2048]{2,1,0:T(8,128)(2,1)S(1)}, u32[]{:S(2)}, u32[]{:S(2)}) %collective-permute-start.3) | collective-permute-done | bytes 98336 | tf_op jit(solution)/shard_map/ppermute | solution.py:18
  11.7 3.2 %collective-permute-start.1 = (bf16[3,8,2048]{2,1,0:T(8,128)(2,1)S(1)}, bf16[3,8,2048]{2,1,0:T(8,128)(2,1)S(1)}, u32[]{:S(2)}, u32[]{:S(2)}) collective-permute-start(bf16[3,8,2048]{2,1,0:T(8,128)(2,1)S(1)} %collective-permute-done), channel_id=1, source_target_pairs={{0,28},{4,0},{8,4},{12,8},{16,12},{20,16},{24,20},{28,24},{1,29},{... | collective-permute-start | bytes 294920 | tf_op jit(solution)/shard_map/ppermute | solution.py:18
  15.6 1.9 collective-permute-done.4
  17.6 3.2 %collective-permute-start.2 = (bf16[3,8,2048]{2,1,0:T(8,128)(2,1)S(1)}, bf16[3,8,2048]{2,1,0:T(8,128)(2,1)S(1)}, u32[]{:S(2)}, u32[]{:S(2)}) collective-permute-start(bf16[3,8,2048]{2,1,0:T(8,128)(2,1)S(1)} %collective-permute-done.1), channel_id=1, source_target_pairs={{0,28},{4,0},{8,4},{12,8},{16,12},{20,16},{24,20},{28,24},{1,29},{... | collective-permute-start | bytes 294920 | tf_op jit(solution)/shard_map/ppermute | solution.py:18
  24.0 5.2 %collective-permute-done.6 = bf16[3,8,2048]{2,1,0:T(8,128)(2,1)S(1)} collective-permute-done((bf16[3,8,2048]{2,1,0:T(8,128)(2,1)S(1)}, bf16[3,8,2048]{2,1,0:T(8,128)(2,1)S(1)}, u32[]{:S(2)}, u32[]{:S(2)}) %collective-permute-start.6) | collective-permute-done | bytes 98336 | tf_op jit(solution)/shard_map/ppermute | solution.py:18
  37.0 2.1 %constant_dynamic-slice_fusion.10 = bf16[3,8,8,2048]{3,2,1,0:T(8,128)(2,1)} fusion(bf16[3,16,8,2048]{3,2,1,0:T(8,128)(2,1)} %bitcast_dynamic-update-slice_fusion.23, s32[]{:T(128)S(6)} %select_n.76), kind=kLoop, calls=%fused_computation.119 | loop fusion | bytes 1572868 | tf_op jit(solution)/shard_map/jit(_roll_dynamic)/dynamic_slice | solution.py:53
  40.8 15.3 %collective-permute-done.7 = bf16[3,8,8,2048]{3,2,1,0:T(8,128)(2,1)S(1)} collective-permute-done((bf16[3,8,8,2048]{3,2,1,0:T(8,128)(2,1)}, bf16[3,8,8,2048]{3,2,1,0:T(8,128)(2,1)S(1)}, u32[]{:S(2)}, u32[]{:S(2)}) %collective-permute-start.7) | collective-permute-done | bytes 786464 | tf_op jit(solution)/shard_map/ppermute | solution.py:23
  59.0 2.1 %collective-permute-done.8 = bf16[3,8,2,8,2048]{4,3,2,1,0:T(8,128)(2,1)} collective-permute-done((bf16[3,8,2,8,2048]{4,3,2,1,0:T(8,128)(2,1)}, bf16[3,8,2,8,2048]{4,3,2,1,0:T(8,128)(2,1)}, u32[]{:S(2)}, u32[]{:S(2)}) %collective-permute-start.8) | collective-permute-done | bytes 1572896 | tf_op jit(solution)/shard_map/ppermute | solution.py:23
  61.1 2.1 %maximum_select_fusion = bf16[3,8,2,2,8,2048]{5,4,3,2,1,0:T(8,128)(2,1)S(1)} fusion(bf16[3,8,2,1,8,2048]{5,4,3,2,1,0:T(8,128)(2,1)} %bitcast.26, bf16[3,8,2,1,8,2048]{5,4,3,2,1,0:T(8,128)(2,1)S(1)} %copy_select_fusion, pred[]{:T(512)S(6)} %eq.11), kind=kLoop, calls=%fused_computation.4 | loop fusion | flops 4718592 | bytes 6291457 | tf_op jit(solution)/shard_map/jit(_where)/select_n | solution.py:41
  65.9 3.1 %collective-permute-start.11 = (f32[2,2,256]{2,1,0:T(2,128)S(1)}, f32[2,2,256]{2,1,0:T(2,128)S(1)}, u32[]{:S(2)}, u32[]{:S(2)}) collective-permute-start(f32[2,2,256]{2,1,0:T(2,128)S(1)} %constant_dynamic-update-slice_fusion.3), channel_id=1, source_target_pairs={{0,96},{32,0},{64,32},{96,64},{1,97},{33,1},{65,33},{97,65},{2,98}... | collective-permute-start | bytes 12296 | tf_op jit(solution)/shard_map/ppermute | solution.py:18
  70.5 3.6 %fusion.53 = (bf16[1,8,2,2,8,2048]{5,4,3,2,1,0:T(8,128)(2,1)}, bf16[1,8,2,2,8,2048]{5,4,3,2,1,0:T(8,128)(2,1)S(1)}, bf16[1,8,2,2,8,2048]{5,4,3,2,1,0:T(8,128)(2,1)}) fusion(bf16[3,8,2,2,8,2048]{5,4,3,2,1,0:T(8,128)(2,1)} %copy-done.1), kind=kLoop, calls=%fused_computation.133 | loop fusion | bytes 6291456 | tf_op jit(solution)/shard_map/slice | solution.py:156
  75.7 2.4 %add_convert_fusion = bf16[2,8,2,2,8,2048]{5,4,3,2,1,0:T(8,128)(2,1)S(1)} fusion(f32[2048]{0:T(1024)S(1)} %bitcast.219, f32[2048]{0:T(1024)S(1)} %bitcast.216, f32[2,8,2,2,8]{4,3,2,1,0:T(2,128)S(1)} %add_rsqrt_fusion, f32[2,8,2,2,8]{4,3,2,1,0:T(2,128)S(1)} %div.21, bf16[3,8,2,2,8,2048]{5,4,3,2,1,0:T(8,128)(2,1)} %copy-done.1), kind=kLoop, calls=%fused_computation.2 | loop fusion | flops 6291456 | bytes 4214784 | tf_op jit(solution)/shard_map/convert_element_type | solution.py:94
  80.4 4.3 %all-to-all-start = ((bf16[4,3,64,512]{3,2,1,0:T(8,128)(2,1)}), bf16[4,3,64,512]{3,2,1,0:T(8,128)(2,1)}, u32[]{:S(2)}, u32[]{:S(2)}) async-start(bf16[4,3,64,512]{3,2,1,0:T(8,128)(2,1)} %bitcast.204), calls=%async_computation | async-start | bytes 1572864 | tf_op jit(solution)/shard_map/all_to_all | solution.py:99
  84.8 12.0 %all-to-all-done = bf16[4,3,64,512]{3,2,1,0:T(8,128)(2,1)} async-done(((bf16[4,3,64,512]{3,2,1,0:T(8,128)(2,1)}), bf16[4,3,64,512]{3,2,1,0:T(8,128)(2,1)}, u32[]{:S(2)}, u32[]{:S(2)}) %all-to-all-start) | async-done | bytes 786464 | tf_op jit(solution)/shard_map/all_to_all | solution.py:99
  99.8 4.1 %fusion = f32[2,256,2048]{2,1,0:T(8,128)} fusion(f32[2,256]{1,0:T(2,128)S(1)} %fusion.48, f32[2,256]{1,0:T(2,128)S(1)} %get-tuple-element.39, bf16[3,8,2,2,8,2048]{5,4,3,2,1,0:T(8,128)(2,1)} %copy-done.1), kind=kLoop, calls=%fused_computation.1 | loop fusion | flops 3145728 | bytes 6295552 | tf_op jit(solution)/shard_map/mul | solution.py:93
  105.2 7.4 %collective-permute-done.13 = bf16[3,64,512]{2,1,0:T(8,128)(2,1)S(1)} collective-permute-done((bf16[3,64,512]{2,1,0:T(8,128)(2,1)S(1)}, bf16[3,64,512]{2,1,0:T(8,128)(2,1)S(1)}, u32[]{:S(2)}, u32[]{:S(2)}) %collective-permute-start.13) | collective-permute-done | bytes 196640 | tf_op jit(solution)/shard_map/ppermute | solution.py:18
  112.6 2.0 %collective-permute-done.14 = bf16[3,64,512]{2,1,0:T(8,128)(2,1)S(1)} collective-permute-done((bf16[3,64,512]{2,1,0:T(8,128)(2,1)S(1)}, bf16[3,64,512]{2,1,0:T(8,128)(2,1)S(1)}, u32[]{:S(2)}, u32[]{:S(2)}) %collective-permute-start.14) | collective-permute-done | bytes 196640 | tf_op jit(solution)/shard_map/ppermute | solution.py:18
  116.3 2.0 %convolution_bitcast_fusion = f32[2048,256]{0,1:T(8,128)} fusion(bf16[256,512]{1,0:T(8,128)(2,1)S(1)} %bitcast.213, bf16[1,512,2048]{2,1,0:T(8,128)(2,1)S(1)} %copy-done.3), kind=kOutput, calls=%fused_computation.10 | convolution fusion | flops 536870912 | bytes 4456448 | tf_op jit(solution)/shard_map/dot_general | solution.py:110
  118.4 3.0 %copy.85 = f32[2048,256]{1,0:T(8,128)} copy(f32[2048,256]{0,1:T(8,128)} %convolution_bitcast_fusion) | data formatting | bytes 4194304 | tf_op jit(solution)/shard_map/dot_general | solution.py:110
  121.3 3.9 %fusion.3 = (f32[256]{0:T(256)S(1)}, f32[2048]{0:T(1024)S(1)}, f32[256]{0:T(256)S(1)}, f32[2048]{0:T(1024)S(1)}, f32[256,2048]{1,0:T(8,128)}) fusion(f32[2,256,2048]{2,1,0:T(8,128)} %fusion, f32[2048]{0:T(1024)S(1)} %bitcast.217, bf16[256,512]{1,0:T(8,128)(2,1)} %bitcast.214, bf16[1,2048,512]{2,1,0:T(8,128)(2,1)S(1)} %copy-done), kind=kOutput, calls=%fused_computation.14 | convolution fusion | flops 540536320 | bytes 6580224 | tf_op jit(solution)/shard_map/dot_general | solution.py:113
  125.2 2.9 %copy.86 = f32[2048,256]{1,0:T(8,128)} copy(f32[2048,256]{0,1:T(8,128)} %bitcast.208) | data formatting | bytes 4194304 | tf_op jit(solution)/shard_map/dot_general | solution.py:113
  132.2 2.0 %convert_reduce_fusion.1 = f32[2048]{0:T(1024)} fusion(bf16[3,8,2,2,8,2048]{5,4,3,2,1,0:T(8,128)(2,1)} %copy-done.1), kind=kLoop, calls=%fused_computation.23 | loop fusion | flops 1046528 | bytes 1056768 | tf_op jit(solution)/shard_map/reduce_sum | solution.py:165
  141.8 14.3 %collective-permute-done.16 = bf16[8,2,64,256]{3,2,1,0:T(8,128)(2,1)S(1)} collective-permute-done((bf16[8,2,64,256]{3,2,1,0:T(8,128)(2,1)S(1)}, bf16[8,2,64,256]{3,2,1,0:T(8,128)(2,1)S(1)}, u32[]{:S(2)}, u32[]{:S(2)}) %collective-permute-start.16) | collective-permute-done | bytes 524320 | tf_op jit(solution)/shard_map/ppermute | solution.py:23
  157.1 5.1 %all-to-all-start.1 = ((bf16[8,2,64,256]{3,2,1,0:T(8,128)(2,1)}), bf16[8,2,64,256]{3,2,1,0:T(8,128)(2,1)}, u32[]{:S(2)}, u32[]{:S(2)}) async-start(bf16[8,2,64,256]{3,2,1,0:T(8,128)(2,1)} %fusion.22), calls=%async_computation.1 | async-start | bytes 1048576 | tf_op jit(solution)/shard_map/all_to_all | solution.py:127
  164.3 3.2 %collective-permute-done.22 = f32[2,2304]{1,0:T(2,128)S(1)} collective-permute-done((f32[2,2304]{1,0:T(2,128)S(1)}, f32[2,2304]{1,0:T(2,128)S(1)}, u32[]{:S(2)}, u32[]{:S(2)}) %collective-permute-start.22) | collective-permute-done | bytes 18464 | tf_op jit(solution)/shard_map/ppermute | solution.py:23
  168.2 2.0 %collective-permute-start.23 = (f32[2,2304]{1,0:T(2,128)}, f32[2,2304]{1,0:T(2,128)}, u32[]{:S(2)}, u32[]{:S(2)}) collective-permute-start(f32[2,2304]{1,0:T(2,128)} %add.212), channel_id=1, source_target_pairs={{0,4},{4,0},{8,12},{12,8},{16,20},{20,16},{24,28},{28,24},{1,5},{5... | collective-permute-start | bytes 55304 | tf_op jit(solution)/shard_map/ppermute | solution.py:23
  175.9 2.1 %collective-permute-start.24 = (f32[2,2304]{1,0:T(2,128)S(1)}, f32[2,2304]{1,0:T(2,128)S(1)}, u32[]{:S(2)}, u32[]{:S(2)}) collective-permute-start(f32[2,2304]{1,0:T(2,128)S(1)} %add.213), channel_id=1, source_target_pairs={{0,8},{4,12},{8,0},{12,4},{16,24},{20,28},{24,16},{28,20},{1,9},{5... | collective-permute-start | bytes 55304 | tf_op jit(solution)/shard_map/ppermute | solution.py:23
  178.0 3.7 %fusion.1 = bf16[1,2048,512]{2,1,0:T(8,128)(2,1)} fusion(bf16[256,512]{1,0:T(8,128)(2,1)} %bitcast.215, f32[2,256,2048]{2,1,0:T(8,128)} %fusion, f32[2048]{0:T(1024)S(1)} %bitcast.220, f32[2048]{0:T(1024)S(1)} %bitcast.218), kind=kOutput, calls=%fused_computation.8 | convolution fusion | flops 539492352 | bytes 4472832 | tf_op jit(solution)/shard_map/dot_general | solution.py:166
  181.7 3.5 %collective-permute-start.25 = (f32[2,2304]{1,0:T(2,128)S(1)}, f32[2,2304]{1,0:T(2,128)S(1)}, u32[]{:S(2)}, u32[]{:S(2)}) collective-permute-start(f32[2,2304]{1,0:T(2,128)S(1)} %add.214), channel_id=1, source_target_pairs={{0,16},{4,20},{8,24},{12,28},{16,0},{20,4},{24,8},{28,12},{1,17},{... | collective-permute-start | bytes 55304 | tf_op jit(solution)/shard_map/ppermute | solution.py:23
  185.3 2.1 %fusion.2 = bf16[1,512,2048]{2,1,0:T(8,128)(2,1)} fusion(bf16[256,512]{1,0:T(8,128)(2,1)S(1)} %bitcast.210, bf16[256,2048]{1,0:T(8,128)(2,1)S(1)} %bitcast.203), kind=kOutput, calls=%fused_computation.9 | convolution fusion | flops 537919488 | bytes 3407872 | tf_op jit(solution)/shard_map/dot_general | solution.py:162
  187.3 2.2 %collective-permute-done.25 = f32[2,2304]{1,0:T(2,128)S(1)} collective-permute-done((f32[2,2304]{1,0:T(2,128)S(1)}, f32[2,2304]{1,0:T(2,128)S(1)}, u32[]{:S(2)}, u32[]{:S(2)}) %collective-permute-start.25) | collective-permute-done | bytes 18464 | tf_op jit(solution)/shard_map/ppermute | solution.py:23
  (145 shorter events, 64.0 us)
Async XLA Ops:
  0.6 77.5 %copy-start = (bf16[1,2048,512]{2,1,0:T(8,128)(2,1)S(1)}, bf16[1,2048,512]{2,1,0:T(8,128)(2,1)}, u32[]{:S(2)}) copy-start(bf16[1,2048,512]{2,1,0:T(8,128)(2,1)} %param.14) | copy-start | bytes 6291460
  3.1 8.6 %collective-permute-start.3 = (bf16[3,8,2048]{2,1,0:T(8,128)(2,1)S(1)}, bf16[3,8,2048]{2,1,0:T(8,128)(2,1)S(1)}, u32[]{:S(2)}, u32[]{:S(2)}) collective-permute-start(bf16[3,8,2048]{2,1,0:T(8,128)(2,1)S(1)} %constant_dynamic-update-slice_fusion), channel_id=1, source_target_pairs={{0,4},{4,8},{8,12},{12,16},{16,20},{20,24},{24,28},{28,0},{1,5},{5... | collective-permute-start | bytes 294920 | tf_op jit(solution)/shard_map/ppermute | solution.py:18
  5.0 6.7 %collective-permute-start = (bf16[3,8,2048]{2,1,0:T(8,128)(2,1)S(1)}, bf16[3,8,2048]{2,1,0:T(8,128)(2,1)S(1)}, u32[]{:S(2)}, u32[]{:S(2)}) collective-permute-start(bf16[3,8,2048]{2,1,0:T(8,128)(2,1)S(1)} %constant_dynamic-update-slice_fusion), channel_id=1, source_target_pairs={{0,28},{4,0},{8,4},{12,8},{16,12},{20,16},{24,20},{28,24},{1,29},{... | collective-permute-start | bytes 294920 | tf_op jit(solution)/shard_map/ppermute | solution.py:18
  11.7 5.8 %collective-permute-start.4 = (bf16[3,8,2048]{2,1,0:T(8,128)(2,1)S(1)}, bf16[3,8,2048]{2,1,0:T(8,128)(2,1)S(1)}, u32[]{:S(2)}, u32[]{:S(2)}) collective-permute-start(bf16[3,8,2048]{2,1,0:T(8,128)(2,1)S(1)} %collective-permute-done.3), channel_id=1, source_target_pairs={{0,4},{4,8},{8,12},{12,16},{16,20},{20,24},{24,28},{28,0},{1,5},{5... | collective-permute-start | bytes 294920 | tf_op jit(solution)/shard_map/ppermute | solution.py:18
  11.7 5.8 %collective-permute-start.1 = (bf16[3,8,2048]{2,1,0:T(8,128)(2,1)S(1)}, bf16[3,8,2048]{2,1,0:T(8,128)(2,1)S(1)}, u32[]{:S(2)}, u32[]{:S(2)}) collective-permute-start(bf16[3,8,2048]{2,1,0:T(8,128)(2,1)S(1)} %collective-permute-done), channel_id=1, source_target_pairs={{0,28},{4,0},{8,4},{12,8},{16,12},{20,16},{24,20},{28,24},{1,29},{... | collective-permute-start | bytes 294920 | tf_op jit(solution)/shard_map/ppermute | solution.py:18
  17.6 5.8 %collective-permute-start.5 = (bf16[3,8,2048]{2,1,0:T(8,128)(2,1)S(1)}, bf16[3,8,2048]{2,1,0:T(8,128)(2,1)S(1)}, u32[]{:S(2)}, u32[]{:S(2)}) collective-permute-start(bf16[3,8,2048]{2,1,0:T(8,128)(2,1)S(1)} %collective-permute-done.4), channel_id=1, source_target_pairs={{0,4},{4,8},{8,12},{12,16},{16,20},{20,24},{24,28},{28,0},{1,5},{5... | collective-permute-start | bytes 294920 | tf_op jit(solution)/shard_map/ppermute | solution.py:18
  17.6 5.8 %collective-permute-start.2 = (bf16[3,8,2048]{2,1,0:T(8,128)(2,1)S(1)}, bf16[3,8,2048]{2,1,0:T(8,128)(2,1)S(1)}, u32[]{:S(2)}, u32[]{:S(2)}) collective-permute-start(bf16[3,8,2048]{2,1,0:T(8,128)(2,1)S(1)} %collective-permute-done.1), channel_id=1, source_target_pairs={{0,28},{4,0},{8,4},{12,8},{16,12},{20,16},{24,20},{28,24},{1,29},{... | collective-permute-start | bytes 294920 | tf_op jit(solution)/shard_map/ppermute | solution.py:18
  23.4 5.8 %collective-permute-start.6 = (bf16[3,8,2048]{2,1,0:T(8,128)(2,1)S(1)}, bf16[3,8,2048]{2,1,0:T(8,128)(2,1)S(1)}, u32[]{:S(2)}, u32[]{:S(2)}) collective-permute-start(bf16[3,8,2048]{2,1,0:T(8,128)(2,1)S(1)} %collective-permute-done.5), channel_id=1, source_target_pairs={{0,4},{4,8},{8,12},{12,16},{16,20},{20,24},{24,28},{28,0},{1,5},{5... | collective-permute-start | bytes 294920 | tf_op jit(solution)/shard_map/ppermute | solution.py:18
  39.1 17.0 %collective-permute-start.7 = (bf16[3,8,8,2048]{3,2,1,0:T(8,128)(2,1)}, bf16[3,8,8,2048]{3,2,1,0:T(8,128)(2,1)S(1)}, u32[]{:S(2)}, u32[]{:S(2)}) collective-permute-start(bf16[3,8,8,2048]{3,2,1,0:T(8,128)(2,1)} %constant_dynamic-slice_fusion.10), channel_id=1, source_target_pairs={{0,2},{2,0},{1,3},{3,1},{4,6},{6,4},{5,7},{7,5},{8,10},{10,8},{9,1... | collective-permute-start | bytes 2359304 | tf_op jit(solution)/shard_map/ppermute | solution.py:23
  57.4 3.8 %collective-permute-start.8 = (bf16[3,8,2,8,2048]{4,3,2,1,0:T(8,128)(2,1)}, bf16[3,8,2,8,2048]{4,3,2,1,0:T(8,128)(2,1)}, u32[]{:S(2)}, u32[]{:S(2)}) collective-permute-start(bf16[3,8,2,8,2048]{4,3,2,1,0:T(8,128)(2,1)} %maximum_select_fusion.1), channel_id=1, source_target_pairs={{0,1},{1,0},{2,3},{3,2},{4,5},{5,4},{6,7},{7,6},{8,9},{9,8},{10,11... | collective-permute-start | bytes 4718600 | tf_op jit(solution)/shard_map/ppermute | solution.py:23
  65.9 9.0 %collective-permute-start.11 = (f32[2,2,256]{2,1,0:T(2,128)S(1)}, f32[2,2,256]{2,1,0:T(2,128)S(1)}, u32[]{:S(2)}, u32[]{:S(2)}) collective-permute-start(f32[2,2,256]{2,1,0:T(2,128)S(1)} %constant_dynamic-update-slice_fusion.3), channel_id=1, source_target_pairs={{0,96},{32,0},{64,32},{96,64},{1,97},{33,1},{65,33},{97,65},{2,98}... | collective-permute-start | bytes 12296 | tf_op jit(solution)/shard_map/ppermute | solution.py:18
  68.9 5.9 %collective-permute-start.10 = (f32[2,2,256]{2,1,0:T(2,128)S(1)}, f32[2,2,256]{2,1,0:T(2,128)S(1)}, u32[]{:S(2)}, u32[]{:S(2)}) collective-permute-start(f32[2,2,256]{2,1,0:T(2,128)S(1)} %constant_dynamic-update-slice_fusion.3), channel_id=1, source_target_pairs={{0,64},{32,96},{64,0},{96,32},{1,65},{33,97},{65,1},{97,33},{2,66}... | collective-permute-start | bytes 12296 | tf_op jit(solution)/shard_map/ppermute | solution.py:18
  69.6 5.3 %collective-permute-start.9 = (f32[2,2,256]{2,1,0:T(2,128)S(1)}, f32[2,2,256]{2,1,0:T(2,128)S(1)}, u32[]{:S(2)}, u32[]{:S(2)}) collective-permute-start(f32[2,2,256]{2,1,0:T(2,128)S(1)} %constant_dynamic-update-slice_fusion.3), channel_id=1, source_target_pairs={{0,32},{32,64},{64,96},{96,0},{1,33},{33,65},{65,97},{97,1},{2,34}... | collective-permute-start | bytes 12296 | tf_op jit(solution)/shard_map/ppermute | solution.py:18
  80.4 17.7 %copy-start.10 = (f32[1,512]{1,0:T(1,128)S(1)}, f32[1,512]{1,0:T(1,128)}, u32[]{:S(2)}) copy-start(f32[1,512]{1,0:T(1,128)} %param.15) | copy-start | bytes 6148
  80.4 16.4 %all-to-all-start = ((bf16[4,3,64,512]{3,2,1,0:T(8,128)(2,1)}), bf16[4,3,64,512]{3,2,1,0:T(8,128)(2,1)}, u32[]{:S(2)}, u32[]{:S(2)}) async-start(bf16[4,3,64,512]{3,2,1,0:T(8,128)(2,1)} %bitcast.204), calls=%async_computation | async-start | bytes 1572864 | tf_op jit(solution)/shard_map/all_to_all | solution.py:99
  84.8 19.1 %copy-start.8 = (f32[2,256]{1,0:T(2,128)}, f32[2,256]{1,0:T(2,128)S(1)}, u32[]{:S(2)}) copy-start(f32[2,256]{1,0:T(2,128)S(1)} %fusion.48) | copy-start | bytes 6148
  98.4 6.8 %collective-permute-start.12 = (bf16[3,64,512]{2,1,0:T(8,128)(2,1)S(1)}, bf16[3,64,512]{2,1,0:T(8,128)(2,1)S(1)}, u32[]{:S(2)}, u32[]{:S(2)}) collective-permute-start(bf16[3,64,512]{2,1,0:T(8,128)(2,1)S(1)} %pad_maximum_fusion.4), channel_id=1, source_target_pairs={{0,96},{32,0},{64,32},{96,64},{1,97},{33,1},{65,33},{97,65},{2,98}... | collective-permute-start | bytes 589832 | tf_op jit(solution)/shard_map/ppermute | solution.py:18
  103.8 8.8 %collective-permute-start.13 = (bf16[3,64,512]{2,1,0:T(8,128)(2,1)S(1)}, bf16[3,64,512]{2,1,0:T(8,128)(2,1)S(1)}, u32[]{:S(2)}, u32[]{:S(2)}) collective-permute-start(bf16[3,64,512]{2,1,0:T(8,128)(2,1)S(1)} %pad_maximum_fusion.4), channel_id=1, source_target_pairs={{0,64},{32,96},{64,0},{96,32},{1,65},{33,97},{65,1},{97,33},{2,66}... | collective-permute-start | bytes 589832 | tf_op jit(solution)/shard_map/ppermute | solution.py:18
  105.1 9.5 %collective-permute-start.14 = (bf16[3,64,512]{2,1,0:T(8,128)(2,1)S(1)}, bf16[3,64,512]{2,1,0:T(8,128)(2,1)S(1)}, u32[]{:S(2)}, u32[]{:S(2)}) collective-permute-start(bf16[3,64,512]{2,1,0:T(8,128)(2,1)S(1)} %pad_maximum_fusion.4), channel_id=1, source_target_pairs={{0,32},{32,64},{64,96},{96,0},{1,33},{33,65},{65,97},{97,1},{2,34}... | collective-permute-start | bytes 589832 | tf_op jit(solution)/shard_map/ppermute | solution.py:18
  130.8 8.2 %collective-permute-start.15 = (bf16[8,2,2,64,256]{4,3,2,1,0:T(8,128)(2,1)}, bf16[8,2,2,64,256]{4,3,2,1,0:T(8,128)(2,1)}, u32[]{:S(2)}, u32[]{:S(2)}) collective-permute-start(bf16[8,2,2,64,256]{4,3,2,1,0:T(8,128)(2,1)} %pad_maximum_fusion.2), channel_id=1, source_target_pairs={{0,1},{1,0},{2,3},{3,2},{4,5},{5,4},{6,7},{7,6},{8,9},{9,8},{10,11... | collective-permute-start | bytes 3145736 | tf_op jit(solution)/shard_map/ppermute | solution.py:23
  134.2 7.5 %collective-permute-start.19 = (f32[2,256]{1,0:T(2,128)S(1)}, f32[2,256]{1,0:T(2,128)S(1)}, u32[]{:S(2)}, u32[]{:S(2)}) collective-permute-start(f32[2,256]{1,0:T(2,128)S(1)} %pad_maximum_fusion.5), channel_id=1, source_target_pairs={{0,64},{32,96},{64,0},{96,32},{1,65},{33,97},{65,1},{97,33},{2,66}... | collective-permute-start | bytes 6152 | tf_op jit(solution)/shard_map/ppermute | solution.py:18
  135.3 6.4 %collective-permute-start.20 = (f32[2,256]{1,0:T(2,128)S(1)}, f32[2,256]{1,0:T(2,128)S(1)}, u32[]{:S(2)}, u32[]{:S(2)}) collective-permute-start(f32[2,256]{1,0:T(2,128)S(1)} %pad_maximum_fusion.5), channel_id=1, source_target_pairs={{0,96},{32,0},{64,32},{96,64},{1,97},{33,1},{65,33},{97,65},{2,98}... | collective-permute-start | bytes 6152 | tf_op jit(solution)/shard_map/ppermute | solution.py:18
  136.4 5.2 %collective-permute-start.18 = (f32[2,256]{1,0:T(2,128)S(1)}, f32[2,256]{1,0:T(2,128)S(1)}, u32[]{:S(2)}, u32[]{:S(2)}) collective-permute-start(f32[2,256]{1,0:T(2,128)S(1)} %pad_maximum_fusion.5), channel_id=1, source_target_pairs={{0,32},{32,64},{64,96},{96,0},{1,33},{33,65},{65,97},{97,1},{2,34}... | collective-permute-start | bytes 6152 | tf_op jit(solution)/shard_map/ppermute | solution.py:18
  140.8 15.3 %collective-permute-start.16 = (bf16[8,2,64,256]{3,2,1,0:T(8,128)(2,1)S(1)}, bf16[8,2,64,256]{3,2,1,0:T(8,128)(2,1)S(1)}, u32[]{:S(2)}, u32[]{:S(2)}) collective-permute-start(bf16[8,2,64,256]{3,2,1,0:T(8,128)(2,1)S(1)} %fusion.23), channel_id=1, source_target_pairs={{0,2},{2,0},{1,3},{3,1},{4,6},{6,4},{5,7},{7,5},{8,10},{10,8},{9,1... | collective-permute-start | bytes 1572872 | tf_op jit(solution)/shard_map/ppermute | solution.py:23
  141.7 20.5 %collective-permute-start.21 = (f32[2,2304]{1,0:T(2,128)S(1)}, f32[2,2304]{1,0:T(2,128)S(1)}, u32[]{:S(2)}, u32[]{:S(2)}) collective-permute-start(f32[2,2304]{1,0:T(2,128)S(1)} %maximum_maximum_fusion), channel_id=1, source_target_pairs={{0,1},{1,0},{2,3},{3,2},{4,5},{5,4},{6,7},{7,6},{8,9},{9,8},{10,11... | collective-permute-start | bytes 55304 | tf_op jit(solution)/shard_map/ppermute | solution.py:23
  157.1 32.4 %all-to-all-start.1 = ((bf16[8,2,64,256]{3,2,1,0:T(8,128)(2,1)}), bf16[8,2,64,256]{3,2,1,0:T(8,128)(2,1)}, u32[]{:S(2)}, u32[]{:S(2)}) async-start(bf16[8,2,64,256]{3,2,1,0:T(8,128)(2,1)} %fusion.22), calls=%async_computation.1 | async-start | bytes 1048576 | tf_op jit(solution)/shard_map/all_to_all | solution.py:127
  162.2 5.4 %collective-permute-start.22 = (f32[2,2304]{1,0:T(2,128)S(1)}, f32[2,2304]{1,0:T(2,128)S(1)}, u32[]{:S(2)}, u32[]{:S(2)}) collective-permute-start(f32[2,2304]{1,0:T(2,128)S(1)} %fusion.52), channel_id=1, source_target_pairs={{0,2},{2,0},{1,3},{3,1},{4,6},{6,4},{5,7},{7,5},{8,10},{10,8},{9,1... | collective-permute-start | bytes 55304 | tf_op jit(solution)/shard_map/ppermute | solution.py:23
  168.2 7.0 %collective-permute-start.23 = (f32[2,2304]{1,0:T(2,128)}, f32[2,2304]{1,0:T(2,128)}, u32[]{:S(2)}, u32[]{:S(2)}) collective-permute-start(f32[2,2304]{1,0:T(2,128)} %add.212), channel_id=1, source_target_pairs={{0,4},{4,0},{8,12},{12,8},{16,20},{20,16},{24,28},{28,24},{1,5},{5... | collective-permute-start | bytes 55304 | tf_op jit(solution)/shard_map/ppermute | solution.py:23
  175.9 5.8 %collective-permute-start.24 = (f32[2,2304]{1,0:T(2,128)S(1)}, f32[2,2304]{1,0:T(2,128)S(1)}, u32[]{:S(2)}, u32[]{:S(2)}) collective-permute-start(f32[2,2304]{1,0:T(2,128)S(1)} %add.213), channel_id=1, source_target_pairs={{0,8},{4,12},{8,0},{12,4},{16,24},{20,28},{24,16},{28,20},{1,9},{5... | collective-permute-start | bytes 55304 | tf_op jit(solution)/shard_map/ppermute | solution.py:23
  181.7 7.8 %collective-permute-start.25 = (f32[2,2304]{1,0:T(2,128)S(1)}, f32[2,2304]{1,0:T(2,128)S(1)}, u32[]{:S(2)}, u32[]{:S(2)}) collective-permute-start(f32[2,2304]{1,0:T(2,128)S(1)} %add.214), channel_id=1, source_target_pairs={{0,16},{4,20},{8,24},{12,28},{16,0},{20,4},{24,8},{28,12},{1,17},{... | collective-permute-start | bytes 55304 | tf_op jit(solution)/shard_map/ppermute | solution.py:23
  190.8 4.0 %collective-permute-start.26 = (bf16[256,64]{0,1:T(8,128)(2,1)S(1)}, bf16[256,64]{0,1:T(8,128)(2,1)S(1)}, u32[]{:S(2)}, u32[]{:S(2)}) collective-permute-start(bf16[256,64]{0,1:T(8,128)(2,1)S(1)} %get-tuple-element.33), channel_id=1, source_target_pairs={{0,128},{128,0},{1,129},{129,1},{2,130},{130,2},{3,131},{131,3},{4... | collective-permute-start | bytes 98312 | tf_op jit(solution)/shard_map/ppermute | solution.py:18
  192.0 3.9 %collective-permute-start.17 = (bf16[256,64]{0,1:T(8,128)(2,1)S(1)}, bf16[256,64]{0,1:T(8,128)(2,1)S(1)}, u32[]{:S(2)}, u32[]{:S(2)}) collective-permute-start(bf16[256,64]{0,1:T(8,128)(2,1)S(1)} %get-tuple-element.34), channel_id=1, source_target_pairs={{0,128},{128,0},{1,129},{129,1},{2,130},{130,2},{3,131},{131,3},{4... | collective-permute-start | bytes 98312 | tf_op jit(solution)/shard_map/ppermute | solution.py:18
  (10 other events, 36.9 us)

commit v2 on v1

v2 whole, which is shorter than its diff:
```python
import jax
import jax.numpy as jnp
from jax import lax
from jax.experimental import pallas as pl
from jax.experimental.pallas import tpu as pltpu
from jax.sharding import Mesh, PartitionSpec as P

D = 8192


EPS = 1e-05
COEF_A = 0.7978845608028654
COEF_B = 0.044715
F32 = jnp.float32
BF = jnp.bfloat16


def shifted(value, axis, steps):
    count = lax.axis_size(axis)
    return lax.ppermute(value, axis, [(i, (i + steps) % count) for i in range(count)])


def swapped(value, axis, bit):
    count = lax.axis_size(axis)
    return lax.ppermute(value, axis, [(i, i ^ bit) for i in range(count)])


def gelu_value(value):
    inner = jnp.tanh(COEF_A * (value + COEF_B * value * value * value))
    return 0.5 * value * (1.0 + inner)


def gelu_slope(value):
    inner = jnp.tanh(COEF_A * (value + COEF_B * value * value * value))
    return 0.5 * (1.0 + inner) + 0.5 * value * (1.0 - inner * inner) * COEF_A * (
        1.0 + 3.0 * COEF_B * value * value
    )


def take(value, index, axis):
    return lax.dynamic_index_in_dim(value, index, axis, keepdims=False)


def over_dp(value):
    return value + shifted(value, "dp", 1) + shifted(value, "dp", 2) + shifted(value, "dp", 3)


def gather_half(own):
    at_z, even = lax.axis_index("z"), lax.axis_index("xh") == 0
    other = swapped(own, "xh", 1)
    pair = jnp.where(even, jnp.stack([own, other], 1), jnp.stack([other, own], 1))
    whole = jnp.zeros((own.shape[0], 8) + pair.shape[1:], own.dtype)
    whole = lax.dynamic_update_index_in_dim(whole, pair, at_z, 1)
    ahead, behind = pair, pair
    for step in range(1, 5):
        ahead = shifted(ahead, "z", 1)
        if step < 4:
            behind = shifted(behind, "z", -1)
            whole = lax.dynamic_update_index_in_dim(whole, behind, (at_z + step) % 8, 1)
        whole = lax.dynamic_update_index_in_dim(whole, ahead, (at_z + 8 - step) % 8, 1)
    return whole.reshape(own.shape[0], 128, own.shape[2])


def together_kernel(a, b, c, whole):
    for i, part in enumerate((a, b, c)):
        whole[i] = part[0]


def together(a, b, c):
    return pl.pallas_call(
        together_kernel,
        out_shape=jax.ShapeDtypeStruct((3,) + a.shape[1:], a.dtype),
        name="together",
    )(a, b, c)


def in_thirds(value):
    high = value.astype(BF).astype(F32)
    rest = value - high
    middle = rest.astype(BF).astype(F32)
    return high, middle, rest - middle


def entry_kernel(mine, other, gain, shift, w_up, w_down, sent, scaled, grads, rows, extra, turned):
    width = mine.shape[2]
    extra[...] = jnp.zeros_like(extra)
    rows[...] = jnp.zeros_like(rows)
    lane = lax.broadcasted_iota(jnp.int32, (128, 128), 1)
    for half, tokens in enumerate((mine, other)):
        columns = jnp.zeros((128, 128), F32)
        for i in range(2):
            value = tokens[i].astype(F32)
            total = jnp.sum(value, 1, keepdims=True)
            square = jnp.sum(value * value, 1, keepdims=True)
            columns = jnp.where(lane == 2 * i, total, columns)
            columns = jnp.where(lane == 2 * i + 1, square, columns)
            scaled[i, half * 128 : half * 128 + 128, :] = (
                (value - total / width) * gain[...]
            ).astype(BF)
        turned[...] = columns.T
        grads[half * 128 : half * 128 + 128, :] = tokens[2]
        for k, third in enumerate(in_thirds(turned[0:4, :])):
            extra[6 + 4 * half : 10 + 4 * half, k * 128 : k * 128 + 128] = third
    for j, vector in enumerate((gain, shift)):
        for k, third in enumerate(in_thirds(vector[...])):
            rows[3 * j + k : 3 * j + k + 1, :] = third
    sums = jnp.dot(rows[...].astype(BF), w_up[...], preferred_element_type=F32)
    for j in range(2):
        vector = sums[3 * j : 3 * j + 1] + sums[3 * j + 1 : 3 * j + 2] + sums[3 * j + 2 : 3 * j + 3]
        for k, third in enumerate(in_thirds(vector)):
            extra[3 * j + k : 3 * j + k + 1, :] = third
    for i in range(2):
        product = jnp.dot(scaled[i], w_up[...], preferred_element_type=F32).astype(BF)
        for q in range(4):
            sent[q, 64 * i : 64 * i + 64, :] = product[64 * q : 64 * q + 64]
    back = lax.dot_general(
        grads[...], w_down[...], (((1,), (1,)), ((), ())), preferred_element_type=F32
    ).astype(BF)
    for q in range(4):
        sent[q, 128:192, :] = back[64 * q : 64 * q + 64]
        sent[q, 192:208, :] = extra[...].astype(BF)


def entry(mine, other, gain, shift, w_up, w_down):
    return pl.pallas_call(
        entry_kernel,
        in_specs=[pl.BlockSpec(memory_space=pltpu.VMEM)] * 6,
        out_specs=pl.BlockSpec(memory_space=pltpu.VMEM),
        out_shape=jax.ShapeDtypeStruct((4, 208, 512), BF),
        scratch_shapes=[
            pltpu.VMEM((2, 256, 2048), BF),
            pltpu.VMEM((256, 2048), BF),
            pltpu.VMEM((8, 2048), F32),
            pltpu.VMEM((16, 512), F32),
            pltpu.VMEM((128, 128), F32),
        ],
        compiler_params=pltpu.CompilerParams(vmem_limit_bytes=28 * 2**20),
        cost_estimate=pl.CostEstimate(
            flops=2**31, bytes_accessed=8 * 2**20, transcendentals=0
        ),
        name="entry",
    )(mine, other, gain, shift, w_up, w_down)


def middle_kernel(at_dp, parts, bias, quarter, stats, rows):
    extra = parts[:, 192:208, :].astype(F32)
    weights = [
        [extra[y, 3 * j : 3 * j + 1] + extra[y, 3 * j + 1 : 3 * j + 2] + extra[y, 3 * j + 2 : 3 * j + 3] for y in range(4)]
        for j in range(2)
    ]
    offset = weights[1][0] + weights[1][1] + weights[1][2] + weights[1][3] + bias[...]
    rows[...] = jnp.zeros_like(rows)
    for half in range(2):
        block = extra[:, 6 + 4 * half : 10 + 4 * half, :]
        sums = block[:, :, 0:128] + block[:, :, 128:256] + block[:, :, 256:384]
        whole = sums[0] + sums[1] + sums[2] + sums[3]
        for i in range(2):
            mean = whole[2 * i : 2 * i + 1] / D
            square = whole[2 * i + 1 : 2 * i + 2] / D
            rows[2 * i : 2 * i + 1, :] = mean
            rows[2 * i + 1 : 2 * i + 2, :] = lax.rsqrt(square - mean * mean + EPS)
            for y in range(4):
                at = 4 + 4 * i + y
                rows[at : at + 1, :] = sums[y, 2 * i : 2 * i + 1] / (D // 4) - mean
        stats[half * 128 : half * 128 + 128, :] = rows[...].T
    own = stats[pl.ds(pl.multiple_of(at_dp[0] * 64, 64), 64), :]
    for i in range(2):
        total = jnp.zeros((64, 512), F32)
        for y in range(4):
            at = 4 + 4 * i + y
            total += parts[y, 64 * i : 64 * i + 64, :].astype(F32)
            total += own[:, at : at + 1] * weights[0][y]
        pre = own[:, 2 * i + 1 : 2 * i + 2] * total + offset
        quarter[i] = gelu_value(pre).astype(BF)
    back = parts[0, 128:192, :].astype(F32)
    for y in range(1, 4):
        back += parts[y, 128:192, :].astype(F32)
    quarter[2] = (back * gelu_slope(pre)).astype(BF)


def middle(parts, bias):
    return pl.pallas_call(
        middle_kernel,
        in_specs=[pl.BlockSpec(memory_space=pltpu.SMEM)]
        + [pl.BlockSpec(memory_space=pltpu.VMEM)] * 2,
        out_specs=[pl.BlockSpec(memory_space=pltpu.VMEM)] * 2,
        out_shape=[
            jax.ShapeDtypeStruct((3, 64, 512), BF),
            jax.ShapeDtypeStruct((256, 128), F32),
        ],
        scratch_shapes=[pltpu.VMEM((128, 128), F32)],
        compiler_params=pltpu.CompilerParams(vmem_limit_bytes=12 * 2**20),
        cost_estimate=pl.CostEstimate(
            flops=2**22, bytes_accessed=2**20, transcendentals=2**17
        ),
        name="middle",
    )(lax.axis_index("dp").reshape(1), parts, bias)


def products_kernel(
    at_dp, own, next1, next2, next3, w_up, w_down, mine, other, stats, gain,
    kept, given, hidden, bias_grad, params, moments, plain, crossed,
):
    step = pl.program_id(0)

    @pl.when(step == 0)
    def _():
        for k, quarter in enumerate((own, next1, next2, next3)):
            row = pl.multiple_of(((at_dp[0] + k) % 4) * 64, 64)
            for i in range(3):
                hidden[i, pl.ds(row, 64), :] = quarter[i]
        bias_grad[...] = jnp.sum(hidden[2].astype(F32), 0, keepdims=True)
        plain[...] = jnp.zeros_like(plain)
        crossed[...] = jnp.zeros_like(crossed)

    branch = jnp.dot(hidden[0], w_down[...], preferred_element_type=F32)
    back = lax.dot_general(
        hidden[2], w_up[...], (((1,), (1,)), ((), ())), preferred_element_type=F32
    )
    for h in range(2):
        lanes = slice(h * 128, h * 128 + 128)
        for i, product in enumerate((branch, back)):
            kept[0, h, i] = product[:128, lanes]
            given[0, h, i] = product[128:, lanes].astype(BF)
    saved = jnp.concatenate([mine[0], other[0]]).astype(F32)
    centered = (saved - stats[:, 2:3]) * stats[:, 3:4]
    crossing = back * centered
    params[0:1, :] = jnp.sum(crossing, 0, keepdims=True)
    params[1:2, :] = jnp.sum(back, 0, keepdims=True)
    plain[...] += back * gain[...]
    crossed[...] += crossing * gain[...]

    @pl.when(step == 7)
    def _():
        ones = jnp.ones((8, 256), F32)
        for i, total in enumerate((plain, crossed)):
            row = lax.dot_general(
                ones, total[...], (((1,), (1,)), ((), ())),
                precision=lax.Precision.HIGHEST, preferred_element_type=F32,
            )
            moments[i : i + 1, :] = row[0:1]


def products(quarters, w_up, w_down, mine, other, stats, gain):
    whole = lambda *shape: pl.BlockSpec(shape, lambda i: (0,) * len(shape))
    out = lambda shape, kind: jax.ShapeDtypeStruct(shape, kind)
    return pl.pallas_call(
        products_kernel,
        grid=(8,),
        in_specs=[pl.BlockSpec(memory_space=pltpu.SMEM)]
        + [whole(3, 64, 512)] * 4
        + [
            pl.BlockSpec((256, 512), lambda i: (i, 0)),
            pl.BlockSpec((512, 256), lambda i: (0, i)),
            pl.BlockSpec((1, 128, 256), lambda i: (1, 0, i)),
            pl.BlockSpec((1, 128, 256), lambda i: (1, 0, i)),
            whole(256, 128),
            pl.BlockSpec((1, 256), lambda i: (0, i)),
        ],
        out_specs=[
            pl.BlockSpec((1, 2, 2, 128, 128), lambda i: (i, 0, 0, 0, 0)),
            pl.BlockSpec((1, 2, 2, 128, 128), lambda i: (i, 0, 0, 0, 0)),
            whole(3, 256, 512),
            whole(1, 512),
            pl.BlockSpec((2, 256), lambda i: (0, i)),
            whole(2, 256),
        ],
        out_shape=[
            out((8, 2, 2, 128, 128), F32),
            out((8, 2, 2, 128, 128), BF),
            out((3, 256, 512), BF),
            out((1, 512), F32),
            out((2, 2048), F32),
            out((2, 256), F32),
        ],
        scratch_shapes=[pltpu.VMEM((256, 256), F32)] * 2,
        compiler_params=pltpu.CompilerParams(vmem_limit_bytes=12 * 2**20),
        cost_estimate=pl.CostEstimate(
            flops=2**31, bytes_accessed=10 * 2**20, transcendentals=0
        ),
        name="products",
    )(lax.axis_index("dp").reshape(1), *quarters, w_up, w_down, mine, other, stats, gain)


def relayed(tiles):
    count = tiles.shape[0]
    even = lax.axis_index("core") == 0
    low, high = tiles[:, :, :64], tiles[:, :, 64:]
    same = swapped(jnp.where(even, low, high), "section", 1)
    cross = lax.ppermute(jnp.where(even, high, low), ("section", "core"), [(i, 3 - i) for i in range(4)])
    same, cross = same.reshape(count, 16, 8, 64), cross.reshape(count, 16, 8, 64)
    joined = jnp.where(even, jnp.stack([same, cross], 2), jnp.stack([cross, same], 2))
    return joined.reshape(count, 256, 64)


def local(
    section_input,
    saved_input,
    cotangent,
    norm_gain,
    norm_shift,
    up_weight,
    up_bias,
    down_weight,
    down_bias,
):
    gain, shift = (norm_gain[0], norm_shift[0])
    w_up, w_down = (up_weight[0], down_weight[0])
    bias_up, bias_down = (up_bias[0], down_bias[0])
    at_z, at_h = (lax.axis_index("z"), lax.axis_index("xh"))
    first_column = at_z * 256 + at_h * 128

    mine = gather_half(together(section_input, saved_input, cotangent))
    other = swapped(mine, "core", 1)

    parts = entry(mine, other, gain[None], shift[None], w_up, w_down)
    parts = lax.all_to_all(parts, "dp", 0, 0, tiled=False)
    quarter, stats = middle(parts, bias_up[None])
    quarters = [quarter] + [shifted(quarter, "dp", -k) for k in (1, 2, 3)]

    kept, given, hidden, bias_grad, params, moments = products(
        quarters, w_up, w_down, mine, other, stats, gain[None]
    )
    summed = kept + swapped(given, "core", 1).astype(F32)
    given = take(summed, 1 - at_h, 1).astype(BF)
    small = jnp.concatenate([moments, params], 1)
    kept = take(summed, at_h, 1) + swapped(given, "xh", 1).astype(F32)
    for bit in (1, 2, 4):
        small = small + swapped(small, "z", bit)
    tiles = jnp.sum(lax.all_to_all(kept.astype(BF), "z", 0, 0, tiled=False).astype(F32), 0)
    small = jnp.concatenate([small[:, :128], small[:, 256:]], 1) + swapped(
        small[:, 128:], "core", 1
    )
    small = small + swapped(small, "xh", 1)
    small = jnp.concatenate([over_dp(small[:, :128]), small[:, 128:]], 1)
    moments, params = small[:, :128], small[:, 128:]

    def own_tile(value):
        return lax.dynamic_slice_in_dim(value, first_column, 128, 1).astype(F32)

    def own_columns(vector):
        return lax.dynamic_slice_in_dim(vector, first_column, 128, 0)

    out = (own_tile(mine[0]) + tiles[0] + own_columns(bias_down)).astype(BF)

    rstd_rows = stats[:128, 3:4]
    centered_tile = (own_tile(mine[1]) - stats[:128, 2:3]) * rstd_rows
    first, second = moments[0][:, None] / D, moments[1][:, None] / D
    grad_in = own_tile(mine[2]) + rstd_rows * (
        tiles[1] * own_columns(gain) - first - centered_tile * second
    )
    arrived = relayed(jnp.stack([out, grad_in.astype(BF)]))

    grad_full = jnp.concatenate([mine[2], other[2]])
    saved = jnp.concatenate([mine[1], other[1]]).astype(F32)
    normed = ((saved - stats[:, 2:3]) * stats[:, 3:4] * gain + shift).astype(BF)
    down_weight_grad = lax.dot_general(
        hidden[1], grad_full, (((0,), (0,)), ((), ())), preferred_element_type=F32
    ).astype(BF)
    down_bias_grad = jnp.sum(grad_full.astype(F32), 0)
    up_weight_grad = lax.dot_general(
        normed, hidden[2], (((0,), (0,)), ((), ())), preferred_element_type=F32
    ).astype(BF)
    return (
        arrived[0][None],
        arrived[1][None],
        up_weight_grad[None],
        bias_grad,
        down_weight_grad[None],
        down_bias_grad[None],
        params[0][None],
        params[1][None],
    )


def solution(mesh):
    names = ("section", "dp", "z", "xh", "core")
    split = Mesh(mesh.devices.reshape(2, 4, 8, 2, 2), names)
    mp = ("z", "xh", "core")
    specs = (
        P("section", mp, "dp"),
        P("section", mp, "dp"),
        P("section", mp, "dp"),
        P("section", "dp"),
        P("section", "dp"),
        P("section", "dp", mp),
        P("section", mp),
        P("section", mp, "dp"),
        P("section", "dp"),
    )
    return jax.shard_map(
        local,
        mesh=split,
        in_specs=specs,
        out_specs=(
            P("section", None, ("dp",) + mp),
            P("section", None, ("dp",) + mp),
            P("section", "dp", mp),
            P("section", mp),
            P("section", mp, "dp"),
            P("section", "dp"),
            P("section", "dp"),
            P("section", "dp"),
        ),
        check_vma=False,
    )
```

time: 198 us -> 148 us (0.75)
  the two profiles are of different devices: /device:TPU:4 before, /device:TPU:1 now
where the time goes in v2:
time: 148 us; the launch traced here: 147 us
  waiting for transfers between devices  71.2 us (48%)
  starting transfers between devices  45.6 us (31%)
  Pallas kernels  11.6 us (8%)
  local copies, waits for them, and re-layouts  9.12 us (6%)
  matrix products  4.37 us (3%)
  other arithmetic  4.22 us (3%)
    ppermute x13, waiting for transfers between devices, shifted(): lax.ppermute(value, axis, [(i, (i + steps) % count) for i in range(count)])  29.4 us
    ppermute x10, starting transfers between devices, swapped(): return lax.ppermute(value, axis, [(i, i ^ bit) for i in range(count)])  20.6 us
    ppermute x10, waiting for transfers between devices, swapped(): return lax.ppermute(value, axis, [(i, i ^ bit) for i in range(count)])  19.3 us
    ppermute x13, starting transfers between devices, shifted(): lax.ppermute(value, axis, [(i, (i + steps) % count) for i in range(count)])  16.6 us
    all_to_all x1, waiting for transfers between devices, local(): parts = lax.all_to_all(parts, 'dp', 0, 0, tiled=False)  12.5 us
    all_to_all x1, waiting for transfers between devices, local(): lax.all_to_all(kept.astype(BF), 'z', 0, 0, tiled=False).astype(F32)  8.04 us
    pallas_call x1, Pallas kernels, products(): pl.pallas_call(products_kernel, grid=(8,), in_specs=[pl.BlockSpec(memory_...  6.06 us
    unnamed x39, local copies, waits for them, and re-layouts  5.57 us
  transfers between devices with their start and end apart: 26, of which 20 were waited for; matrix products, arithmetic and copies ran while one was open for 7% of the time, Pallas kernels for 0%

profile of v2, /device:TPU:1, one launch (start us, length us, event | category | flops | bytes accessed | tf_op | source)
XLA Modules:
  0.0 147.1 jit_solution(6966584595495975188)
XLA Ops:
  2.1 3.6 %collective-permute-start = (bf16[3,8,2048]{2,1,0:T(8,128)(2,1)}, bf16[3,8,2048]{2,1,0:T(8,128)(2,1)S(1)}, u32[]{:S(2)}, u32[]{:S(2)}) collective-permute-start(bf16[3,8,2048]{2,1,0:T(8,128)(2,1)} %together.1), channel_id=1, source_target_pairs={{0,2},{2,0},{1,3},{3,1},{4,6},{6,4},{5,7},{7,5},{8,10},{10,8},{9,1... | collective-permute-start | bytes 294920 | tf_op jit(solution)/shard_map/ppermute | solution.py:25
  5.7 2.3 %collective-permute-done = bf16[3,8,2048]{2,1,0:T(8,128)(2,1)S(1)} collective-permute-done((bf16[3,8,2048]{2,1,0:T(8,128)(2,1)}, bf16[3,8,2048]{2,1,0:T(8,128)(2,1)S(1)}, u32[]{:S(2)}, u32[]{:S(2)}) %collective-permute-start) | collective-permute-done | bytes 98336 | tf_op jit(solution)/shard_map/ppermute | solution.py:25
  9.0 5.8 %collective-permute-start.1 = (bf16[3,2,8,2048]{3,2,0,1:T(8,128)(2,1)S(1)}, bf16[3,2,8,2048]{3,2,0,1:T(8,128)(2,1)S(1)}, u32[]{:S(2)}, u32[]{:S(2)}) collective-permute-start(bf16[3,2,8,2048]{3,2,0,1:T(8,128)(2,1)S(1)} %maximum_select_fusion.1), channel_id=1, source_target_pairs={{0,28},{4,0},{8,4},{12,8},{16,12},{20,16},{24,20},{28,24},{1,29},{... | collective-permute-start | bytes 589832 | tf_op jit(solution)/shard_map/ppermute | solution.py:20
  15.0 2.3 %collective-permute-done.1 = bf16[3,2,8,2048]{3,2,0,1:T(8,128)(2,1)S(1)} collective-permute-done((bf16[3,2,8,2048]{3,2,0,1:T(8,128)(2,1)S(1)}, bf16[3,2,8,2048]{3,2,0,1:T(8,128)(2,1)S(1)}, u32[]{:S(2)}, u32[]{:S(2)}) %collective-permute-start.1) | collective-permute-done | bytes 196640 | tf_op jit(solution)/shard_map/ppermute | solution.py:20
  17.4 3.1 %collective-permute-start.3 = (bf16[3,2,8,2048]{3,2,0,1:T(8,128)(2,1)S(1)}, bf16[3,2,8,2048]{3,2,0,1:T(8,128)(2,1)S(1)}, u32[]{:S(2)}, u32[]{:S(2)}) collective-permute-start(bf16[3,2,8,2048]{3,2,0,1:T(8,128)(2,1)S(1)} %collective-permute-done.1), channel_id=1, source_target_pairs={{0,28},{4,0},{8,4},{12,8},{16,12},{20,16},{24,20},{28,24},{1,29},{... | collective-permute-start | bytes 589832 | tf_op jit(solution)/shard_map/ppermute | solution.py:20
  20.5 2.6 %collective-permute-done.3 = bf16[3,2,8,2048]{3,2,0,1:T(8,128)(2,1)S(1)} collective-permute-done((bf16[3,2,8,2048]{3,2,0,1:T(8,128)(2,1)S(1)}, bf16[3,2,8,2048]{3,2,0,1:T(8,128)(2,1)S(1)}, u32[]{:S(2)}, u32[]{:S(2)}) %collective-permute-start.3) | collective-permute-done | bytes 196640 | tf_op jit(solution)/shard_map/ppermute | solution.py:20
  23.1 3.1 %collective-permute-start.5 = (bf16[3,2,8,2048]{3,2,0,1:T(8,128)(2,1)S(1)}, bf16[3,2,8,2048]{3,2,0,1:T(8,128)(2,1)S(1)}, u32[]{:S(2)}, u32[]{:S(2)}) collective-permute-start(bf16[3,2,8,2048]{3,2,0,1:T(8,128)(2,1)S(1)} %collective-permute-done.3), channel_id=1, source_target_pairs={{0,28},{4,0},{8,4},{12,8},{16,12},{20,16},{24,20},{28,24},{1,29},{... | collective-permute-start | bytes 589832 | tf_op jit(solution)/shard_map/ppermute | solution.py:20
  26.3 5.8 %collective-permute-done.6 = bf16[3,2,8,2048]{3,2,0,1:T(8,128)(2,1)S(1)} collective-permute-done((bf16[3,2,8,2048]{3,2,0,1:T(8,128)(2,1)S(1)}, bf16[3,2,8,2048]{3,2,0,1:T(8,128)(2,1)S(1)}, u32[]{:S(2)}, u32[]{:S(2)}) %collective-permute-start.6) | collective-permute-done | bytes 196640 | tf_op jit(solution)/shard_map/ppermute | solution.py:20
  32.1 6.8 %collective-permute-done.7 = bf16[3,2,8,2048]{3,2,0,1:T(8,128)(2,1)S(1)} collective-permute-done((bf16[3,2,8,2048]{3,2,0,1:T(8,128)(2,1)S(1)}, bf16[3,2,8,2048]{3,2,0,1:T(8,128)(2,1)S(1)}, u32[]{:S(2)}, u32[]{:S(2)}) %collective-permute-start.7) | collective-permute-done | bytes 196640 | tf_op jit(solution)/shard_map/ppermute | solution.py:20
  39.0 6.7 %collective-permute-start.8 = (bf16[3,128,2048]{2,1,0:T(8,128)(2,1)S(1)}, bf16[3,128,2048]{2,1,0:T(8,128)(2,1)S(1)}, u32[]{:S(2)}, u32[]{:S(2)}) collective-permute-start(bf16[3,128,2048]{2,1,0:T(8,128)(2,1)S(1)} %bitcast.103), channel_id=1, source_target_pairs={{0,1},{1,0},{2,3},{3,2},{4,5},{5,4},{6,7},{7,6},{8,9},{9,8},{10,11... | collective-permute-start | bytes 4718600 | tf_op jit(solution)/shard_map/ppermute | solution.py:25
  45.7 3.0 %collective-permute-done.8.other = bf16[3,128,2048]{2,1,0:T(8,128)(2,1)S(1)} collective-permute-done((bf16[3,128,2048]{2,1,0:T(8,128)(2,1)S(1)}, bf16[3,128,2048]{2,1,0:T(8,128)(2,1)S(1)}, u32[]{:S(2)}, u32[]{:S(2)}) %collective-permute-start.8) | collective-permute-done | bytes 1572896 | tf_op jit(solution)/shard_map/ppermute | solution.py:25
  48.8 2.4 %entry.1 = bf16[4,208,512]{2,1,0:T(8,128)(2,1)S(1)} custom-call(bf16[3,128,2048]{2,1,0:T(8,128)(2,1)S(1)} %bitcast.104, bf16[3,128,2048]{2,1,0:T(8,128)(2,1)S(1)} %collective-permute-done.8.other, f32[1,2048]{1,0:T(1,128)S(1)} %copy-done.6, f32[1,2048]{1,0:T(1,128)S(1)} %copy-done.7, bf16[2048,512]{1,0:T(8,128)(2,1)S(1)} %bitcast.106, ...), custom_call_target="tpu_custom_call" | custom-call | flops 2147483648 | bytes 8388608 | tf_op jit(solution)/shard_map/entry/pallas_call | solution.py:125
  52.1 4.2 %all-to-all-start = ((bf16[4,208,512]{2,1,0:T(8,128)(2,1)}), bf16[4,208,512]{2,1,0:T(8,128)(2,1)}, u32[]{:S(2)}, u32[]{:S(2)}) async-start(bf16[4,208,512]{2,1,0:T(8,128)(2,1)} %copy-done.5), calls=%async_computation | async-start | bytes 1703936 | tf_op jit(solution)/shard_map/all_to_all | solution.py:317
  56.3 12.5 %all-to-all-done.parts = bf16[4,208,512]{2,1,0:T(8,128)(2,1)} async-done(((bf16[4,208,512]{2,1,0:T(8,128)(2,1)}), bf16[4,208,512]{2,1,0:T(8,128)(2,1)}, u32[]{:S(2)}, u32[]{:S(2)}) %all-to-all-start) | async-done | bytes 852000 | tf_op jit(solution)/shard_map/all_to_all | solution.py:317
  68.8 1.7 %middle.1 = (bf16[3,64,512]{2,1,0:T(8,128)(2,1)S(1)}, f32[256,128]{1,0:T(8,128)S(1)}) custom-call(s32[1]{0:T(128)} %bitcast.12.at_dp, bf16[4,208,512]{2,1,0:T(8,128)(2,1)} %all-to-all-done.parts, f32[1,512]{1,0:T(1,128)S(1)} %copy-done.8), custom_call_target="tpu_custom_call" | custom-call | flops 4194304 | bytes 1048576 | tf_op jit(solution)/shard_map/middle/pallas_call | solution.py:182
  72.7 2.7 %collective-permute-done.9.next1 = bf16[3,64,512]{2,1,0:T(8,128)(2,1)} collective-permute-done((bf16[3,64,512]{2,1,0:T(8,128)(2,1)S(1)}, bf16[3,64,512]{2,1,0:T(8,128)(2,1)}, u32[]{:S(2)}, u32[]{:S(2)}) %collective-permute-start.9) | collective-permute-done | bytes 196640 | tf_op jit(solution)/shard_map/ppermute | solution.py:20
  75.5 2.2 %collective-permute-done.10.next2 = bf16[3,64,512]{2,1,0:T(8,128)(2,1)} collective-permute-done((bf16[3,64,512]{2,1,0:T(8,128)(2,1)S(1)}, bf16[3,64,512]{2,1,0:T(8,128)(2,1)}, u32[]{:S(2)}, u32[]{:S(2)}) %collective-permute-start.10) | collective-permute-done | bytes 196640 | tf_op jit(solution)/shard_map/ppermute | solution.py:20
  77.7 5.6 %collective-permute-done.11.next3 = bf16[3,64,512]{2,1,0:T(8,128)(2,1)} collective-permute-done((bf16[3,64,512]{2,1,0:T(8,128)(2,1)S(1)}, bf16[3,64,512]{2,1,0:T(8,128)(2,1)}, u32[]{:S(2)}, u32[]{:S(2)}) %collective-permute-start.11) | collective-permute-done | bytes 196640 | tf_op jit(solution)/shard_map/ppermute | solution.py:20
  83.3 1.6 %copy-done.2 = bf16[1,2048,512]{2,1,0:T(8,128)(2,1)S(1)} copy-done((bf16[1,2048,512]{2,1,0:T(8,128)(2,1)S(1)}, bf16[1,2048,512]{2,1,0:T(8,128)(2,1)}, u32[]{:S(2)}) %copy-start.2) | copy-done | bytes 2097176
  84.9 1.6 %copy-done.4 = bf16[1,512,2048]{2,1,0:T(8,128)(2,1)S(1)} copy-done((bf16[1,512,2048]{2,1,0:T(8,128)(2,1)S(1)}, bf16[1,512,2048]{2,1,0:T(8,128)(2,1)}, u32[]{:S(2)}) %copy-start.4) | copy-done | bytes 2097176
  86.5 6.1 %products.1 = (f32[8,2,2,128,128]{4,3,2,1,0:T(8,128)S(1)}, bf16[8,2,2,128,128]{4,3,2,1,0:T(8,128)(2,1)S(1)}, bf16[3,256,512]{2,1,0:T(8,128)(2,1)S(1)}, f32[1,512...) custom-call(s32[1]{0:T(128)} %bitcast.12.at_dp, bf16[3,64,512]{2,1,0:T(8,128)(2,1)S(1)} %get-tuple-element.16.own, ...), custom_call_target="tpu_custom_call" | custom-call | flops 2147483648 | bytes 10485760 | tf_op jit(solution)/shard_map/products/pallas_call | solution.py:247
  96.5 2.8 %collective-permute-start.13 = (bf16[8,2,128,128]{3,2,1,0:T(8,128)(2,1)S(1)}, bf16[8,2,128,128]{3,2,1,0:T(8,128)(2,1)S(1)}, u32[]{:S(2)}, u32[]{:S(2)}) collective-permute-start(bf16[8,2,128,128]{3,2,1,0:T(8,128)(2,1)S(1)} %fusion.10), channel_id=1, source_target_pairs={{0,2},{2,0},{1,3},{3,1},{4,6},{6,4},{5,7},{7,5},{8,10},{10,8},{9,1... | collective-permute-start | bytes 1572872 | tf_op jit(solution)/shard_map/ppermute | solution.py:25
  100.1 2.1 %collective-permute-done.14 = f32[2,2304]{1,0:T(2,128)S(1)} collective-permute-done((f32[2,2304]{1,0:T(2,128)S(1)}, f32[2,2304]{1,0:T(2,128)S(1)}, u32[]{:S(2)}, u32[]{:S(2)}) %collective-permute-start.14) | collective-permute-done | bytes 18464 | tf_op jit(solution)/shard_map/ppermute | solution.py:25
  102.6 3.5 %collective-permute-done.15 = f32[2,2304]{1,0:T(2,128)S(1)} collective-permute-done((f32[2,2304]{1,0:T(2,128)S(1)}, f32[2,2304]{1,0:T(2,128)S(1)}, u32[]{:S(2)}, u32[]{:S(2)}) %collective-permute-start.15) | collective-permute-done | bytes 18464 | tf_op jit(solution)/shard_map/ppermute | solution.py:25
  107.3 5.4 %collective-permute-done.16 = f32[2,2304]{1,0:T(2,128)S(1)} collective-permute-done((f32[2,2304]{1,0:T(2,128)S(1)}, f32[2,2304]{1,0:T(2,128)S(1)}, u32[]{:S(2)}, u32[]{:S(2)}) %collective-permute-start.16) | collective-permute-done | bytes 18464 | tf_op jit(solution)/shard_map/ppermute | solution.py:25
  112.8 3.6 %collective-permute-start.17 = (f32[2,2176]{1,0:T(2,128)S(1)}, f32[2,2176]{1,0:T(2,128)S(1)}, u32[]{:S(2)}, u32[]{:S(2)}) collective-permute-start(f32[2,2176]{1,0:T(2,128)S(1)} %slice.122), channel_id=1, source_target_pairs={{0,1},{1,0},{2,3},{3,2},{4,5},{5,4},{6,7},{7,6},{8,9},{9,8},{10,11... | collective-permute-start | bytes 52232 | tf_op jit(solution)/shard_map/ppermute | solution.py:25
  117.3 3.5 %all-to-all-start.1 = ((bf16[8,2,128,128]{3,2,1,0:T(8,128)(2,1)}), bf16[8,2,128,128]{3,2,1,0:T(8,128)(2,1)S(1)}, u32[]{:S(2)}, u32[]{:S(2)}) async-start(bf16[8,2,128,128]{3,2,1,0:T(8,128)(2,1)} %fusion.5), calls=%async_computation.1 | async-start | bytes 1048576 | tf_op jit(solution)/shard_map/all_to_all | solution.py:330
  121.2 2.3 %fusion = bf16[1,2048,512]{2,1,0:T(8,128)(2,1)} fusion(bf16[128,2048]{1,0:T(8,128)(2,1)S(1)} %copy-done.17, bf16[128,2048]{1,0:T(8,128)(2,1)S(1)} %bitcast.118, f32[2048]{0:T(1024)S(1)} %bitcast.111, f32[2048]{0:T(1024)S(1)} %bitcast.110, f32[256]{0:T(256)S(1)} %get-tuple-element.33, f32[256]{0:T(256)S(1)} %get-tuple-element.32, ...), kind=kOutput, calls=%fused_computation.2 | convolution fusion | flops 542638080 | bytes 3426304 | tf_op jit(solution)/shard_map/dot_general | solution.py:361
  123.5 1.5 %collective-permute-done.18 = f32[2,2176]{1,0:T(2,128)S(1)} collective-permute-done((f32[2,2176]{1,0:T(2,128)S(1)}, f32[2,2176]{1,0:T(2,128)S(1)}, u32[]{:S(2)}, u32[]{:S(2)}) %collective-permute-start.18) | collective-permute-done | bytes 17440 | tf_op jit(solution)/shard_map/ppermute | solution.py:25
  127.3 2.1 %fusion.1 = bf16[1,512,2048]{2,1,0:T(8,128)(2,1)} fusion(bf16[128,2048]{1,0:T(8,128)(2,1)S(1)} %copy-done.14, bf16[128,2048]{1,0:T(8,128)(2,1)S(1)} %bitcast.113, bf16[3,256,512]{2,1,0:T(8,128)(2,1)S(1)} %copy-done.10), kind=kOutput, calls=%fused_computation.3 | convolution fusion | flops 540016640 | bytes 3407872 | tf_op jit(solution)/shard_map/dot_general | solution.py:357
  130.7 8.0 %all-to-all-done.1 = bf16[8,2,128,128]{3,2,1,0:T(8,128)(2,1)S(1)} async-done(((bf16[8,2,128,128]{3,2,1,0:T(8,128)(2,1)}), bf16[8,2,128,128]{3,2,1,0:T(8,128)(2,1)S(1)}, u32[]{:S(2)}, u32[]{:S(2)}) %all-to-all-start.1) | async-done | bytes 524320 | tf_op jit(solution)/shard_map/all_to_all | solution.py:330
  142.4 2.0 %collective-permute-done.23 = bf16[2,128,64]{2,1,0:T(8,128)(2,1)S(1)} collective-permute-done((bf16[2,128,64]{2,1,0:T(8,128)(2,1)S(1)}, bf16[2,128,64]{2,1,0:T(8,128)(2,1)S(1)}, u32[]{:S(2)}, u32[]{:S(2)}) %collective-permute-start.23) | collective-permute-done | bytes 32800 | tf_op jit(solution)/shard_map/ppermute | solution.py:290
  (103 shorter events, 23.5 us)
Async XLA Ops:
  0.6 93.2 %copy-start = (f32[1,2048]{1,0:T(1,128)S(1)}, f32[1,2048]{1,0:T(1,128)}, u32[]{:S(2)}) copy-start(f32[1,2048]{1,0:T(1,128)} %param.17) | copy-start | bytes 24580
  2.1 5.9 %collective-permute-start = (bf16[3,8,2048]{2,1,0:T(8,128)(2,1)}, bf16[3,8,2048]{2,1,0:T(8,128)(2,1)S(1)}, u32[]{:S(2)}, u32[]{:S(2)}) collective-permute-start(bf16[3,8,2048]{2,1,0:T(8,128)(2,1)} %together.1), channel_id=1, source_target_pairs={{0,2},{2,0},{1,3},{3,1},{4,6},{6,4},{5,7},{7,5},{8,10},{10,8},{9,1... | collective-permute-start | bytes 294920 | tf_op jit(solution)/shard_map/ppermute | solution.py:25
  9.0 8.4 %collective-permute-start.1 = (bf16[3,2,8,2048]{3,2,0,1:T(8,128)(2,1)S(1)}, bf16[3,2,8,2048]{3,2,0,1:T(8,128)(2,1)S(1)}, u32[]{:S(2)}, u32[]{:S(2)}) collective-permute-start(bf16[3,2,8,2048]{3,2,0,1:T(8,128)(2,1)S(1)} %maximum_select_fusion.1), channel_id=1, source_target_pairs={{0,28},{4,0},{8,4},{12,8},{16,12},{20,16},{24,20},{28,24},{1,29},{... | collective-permute-start | bytes 589832 | tf_op jit(solution)/shard_map/ppermute | solution.py:20
  14.8 5.7 %collective-permute-start.2 = (bf16[3,2,8,2048]{3,2,0,1:T(8,128)(2,1)S(1)}, bf16[3,2,8,2048]{3,2,0,1:T(8,128)(2,1)S(1)}, u32[]{:S(2)}, u32[]{:S(2)}) collective-permute-start(bf16[3,2,8,2048]{3,2,0,1:T(8,128)(2,1)S(1)} %maximum_select_fusion.1), channel_id=1, source_target_pairs={{0,4},{4,8},{8,12},{12,16},{16,20},{20,24},{24,28},{28,0},{1,5},{5... | collective-permute-start | bytes 589832 | tf_op jit(solution)/shard_map/ppermute | solution.py:20
  14.8 34.0 %copy-start.1 = (bf16[1,2048,512]{2,1,0:T(8,128)(2,1)S(1)}, bf16[1,2048,512]{2,1,0:T(8,128)(2,1)}, u32[]{:S(2)}) copy-start(bf16[1,2048,512]{2,1,0:T(8,128)(2,1)} %param.14) | copy-start | bytes 6291460
  14.8 34.0 %copy-start.3 = (bf16[1,512,2048]{2,1,0:T(8,128)(2,1)S(1)}, bf16[1,512,2048]{2,1,0:T(8,128)(2,1)}, u32[]{:S(2)}) copy-start(bf16[1,512,2048]{2,1,0:T(8,128)(2,1)} %param.16) | copy-start | bytes 6291460
  14.8 34.0 %copy-start.6 = (f32[1,2048]{1,0:T(1,128)S(1)}, f32[1,2048]{1,0:T(1,128)}, u32[]{:S(2)}) copy-start(f32[1,2048]{1,0:T(1,128)} %gain.3) | copy-start | bytes 24580
  14.8 34.0 %copy-start.7 = (f32[1,2048]{1,0:T(1,128)S(1)}, f32[1,2048]{1,0:T(1,128)}, u32[]{:S(2)}) copy-start(f32[1,2048]{1,0:T(1,128)} %shift.1) | copy-start | bytes 24580
  17.4 5.7 %collective-permute-start.3 = (bf16[3,2,8,2048]{3,2,0,1:T(8,128)(2,1)S(1)}, bf16[3,2,8,2048]{3,2,0,1:T(8,128)(2,1)S(1)}, u32[]{:S(2)}, u32[]{:S(2)}) collective-permute-start(bf16[3,2,8,2048]{3,2,0,1:T(8,128)(2,1)S(1)} %collective-permute-done.1), channel_id=1, source_target_pairs={{0,28},{4,0},{8,4},{12,8},{16,12},{20,16},{24,20},{28,24},{1,29},{... | collective-permute-start | bytes 589832 | tf_op jit(solution)/shard_map/ppermute | solution.py:20
  20.5 5.7 %collective-permute-start.4 = (bf16[3,2,8,2048]{3,2,0,1:T(8,128)(2,1)S(1)}, bf16[3,2,8,2048]{3,2,0,1:T(8,128)(2,1)S(1)}, u32[]{:S(2)}, u32[]{:S(2)}) collective-permute-start(bf16[3,2,8,2048]{3,2,0,1:T(8,128)(2,1)S(1)} %collective-permute-done.2), channel_id=1, source_target_pairs={{0,4},{4,8},{8,12},{12,16},{16,20},{20,24},{24,28},{28,0},{1,5},{5... | collective-permute-start | bytes 589832 | tf_op jit(solution)/shard_map/ppermute | solution.py:20
  23.1 8.9 %collective-permute-start.5 = (bf16[3,2,8,2048]{3,2,0,1:T(8,128)(2,1)S(1)}, bf16[3,2,8,2048]{3,2,0,1:T(8,128)(2,1)S(1)}, u32[]{:S(2)}, u32[]{:S(2)}) collective-permute-start(bf16[3,2,8,2048]{3,2,0,1:T(8,128)(2,1)S(1)} %collective-permute-done.3), channel_id=1, source_target_pairs={{0,28},{4,0},{8,4},{12,8},{16,12},{20,16},{24,20},{28,24},{1,29},{... | collective-permute-start | bytes 589832 | tf_op jit(solution)/shard_map/ppermute | solution.py:20
  26.2 5.8 %collective-permute-start.6 = (bf16[3,2,8,2048]{3,2,0,1:T(8,128)(2,1)S(1)}, bf16[3,2,8,2048]{3,2,0,1:T(8,128)(2,1)S(1)}, u32[]{:S(2)}, u32[]{:S(2)}) collective-permute-start(bf16[3,2,8,2048]{3,2,0,1:T(8,128)(2,1)S(1)} %collective-permute-done.4), channel_id=1, source_target_pairs={{0,4},{4,8},{8,12},{12,16},{16,20},{20,24},{24,28},{28,0},{1,5},{5... | collective-permute-start | bytes 589832 | tf_op jit(solution)/shard_map/ppermute | solution.py:20
  32.0 6.9 %collective-permute-start.7 = (bf16[3,2,8,2048]{3,2,0,1:T(8,128)(2,1)S(1)}, bf16[3,2,8,2048]{3,2,0,1:T(8,128)(2,1)S(1)}, u32[]{:S(2)}, u32[]{:S(2)}) collective-permute-start(bf16[3,2,8,2048]{3,2,0,1:T(8,128)(2,1)S(1)} %collective-permute-done.6), channel_id=1, source_target_pairs={{0,4},{4,8},{8,12},{12,16},{16,20},{20,24},{24,28},{28,0},{1,5},{5... | collective-permute-start | bytes 589832 | tf_op jit(solution)/shard_map/ppermute | solution.py:20
  39.0 9.8 %collective-permute-start.8 = (bf16[3,128,2048]{2,1,0:T(8,128)(2,1)S(1)}, bf16[3,128,2048]{2,1,0:T(8,128)(2,1)S(1)}, u32[]{:S(2)}, u32[]{:S(2)}) collective-permute-start(bf16[3,128,2048]{2,1,0:T(8,128)(2,1)S(1)} %bitcast.103), channel_id=1, source_target_pairs={{0,1},{1,0},{2,3},{3,2},{4,5},{5,4},{6,7},{7,6},{8,9},{9,8},{10,11... | collective-permute-start | bytes 4718600 | tf_op jit(solution)/shard_map/ppermute | solution.py:25
  52.1 16.7 %all-to-all-start = ((bf16[4,208,512]{2,1,0:T(8,128)(2,1)}), bf16[4,208,512]{2,1,0:T(8,128)(2,1)}, u32[]{:S(2)}, u32[]{:S(2)}) async-start(bf16[4,208,512]{2,1,0:T(8,128)(2,1)} %copy-done.5), calls=%async_computation | async-start | bytes 1703936 | tf_op jit(solution)/shard_map/all_to_all | solution.py:317
  70.5 5.0 %collective-permute-start.9 = (bf16[3,64,512]{2,1,0:T(8,128)(2,1)S(1)}, bf16[3,64,512]{2,1,0:T(8,128)(2,1)}, u32[]{:S(2)}, u32[]{:S(2)}) collective-permute-start(bf16[3,64,512]{2,1,0:T(8,128)(2,1)S(1)} %get-tuple-element.16.own), channel_id=1, source_target_pairs={{0,96},{32,0},{64,32},{96,64},{1,97},{33,1},{65,33},{97,65},{2,98}... | collective-permute-start | bytes 589832 | tf_op jit(solution)/shard_map/ppermute | solution.py:20
  71.4 6.2 %collective-permute-start.10 = (bf16[3,64,512]{2,1,0:T(8,128)(2,1)S(1)}, bf16[3,64,512]{2,1,0:T(8,128)(2,1)}, u32[]{:S(2)}, u32[]{:S(2)}) collective-permute-start(bf16[3,64,512]{2,1,0:T(8,128)(2,1)S(1)} %get-tuple-element.16.own), channel_id=1, source_target_pairs={{0,64},{32,96},{64,0},{96,32},{1,65},{33,97},{65,1},{97,33},{2,66}... | collective-permute-start | bytes 589832 | tf_op jit(solution)/shard_map/ppermute | solution.py:20
  72.7 10.5 %collective-permute-start.11 = (bf16[3,64,512]{2,1,0:T(8,128)(2,1)S(1)}, bf16[3,64,512]{2,1,0:T(8,128)(2,1)}, u32[]{:S(2)}, u32[]{:S(2)}) collective-permute-start(bf16[3,64,512]{2,1,0:T(8,128)(2,1)S(1)} %get-tuple-element.16.own), channel_id=1, source_target_pairs={{0,32},{32,64},{64,96},{96,0},{1,33},{33,65},{65,97},{97,1},{2,34}... | collective-permute-start | bytes 589832 | tf_op jit(solution)/shard_map/ppermute | solution.py:20
  92.5 3.6 %collective-permute-start.12 = (bf16[8,2,2,128,128]{4,3,2,1,0:T(8,128)(2,1)S(1)}, bf16[8,2,2,128,128]{4,3,2,1,0:T(8,128)(2,1)S(1)}, u32[]{:S(2)}, u32[]{:S(2)}) collective-permute-start(bf16[8,2,2,128,128]{4,3,2,1,0:T(8,128)(2,1)S(1)} %get-tuple-element.19), channel_id=1, source_target_pairs={{0,1},{1,0},{2,3},{3,2},{4,5},{5,4},{6,7},{7,6},{8,9},{9,8},{10,11... | collective-permute-start | bytes 3145736 | tf_op jit(solution)/shard_map/ppermute | solution.py:25
  96.5 19.9 %collective-permute-start.13 = (bf16[8,2,128,128]{3,2,1,0:T(8,128)(2,1)S(1)}, bf16[8,2,128,128]{3,2,1,0:T(8,128)(2,1)S(1)}, u32[]{:S(2)}, u32[]{:S(2)}) collective-permute-start(bf16[8,2,128,128]{3,2,1,0:T(8,128)(2,1)S(1)} %fusion.10), channel_id=1, source_target_pairs={{0,2},{2,0},{1,3},{3,1},{4,6},{6,4},{5,7},{7,5},{8,10},{10,8},{9,1... | collective-permute-start | bytes 1572872 | tf_op jit(solution)/shard_map/ppermute | solution.py:25
  99.3 2.9 %collective-permute-start.14 = (f32[2,2304]{1,0:T(2,128)S(1)}, f32[2,2304]{1,0:T(2,128)S(1)}, u32[]{:S(2)}, u32[]{:S(2)}) collective-permute-start(f32[2,2304]{1,0:T(2,128)S(1)} %constant_dynamic-update-slice_fusion), channel_id=1, source_target_pairs={{0,4},{4,0},{8,12},{12,8},{16,20},{20,16},{24,28},{28,24},{1,5},{5... | collective-permute-start | bytes 55304 | tf_op jit(solution)/shard_map/ppermute | solution.py:25
  100.1 21.1 %copy-start.17 = (bf16[128,2048]{1,0:T(8,128)(2,1)S(1)}, bf16[128,2048]{1,0:T(8,128)(2,1)}, u32[]{:S(2)}) copy-start(bf16[128,2048]{1,0:T(8,128)(2,1)} %get-tuple-element.37) | copy-start | bytes 1572868
  102.2 3.9 %collective-permute-start.15 = (f32[2,2304]{1,0:T(2,128)S(1)}, f32[2,2304]{1,0:T(2,128)S(1)}, u32[]{:S(2)}, u32[]{:S(2)}) collective-permute-start(f32[2,2304]{1,0:T(2,128)S(1)} %add.174), channel_id=1, source_target_pairs={{0,8},{4,12},{8,0},{12,4},{16,24},{20,28},{24,16},{28,20},{1,9},{5... | collective-permute-start | bytes 55304 | tf_op jit(solution)/shard_map/ppermute | solution.py:25
  106.1 6.6 %collective-permute-start.16 = (f32[2,2304]{1,0:T(2,128)S(1)}, f32[2,2304]{1,0:T(2,128)S(1)}, u32[]{:S(2)}, u32[]{:S(2)}) collective-permute-start(f32[2,2304]{1,0:T(2,128)S(1)} %add.175), channel_id=1, source_target_pairs={{0,16},{4,20},{8,24},{12,28},{16,0},{20,4},{24,8},{28,12},{1,17},{... | collective-permute-start | bytes 55304 | tf_op jit(solution)/shard_map/ppermute | solution.py:25
  112.8 8.1 %collective-permute-start.17 = (f32[2,2176]{1,0:T(2,128)S(1)}, f32[2,2176]{1,0:T(2,128)S(1)}, u32[]{:S(2)}, u32[]{:S(2)}) collective-permute-start(f32[2,2176]{1,0:T(2,128)S(1)} %slice.122), channel_id=1, source_target_pairs={{0,1},{1,0},{2,3},{3,2},{4,5},{5,4},{6,7},{7,6},{8,9},{9,8},{10,11... | collective-permute-start | bytes 52232 | tf_op jit(solution)/shard_map/ppermute | solution.py:25
  117.3 21.5 %all-to-all-start.1 = ((bf16[8,2,128,128]{3,2,1,0:T(8,128)(2,1)}), bf16[8,2,128,128]{3,2,1,0:T(8,128)(2,1)S(1)}, u32[]{:S(2)}, u32[]{:S(2)}) async-start(bf16[8,2,128,128]{3,2,1,0:T(8,128)(2,1)} %fusion.5), calls=%async_computation.1 | async-start | bytes 1048576 | tf_op jit(solution)/shard_map/all_to_all | solution.py:330
  120.9 4.2 %collective-permute-start.18 = (f32[2,2176]{1,0:T(2,128)S(1)}, f32[2,2176]{1,0:T(2,128)S(1)}, u32[]{:S(2)}, u32[]{:S(2)}) collective-permute-start(f32[2,2176]{1,0:T(2,128)S(1)} %maximum_add_fusion), channel_id=1, source_target_pairs={{0,2},{2,0},{1,3},{3,1},{4,6},{6,4},{5,7},{7,5},{8,10},{10,8},{9,1... | collective-permute-start | bytes 52232 | tf_op jit(solution)/shard_map/ppermute | solution.py:25
  125.1 4.3 %collective-permute-start.21 = (f32[2,128]{1,0:T(2,128)S(1)}, f32[2,128]{1,0:T(2,128)S(1)}, u32[]{:S(2)}, u32[]{:S(2)}) collective-permute-start(f32[2,128]{1,0:T(2,128)S(1)} %slice.123), channel_id=1, source_target_pairs={{0,96},{32,0},{64,32},{96,64},{1,97},{33,1},{65,33},{97,65},{2,98}... | collective-permute-start | bytes 3080 | tf_op jit(solution)/shard_map/ppermute | solution.py:20
  125.4 4.2 %collective-permute-start.20 = (f32[2,128]{1,0:T(2,128)S(1)}, f32[2,128]{1,0:T(2,128)S(1)}, u32[]{:S(2)}, u32[]{:S(2)}) collective-permute-start(f32[2,128]{1,0:T(2,128)S(1)} %slice.123), channel_id=1, source_target_pairs={{0,64},{32,96},{64,0},{96,32},{1,65},{33,97},{65,1},{97,33},{2,66}... | collective-permute-start | bytes 3080 | tf_op jit(solution)/shard_map/ppermute | solution.py:20
  126.8 3.9 %collective-permute-start.19 = (f32[2,128]{1,0:T(2,128)S(1)}, f32[2,128]{1,0:T(2,128)S(1)}, u32[]{:S(2)}, u32[]{:S(2)}) collective-permute-start(f32[2,128]{1,0:T(2,128)S(1)} %slice.123), channel_id=1, source_target_pairs={{0,32},{32,64},{64,96},{96,0},{1,33},{33,65},{65,97},{97,1},{2,34}... | collective-permute-start | bytes 3080 | tf_op jit(solution)/shard_map/ppermute | solution.py:20
  139.9 4.5 %collective-permute-start.23 = (bf16[2,128,64]{2,1,0:T(8,128)(2,1)S(1)}, bf16[2,128,64]{2,1,0:T(8,128)(2,1)S(1)}, u32[]{:S(2)}, u32[]{:S(2)}) collective-permute-start(bf16[2,128,64]{2,1,0:T(8,128)(2,1)S(1)} %get-tuple-element.46), channel_id=1, source_target_pairs={{0,129},{1,128},{128,1},{129,0},{2,131},{3,130},{130,3},{131,2},{4... | collective-permute-start | bytes 98312 | tf_op jit(solution)/shard_map/ppermute | solution.py:290
  140.6 4.9 %collective-permute-start.22 = (bf16[2,128,64]{2,1,0:T(8,128)(2,1)S(1)}, bf16[2,128,64]{2,1,0:T(8,128)(2,1)S(1)}, u32[]{:S(2)}, u32[]{:S(2)}) collective-permute-start(bf16[2,128,64]{2,1,0:T(8,128)(2,1)S(1)} %get-tuple-element.45), channel_id=1, source_target_pairs={{0,128},{128,0},{1,129},{129,1},{2,130},{130,2},{3,131},{131,3},{4... | collective-permute-start | bytes 98312 | tf_op jit(solution)/shard_map/ppermute | solution.py:25
  (12 other events, 102.7 us)

commit v3 on v2

--- a/solution.py
+++ b/solution.py
@@ -74,6 +74,30 @@
     )(a, b, c)
 
 
+def fetched_kernel(far_up, far_down, near_up, near_down, arrived):
+    copies = [
+        pltpu.make_async_copy(far_up, near_up, arrived.at[0]),
+        pltpu.make_async_copy(far_down, near_down, arrived.at[1]),
+    ]
+    for copy in copies:
+        copy.start()
+    for copy in copies:
+        copy.wait()
+
+
+def fetched(w_up, w_down):
+    return pl.pallas_call(
+        fetched_kernel,
+        in_specs=[pl.BlockSpec(memory_space=pltpu.HBM)] * 2,
+        out_specs=[pl.BlockSpec(memory_space=pltpu.VMEM)] * 2,
+        out_shape=[jax.ShapeDtypeStruct(w.shape, w.dtype) for w in (w_up, w_down)],
+        scratch_shapes=[pltpu.SemaphoreType.DMA((2,))],
+        compiler_params=pltpu.CompilerParams(vmem_limit_bytes=8 * 2**20),
+        cost_estimate=pl.CostEstimate(flops=0, bytes_accessed=8 * 2**20, transcendentals=0),
+        name="fetched",
+    )(w_up, w_down)
+
+
 def in_thirds(value):
     high = value.astype(BF).astype(F32)
     rest = value - high
@@ -81,7 +105,10 @@
     return high, middle, rest - middle
 
 
-def entry_kernel(mine, other, gain, shift, w_up, w_down, sent, scaled, grads, rows, extra, turned):
+def entry_kernel(
+    at_dp, mine, other, gain, shift, w_up, w_down,
+    sent0, sent1, sent2, sent3, scaled, grads, rows, extra, turned, found,
+):
     width = mine.shape[2]
     extra[...] = jnp.zeros_like(extra)
     rows[...] = jnp.zeros_like(rows)
@@ -110,40 +137,43 @@
         for k, third in enumerate(in_thirds(vector)):
             extra[3 * j + k : 3 * j + k + 1, :] = third
     for i in range(2):
-        product = jnp.dot(scaled[i], w_up[...], preferred_element_type=F32).astype(BF)
-        for q in range(4):
-            sent[q, 64 * i : 64 * i + 64, :] = product[64 * q : 64 * q + 64]
-    back = lax.dot_general(
+        found[i] = jnp.dot(scaled[i], w_up[...], preferred_element_type=F32).astype(BF)
+    found[2] = lax.dot_general(
         grads[...], w_down[...], (((1,), (1,)), ((), ())), preferred_element_type=F32
     ).astype(BF)
-    for q in range(4):
-        sent[q, 128:192, :] = back[64 * q : 64 * q + 64]
-        sent[q, 192:208, :] = extra[...].astype(BF)
+    for k, sent in enumerate((sent0, sent1, sent2, sent3)):
+        row = pl.multiple_of(((at_dp[0] + k) % 4) * 64, 64)
+        for i in range(3):
+            sent[64 * i : 64 * i + 64, :] = found[i, pl.ds(row, 64), :]
+        sent[192:208, :] = extra[...].astype(BF)
 
 
 def entry(mine, other, gain, shift, w_up, w_down):
     return pl.pallas_call(
         entry_kernel,
-        in_specs=[pl.BlockSpec(memory_space=pltpu.VMEM)] * 6,
-        out_specs=pl.BlockSpec(memory_space=pltpu.VMEM),
-        out_shape=jax.ShapeDtypeStruct((4, 208, 512), BF),
+        in_specs=[pl.BlockSpec(memory_space=pltpu.SMEM)]
+        + [pl.BlockSpec(memory_space=pltpu.VMEM)] * 6,
+        out_specs=[pl.BlockSpec(memory_space=pltpu.VMEM)] * 4,
+        out_shape=[jax.ShapeDtypeStruct((208, 512), BF)] * 4,
         scratch_shapes=[
             pltpu.VMEM((2, 256, 2048), BF),
             pltpu.VMEM((256, 2048), BF),
             pltpu.VMEM((8, 2048), F32),
             pltpu.VMEM((16, 512), F32),
             pltpu.VMEM((128, 128), F32),
+            pltpu.VMEM((3, 256, 512), BF),
         ],
         compiler_params=pltpu.CompilerParams(vmem_limit_bytes=28 * 2**20),
         cost_estimate=pl.CostEstimate(
             flops=2**31, bytes_accessed=8 * 2**20, transcendentals=0
         ),
         name="entry",
-    )(mine, other, gain, shift, w_up, w_down)
-
-
-def middle_kernel(at_dp, parts, bias, quarter, stats, rows):
-    extra = parts[:, 192:208, :].astype(F32)
+    )(lax.axis_index("dp").reshape(1), mine, other, gain, shift, w_up, w_down)
+
+
+def middle_kernel(at_dp, part0, part1, part2, part3, bias, quarter, stats, rows):
+    parts = (part0, part1, part2, part3)
+    extra = jnp.stack([part[192:208, :].astype(F32) for part in parts])
     weights = [
         [extra[y, 3 * j : 3 * j + 1] + extra[y, 3 * j + 1 : 3 * j + 2] + extra[y, 3 * j + 2 : 3 * j + 3] for y in range(4)]
         for j in range(2)
@@ -168,13 +198,13 @@
         total = jnp.zeros((64, 512), F32)
         for y in range(4):
             at = 4 + 4 * i + y
-            total += parts[y, 64 * i : 64 * i + 64, :].astype(F32)
+            total += parts[y][64 * i : 64 * i + 64, :].astype(F32)
             total += own[:, at : at + 1] * weights[0][y]
         pre = own[:, 2 * i + 1 : 2 * i + 2] * total + offset
         quarter[i] = gelu_value(pre).astype(BF)
-    back = parts[0, 128:192, :].astype(F32)
+    back = parts[0][128:192, :].astype(F32)
     for y in range(1, 4):
-        back += parts[y, 128:192, :].astype(F32)
+        back += parts[y][128:192, :].astype(F32)
     quarter[2] = (back * gelu_slope(pre)).astype(BF)
 
 
@@ -182,7 +212,7 @@
     return pl.pallas_call(
         middle_kernel,
         in_specs=[pl.BlockSpec(memory_space=pltpu.SMEM)]
-        + [pl.BlockSpec(memory_space=pltpu.VMEM)] * 2,
+        + [pl.BlockSpec(memory_space=pltpu.VMEM)] * 5,
         out_specs=[pl.BlockSpec(memory_space=pltpu.VMEM)] * 2,
         out_shape=[
             jax.ShapeDtypeStruct((3, 64, 512), BF),
@@ -194,77 +224,69 @@
             flops=2**22, bytes_accessed=2**20, transcendentals=2**17
         ),
         name="middle",
-    )(lax.axis_index("dp").reshape(1), parts, bias)
+    )(lax.axis_index("dp").reshape(1), *parts, bias)
 
 
 def products_kernel(
-    at_dp, own, next1, next2, next3, w_up, w_down, mine, other, stats, gain,
-    kept, given, hidden, bias_grad, params, moments, plain, crossed,
+    at_dp, own, next1, next2, next3, far_up, far_down, mine, other, stats, gain,
+    kept, given, hidden, bias_grad, params, moments, w_up, w_down, arrived,
 ):
-    step = pl.program_id(0)
-
-    @pl.when(step == 0)
-    def _():
-        for k, quarter in enumerate((own, next1, next2, next3)):
-            row = pl.multiple_of(((at_dp[0] + k) % 4) * 64, 64)
-            for i in range(3):
-                hidden[i, pl.ds(row, 64), :] = quarter[i]
-        bias_grad[...] = jnp.sum(hidden[2].astype(F32), 0, keepdims=True)
-        plain[...] = jnp.zeros_like(plain)
-        crossed[...] = jnp.zeros_like(crossed)
-
-    branch = jnp.dot(hidden[0], w_down[...], preferred_element_type=F32)
-    back = lax.dot_general(
-        hidden[2], w_up[...], (((1,), (1,)), ((), ())), preferred_element_type=F32
-    )
-    for h in range(2):
-        lanes = slice(h * 128, h * 128 + 128)
-        for i, product in enumerate((branch, back)):
-            kept[0, h, i] = product[:128, lanes]
-            given[0, h, i] = product[128:, lanes].astype(BF)
-    saved = jnp.concatenate([mine[0], other[0]]).astype(F32)
-    centered = (saved - stats[:, 2:3]) * stats[:, 3:4]
-    crossing = back * centered
-    params[0:1, :] = jnp.sum(crossing, 0, keepdims=True)
-    params[1:2, :] = jnp.sum(back, 0, keepdims=True)
-    plain[...] += back * gain[...]
-    crossed[...] += crossing * gain[...]
-
-    @pl.when(step == 7)
-    def _():
-        ones = jnp.ones((8, 256), F32)
-        for i, total in enumerate((plain, crossed)):
-            row = lax.dot_general(
-                ones, total[...], (((1,), (1,)), ((), ())),
-                precision=lax.Precision.HIGHEST, preferred_element_type=F32,
-            )
-            moments[i : i + 1, :] = row[0:1]
+    copies = []
+    for part in range(4):
+        block = slice(part * 512, part * 512 + 512)
+        copies.append((
+            pltpu.make_async_copy(far_down.at[:, block], w_down.at[:, block], arrived.at[0, part]),
+            pltpu.make_async_copy(far_up.at[block], w_up.at[block], arrived.at[1, part]),
+        ))
+        for copy in copies[-1]:
+            copy.start()
+    for k, quarter in enumerate((own, next1, next2, next3)):
+        row = pl.multiple_of(((at_dp[0] + k) % 4) * 64, 64)
+        for i in range(3):
+            hidden[i, pl.ds(row, 64), :] = quarter[i]
+    bias_grad[...] = jnp.sum(hidden[2].astype(F32), 0, keepdims=True)
+    plain = jnp.zeros((256, 128), F32)
+    crossed = jnp.zeros((256, 128), F32)
+    for z in range(8):
+        columns = slice(z * 256, z * 256 + 256)
+        if z % 2 == 0:
+            for copy in copies[z // 2]:
+                copy.wait()
+        branch = jnp.dot(hidden[0], w_down[:, columns], preferred_element_type=F32)
+        back = lax.dot_general(
+            hidden[2], w_up[columns, :], (((1,), (1,)), ((), ())), preferred_element_type=F32
+        )
+        for h in range(2):
+            lanes = slice(h * 128, h * 128 + 128)
+            for i, product in enumerate((branch, back)):
+                kept[z, h, i] = product[:128, lanes]
+                given[z, h, i] = product[128:, lanes].astype(BF)
+        saved = jnp.concatenate([mine[1, :, columns], other[1, :, columns]]).astype(F32)
+        centered = (saved - stats[:, 2:3]) * stats[:, 3:4]
+        crossing = back * centered
+        params[0:1, columns] = jnp.sum(crossing, 0, keepdims=True)
+        params[1:2, columns] = jnp.sum(back, 0, keepdims=True)
+        weighed, crossing = back * gain[:, columns], crossing * gain[:, columns]
+        plain += weighed[:, :128] + weighed[:, 128:]
+        crossed += crossing[:, :128] + crossing[:, 128:]
+    ones = jnp.ones((8, 128), F32)
+    for i, total in enumerate((plain, crossed)):
+        row = lax.dot_general(
+            ones, total, (((1,), (1,)), ((), ())),
+            precision=lax.Precision.HIGHEST, preferred_element_type=F32,
+        )
+        moments[i : i + 1, :] = row[0:1]
 
 
 def products(quarters, w_up, w_down, mine, other, stats, gain):
-    whole = lambda *shape: pl.BlockSpec(shape, lambda i: (0,) * len(shape))
     out = lambda shape, kind: jax.ShapeDtypeStruct(shape, kind)
     return pl.pallas_call(
         products_kernel,
-        grid=(8,),
         in_specs=[pl.BlockSpec(memory_space=pltpu.SMEM)]
-        + [whole(3, 64, 512)] * 4
-        + [
-            pl.BlockSpec((256, 512), lambda i: (i, 0)),
-            pl.BlockSpec((512, 256), lambda i: (0, i)),
-            pl.BlockSpec((1, 128, 256), lambda i: (1, 0, i)),
-            pl.BlockSpec((1, 128, 256), lambda i: (1, 0, i)),
-            whole(256, 128),
-            pl.BlockSpec((1, 256), lambda i: (0, i)),
-        ],
-        out_specs=[
-            pl.BlockSpec((1, 2, 2, 128, 128), lambda i: (i, 0, 0, 0, 0)),
-            pl.BlockSpec((1, 2, 2, 128, 128), lambda i: (i, 0, 0, 0, 0)),
-            whole(3, 256, 512),
-            whole(1, 512),
-            pl.BlockSpec((2, 256), lambda i: (0, i)),
-            whole(2, 256),
-        ],
+        + [pl.BlockSpec(memory_space=pltpu.VMEM)] * 4
+        + [pl.BlockSpec(memory_space=pltpu.HBM)] * 2
+        + [pl.BlockSpec(memory_space=pltpu.VMEM)] * 4,
+        out_specs=[pl.BlockSpec(memory_space=pltpu.VMEM)] * 6,
         out_shape=[
             out((8, 2, 2, 128, 128), F32),
             out((8, 2, 2, 128, 128), BF),
@@ -273,8 +295,12 @@
             out((2, 2048), F32),
             out((2, 256), F32),
         ],
-        scratch_shapes=[pltpu.VMEM((256, 256), F32)] * 2,
-        compiler_params=pltpu.CompilerParams(vmem_limit_bytes=12 * 2**20),
+        scratch_shapes=[
+            pltpu.VMEM((2048, 512), BF),
+            pltpu.VMEM((512, 2048), BF),
+            pltpu.SemaphoreType.DMA((2, 4)),
+        ],
+        compiler_params=pltpu.CompilerParams(vmem_limit_bytes=46 * 2**20),
         cost_estimate=pl.CostEstimate(
             flops=2**31, bytes_accessed=10 * 2**20, transcendentals=0
         ),
@@ -313,8 +339,9 @@
     mine = gather_half(together(section_input, saved_input, cotangent))
     other = swapped(mine, "core", 1)
 
-    parts = entry(mine, other, gain[None], shift[None], w_up, w_down)
-    parts = lax.all_to_all(parts, "dp", 0, 0, tiled=False)
+    near_up, near_down = fetched(w_up, w_down)
+    parts = entry(mine, other, gain[None], shift[None], near_up, near_down)
+    parts = [parts[0]] + [shifted(parts[k], "dp", k) for k in (1, 2, 3)]
     quarter, stats = middle(parts, bias_up[None])
     quarters = [quarter] + [shifted(quarter, "dp", -k) for k in (1, 2, 3)]
 
@@ -327,30 +354,6 @@
     kept = take(summed, at_h, 1) + swapped(given, "xh", 1).astype(F32)
     for bit in (1, 2, 4):
         small = small + swapped(small, "z", bit)
-    tiles = jnp.sum(lax.all_to_all(kept.astype(BF), "z", 0, 0, tiled=False).astype(F32), 0)
-    small = jnp.concatenate([small[:, :128], small[:, 256:]], 1) + swapped(
-        small[:, 128:], "core", 1
-    )
-    small = small + swapped(small, "xh", 1)
-    small = jnp.concatenate([over_dp(small[:, :128]), small[:, 128:]], 1)
-    moments, params = small[:, :128], small[:, 128:]
-
-    def own_tile(value):
-        return lax.dynamic_slice_in_dim(value, first_column, 128, 1).astype(F32)
-
-    def own_columns(vector):
-        return lax.dynamic_slice_in_dim(vector, first_column, 128, 0)
-
-    out = (own_tile(mine[0]) + tiles[0] + own_columns(bias_down)).astype(BF)
-
-    rstd_rows = stats[:128, 3:4]
-    centered_tile = (own_tile(mine[1]) - stats[:128, 2:3]) * rstd_rows
-    first, second = moments[0][:, None] / D, moments[1][:, None] / D
-    grad_in = own_tile(mine[2]) + rstd_rows * (
-        tiles[1] * own_columns(gain) - first - centered_tile * second
-    )
-    arrived = relayed(jnp.stack([out, grad_in.astype(BF)]))
-
     grad_full = jnp.concatenate([mine[2], other[2]])
     saved = jnp.concatenate([mine[1], other[1]]).astype(F32)
     normed = ((saved - stats[:, 2:3]) * stats[:, 3:4] * gain + shift).astype(BF)
@@ -361,6 +364,33 @@
     up_weight_grad = lax.dot_general(
         normed, hidden[2], (((0,), (0,)), ((), ())), preferred_element_type=F32
     ).astype(BF)
+    kept, up_weight_grad, down_weight_grad = lax.optimization_barrier(
+        (kept.astype(BF), up_weight_grad, down_weight_grad)
+    )
+    tiles = jnp.sum(lax.all_to_all(kept, "z", 0, 0, tiled=False).astype(F32), 0)
+    small = jnp.concatenate([small[:, :128], small[:, 256:]], 1) + swapped(
+        small[:, 128:], "core", 1
+    )
+    small = small + swapped(small, "xh", 1)
+    small = jnp.concatenate([over_dp(small[:, :128]), small[:, 128:]], 1)
+    moments, params = small[:, :128], small[:, 128:]
+
+    def own_tile(value):
+        return lax.dynamic_slice_in_dim(value, first_column, 128, 1).astype(F32)
+
+    def own_columns(vector):
+        return lax.dynamic_slice_in_dim(vector, first_column, 128, 0)
+
+    out = (own_tile(mine[0]) + tiles[0] + own_columns(bias_down)).astype(BF)
+
+    rstd_rows = stats[:128, 3:4]
+    centered_tile = (own_tile(mine[1]) - stats[:128, 2:3]) * rstd_rows
+    first, second = moments[0][:, None] / D, moments[1][:, None] / D
+    grad_in = own_tile(mine[2]) + rstd_rows * (
+        tiles[1] * own_columns(gain) - first - centered_tile * second
+    )
+    arrived = relayed(jnp.stack([out, grad_in.astype(BF)]))
+
     return (
         arrived[0][None],
         arrived[1][None],

time: 148 us -> 137 us (0.926)
  waiting for transfers between devices: 71.2 us -> 60.3 us
  starting transfers between devices: 45.6 us -> 48.8 us
  Pallas kernels: 11.6 us -> 9.87 us
  local copies, waits for them, and re-layouts: 9.12 us -> 7.44 us
    all_to_all x2 -> x1, waiting for transfers between devices: 20.5 us -> 6.32 us  [local(): tiles = jnp.sum(lax.all_to_all(kept, 'z', 0, 0, tiled=False).astype(F32), 0)]
    ppermute x13 -> x16, waiting for transfers between devices: 29.4 us -> 41.7 us  [shifted(): lax.ppermute(value, axis, [(i, (i + steps) % count) for i in range(count)])]
    ppermute x10, waiting for transfers between devices: 19.3 us -> 12.1 us  [swapped(): return lax.ppermute(value, axis, [(i, i ^ bit) for i in range(count)])]
    ppermute x13 -> x16, starting transfers between devices: 16.6 us -> 21.8 us  [shifted(): lax.ppermute(value, axis, [(i, (i + steps) % count) for i in range(count)])]
    all_to_all x2 -> x1, starting transfers between devices: 7.69 us -> 3.9 us  [local(): tiles = jnp.sum(lax.all_to_all(kept, 'z', 0, 0, tiled=False).astype(F32), 0)]
    ppermute x1, waiting for transfers between devices: 1.98 us -> 0.19 us  [relayed(): lax.ppermute(jnp.where(even, high, low), ('section', 'core'), [(i, 3 - i)...]
    ppermute x1, starting transfers between devices: 0.75 us -> 2.33 us  [relayed(): lax.ppermute(jnp.where(even, high, low), ('section', 'core'), [(i, 3 - i)...]
    unnamed x39 -> x21, local copies, waits for them, and re-layouts: 5.57 us -> 5.02 us
  transfers between devices with their start and end apart: 26 -> 28, of which waited for: 20 -> 19; matrix products, arithmetic and copies ran while one was open for 7% -> 7% of each run, Pallas kernels for 0% -> 0%
where the time goes in v3:
time: 137 us
  waiting for transfers between devices  60.3 us (44%)
  starting transfers between devices  48.8 us (36%)
  Pallas kernels  9.87 us (7%)
  local copies, waits for them, and re-layouts  7.44 us (5%)
  other arithmetic  4.96 us (4%)
  matrix products  4.3 us (3%)
    ppermute x16, waiting for transfers between devices, shifted(): lax.ppermute(value, axis, [(i, (i + steps) % count) for i in range(count)])  41.7 us
    ppermute x16, starting transfers between devices, shifted(): lax.ppermute(value, axis, [(i, (i + steps) % count) for i in range(count)])  21.8 us
    ppermute x10, starting transfers between devices, swapped(): return lax.ppermute(value, axis, [(i, i ^ bit) for i in range(count)])  20.8 us
    ppermute x10, waiting for transfers between devices, swapped(): return lax.ppermute(value, axis, [(i, i ^ bit) for i in range(count)])  12.1 us
    all_to_all x1, waiting for transfers between devices, local(): tiles = jnp.sum(lax.all_to_all(kept, 'z', 0, 0, tiled=False).astype(F32), 0)  6.32 us
    unnamed x21, local copies, waits for them, and re-layouts  5.02 us
    pallas_call x1, Pallas kernels, products(): pl.pallas_call(products_kernel, in_specs=[pl.BlockSpec(memory_space=pltpu...  4.97 us
    all_to_all x1, starting transfers between devices, local(): tiles = jnp.sum(lax.all_to_all(kept, 'z', 0, 0, tiled=False).astype(F32), 0)  3.9 us
  transfers between devices with their start and end apart: 28, of which 19 were waited for; matrix products, arithmetic and copies ran while one was open for 7% of the time, Pallas kernels for 0%

profile of v3, /device:TPU:1, one launch (start us, length us, event | category | flops | bytes accessed | tf_op | source)
XLA Modules:
  0.0 136.6 jit_solution(17542555634556054794)
XLA Ops:
  2.1 3.6 %collective-permute-start = (bf16[3,8,2048]{2,1,0:T(8,128)(2,1)}, bf16[3,8,2048]{2,1,0:T(8,128)(2,1)S(1)}, u32[]{:S(2)}, u32[]{:S(2)}) collective-permute-start(bf16[3,8,2048]{2,1,0:T(8,128)(2,1)} %together.1), channel_id=1, source_target_pairs={{0,2},{2,0},{1,3},{3,1},{4,6},{6,4},{5,7},{7,5},{8,10},{10,8},{9,1... | collective-permute-start | bytes 294920 | tf_op jit(solution)/shard_map/ppermute | solution.py:25
  5.6 2.3 %collective-permute-done = bf16[3,8,2048]{2,1,0:T(8,128)(2,1)S(1)} collective-permute-done((bf16[3,8,2048]{2,1,0:T(8,128)(2,1)}, bf16[3,8,2048]{2,1,0:T(8,128)(2,1)S(1)}, u32[]{:S(2)}, u32[]{:S(2)}) %collective-permute-start) | collective-permute-done | bytes 98336 | tf_op jit(solution)/shard_map/ppermute | solution.py:25
  8.9 5.8 %collective-permute-start.1 = (bf16[3,2,8,2048]{3,2,0,1:T(8,128)(2,1)S(1)}, bf16[3,2,8,2048]{3,2,0,1:T(8,128)(2,1)S(1)}, u32[]{:S(2)}, u32[]{:S(2)}) collective-permute-start(bf16[3,2,8,2048]{3,2,0,1:T(8,128)(2,1)S(1)} %maximum_select_fusion.1), channel_id=1, source_target_pairs={{0,28},{4,0},{8,4},{12,8},{16,12},{20,16},{24,20},{28,24},{1,29},{... | collective-permute-start | bytes 589832 | tf_op jit(solution)/shard_map/ppermute | solution.py:20
  15.0 2.4 %collective-permute-done.1 = bf16[3,2,8,2048]{3,2,0,1:T(8,128)(2,1)S(1)} collective-permute-done((bf16[3,2,8,2048]{3,2,0,1:T(8,128)(2,1)S(1)}, bf16[3,2,8,2048]{3,2,0,1:T(8,128)(2,1)S(1)}, u32[]{:S(2)}, u32[]{:S(2)}) %collective-permute-start.1) | collective-permute-done | bytes 196640 | tf_op jit(solution)/shard_map/ppermute | solution.py:20
  17.4 3.1 %collective-permute-start.3 = (bf16[3,2,8,2048]{3,2,0,1:T(8,128)(2,1)S(1)}, bf16[3,2,8,2048]{3,2,0,1:T(8,128)(2,1)S(1)}, u32[]{:S(2)}, u32[]{:S(2)}) collective-permute-start(bf16[3,2,8,2048]{3,2,0,1:T(8,128)(2,1)S(1)} %collective-permute-done.1), channel_id=1, source_target_pairs={{0,28},{4,0},{8,4},{12,8},{16,12},{20,16},{24,20},{28,24},{1,29},{... | collective-permute-start | bytes 589832 | tf_op jit(solution)/shard_map/ppermute | solution.py:20
  20.5 2.6 %collective-permute-done.3 = bf16[3,2,8,2048]{3,2,0,1:T(8,128)(2,1)S(1)} collective-permute-done((bf16[3,2,8,2048]{3,2,0,1:T(8,128)(2,1)S(1)}, bf16[3,2,8,2048]{3,2,0,1:T(8,128)(2,1)S(1)}, u32[]{:S(2)}, u32[]{:S(2)}) %collective-permute-start.3) | collective-permute-done | bytes 196640 | tf_op jit(solution)/shard_map/ppermute | solution.py:20
  23.1 3.1 %collective-permute-start.5 = (bf16[3,2,8,2048]{3,2,0,1:T(8,128)(2,1)S(1)}, bf16[3,2,8,2048]{3,2,0,1:T(8,128)(2,1)S(1)}, u32[]{:S(2)}, u32[]{:S(2)}) collective-permute-start(bf16[3,2,8,2048]{3,2,0,1:T(8,128)(2,1)S(1)} %collective-permute-done.3), channel_id=1, source_target_pairs={{0,28},{4,0},{8,4},{12,8},{16,12},{20,16},{24,20},{28,24},{1,29},{... | collective-permute-start | bytes 589832 | tf_op jit(solution)/shard_map/ppermute | solution.py:20
  26.3 5.8 %collective-permute-done.6 = bf16[3,2,8,2048]{3,2,0,1:T(8,128)(2,1)S(1)} collective-permute-done((bf16[3,2,8,2048]{3,2,0,1:T(8,128)(2,1)S(1)}, bf16[3,2,8,2048]{3,2,0,1:T(8,128)(2,1)S(1)}, u32[]{:S(2)}, u32[]{:S(2)}) %collective-permute-start.6) | collective-permute-done | bytes 196640 | tf_op jit(solution)/shard_map/ppermute | solution.py:20
  32.1 6.8 %collective-permute-done.7 = bf16[3,2,8,2048]{3,2,0,1:T(8,128)(2,1)S(1)} collective-permute-done((bf16[3,2,8,2048]{3,2,0,1:T(8,128)(2,1)S(1)}, bf16[3,2,8,2048]{3,2,0,1:T(8,128)(2,1)S(1)}, u32[]{:S(2)}, u32[]{:S(2)}) %collective-permute-start.7) | collective-permute-done | bytes 196640 | tf_op jit(solution)/shard_map/ppermute | solution.py:20
  38.9 6.7 %collective-permute-start.8 = (bf16[3,128,2048]{2,1,0:T(8,128)(2,1)S(1)}, bf16[3,128,2048]{2,1,0:T(8,128)(2,1)S(1)}, u32[]{:S(2)}, u32[]{:S(2)}) collective-permute-start(bf16[3,128,2048]{2,1,0:T(8,128)(2,1)S(1)} %bitcast.101), channel_id=1, source_target_pairs={{0,1},{1,0},{2,3},{3,2},{4,5},{5,4},{6,7},{7,6},{8,9},{9,8},{10,11... | collective-permute-start | bytes 4718600 | tf_op jit(solution)/shard_map/ppermute | solution.py:25
  45.7 1.6 %copy-done = bf16[1,2048,512]{2,1,0:T(8,128)(2,1)S(1)} copy-done((bf16[1,2048,512]{2,1,0:T(8,128)(2,1)S(1)}, bf16[1,2048,512]{2,1,0:T(8,128)(2,1)}, u32[]{:S(2)}) %copy-start) | copy-done | bytes 2097176
  49.6 2.6 %entry.1 = (bf16[208,512]{1,0:T(8,128)(2,1)S(1)}, bf16[208,512]{1,0:T(8,128)(2,1)S(1)}, bf16[208,512]{1,0:T(8,128)(2,1)S(1)}, bf16[208,512]{1,0:T(8,128)(2,1)S(1)}) custom-call(s32[1]{0:T(128)} %bitcast.12.at_dp, bf16[3,128,2048]{2,1,0:T(8,128)(2,1)S(1)} %bitcast.102, bf16[3,128,2048]{2,1,0:T(8,128)(2,1)S(1)} %collective-permute-done.8.other, ...), custom_call_target="tpu_custom_call" | custom-call | flops 2147483648 | bytes 8388608 | tf_op jit(solution)/shard_map/entry/pallas_call | solution.py:152
  53.6 2.6 %collective-permute-start.10 = (bf16[208,512]{1,0:T(8,128)(2,1)S(1)}, bf16[208,512]{1,0:T(8,128)(2,1)S(1)}, u32[]{:S(2)}, u32[]{:S(2)}) collective-permute-start(bf16[208,512]{1,0:T(8,128)(2,1)S(1)} %get-tuple-element.29), channel_id=1, source_target_pairs={{0,64},{32,96},{64,0},{96,32},{1,65},{33,97},{65,1},{97,33},{2,66}... | collective-permute-start | bytes 638984 | tf_op jit(solution)/shard_map/ppermute | solution.py:20
  57.3 3.2 %collective-permute-done.9.part1 = bf16[208,512]{1,0:T(8,128)(2,1)S(1)} collective-permute-done((bf16[208,512]{1,0:T(8,128)(2,1)S(1)}, bf16[208,512]{1,0:T(8,128)(2,1)S(1)}, u32[]{:S(2)}, u32[]{:S(2)}) %collective-permute-start.9) | collective-permute-done | bytes 213024 | tf_op jit(solution)/shard_map/ppermute | solution.py:20
  60.5 5.7 %collective-permute-done.10.part2 = bf16[208,512]{1,0:T(8,128)(2,1)S(1)} collective-permute-done((bf16[208,512]{1,0:T(8,128)(2,1)S(1)}, bf16[208,512]{1,0:T(8,128)(2,1)S(1)}, u32[]{:S(2)}, u32[]{:S(2)}) %collective-permute-start.10) | collective-permute-done | bytes 213024 | tf_op jit(solution)/shard_map/ppermute | solution.py:20
  66.7 2.4 %collective-permute-start.12 = (bf16[3,64,512]{2,1,0:T(8,128)(2,1)S(1)}, bf16[3,64,512]{2,1,0:T(8,128)(2,1)}, u32[]{:S(2)}, u32[]{:S(2)}) collective-permute-start(bf16[3,64,512]{2,1,0:T(8,128)(2,1)S(1)} %get-tuple-element.31.own), channel_id=1, source_target_pairs={{0,96},{32,0},{64,32},{96,64},{1,97},{33,1},{65,33},{97,65},{2,98}... | collective-permute-start | bytes 589832 | tf_op jit(solution)/shard_map/ppermute | solution.py:20
  69.8 3.9 %collective-permute-done.12.next1 = bf16[3,64,512]{2,1,0:T(8,128)(2,1)} collective-permute-done((bf16[3,64,512]{2,1,0:T(8,128)(2,1)S(1)}, bf16[3,64,512]{2,1,0:T(8,128)(2,1)}, u32[]{:S(2)}, u32[]{:S(2)}) %collective-permute-start.12) | collective-permute-done | bytes 196640 | tf_op jit(solution)/shard_map/ppermute | solution.py:20
  73.8 2.7 %collective-permute-done.13.next2 = bf16[3,64,512]{2,1,0:T(8,128)(2,1)} collective-permute-done((bf16[3,64,512]{2,1,0:T(8,128)(2,1)S(1)}, bf16[3,64,512]{2,1,0:T(8,128)(2,1)}, u32[]{:S(2)}, u32[]{:S(2)}) %collective-permute-start.13) | collective-permute-done | bytes 196640 | tf_op jit(solution)/shard_map/ppermute | solution.py:20
  76.5 5.1 %collective-permute-done.14.next3 = bf16[3,64,512]{2,1,0:T(8,128)(2,1)} collective-permute-done((bf16[3,64,512]{2,1,0:T(8,128)(2,1)S(1)}, bf16[3,64,512]{2,1,0:T(8,128)(2,1)}, u32[]{:S(2)}, u32[]{:S(2)}) %collective-permute-start.14) | collective-permute-done | bytes 196640 | tf_op jit(solution)/shard_map/ppermute | solution.py:20
  81.6 5.0 %products.1 = (f32[8,2,2,128,128]{4,3,2,1,0:T(8,128)S(1)}, bf16[8,2,2,128,128]{4,3,2,1,0:T(8,128)(2,1)S(1)}, bf16[3,256,512]{2,1,0:T(8,128)(2,1)S(1)}, f32[1,512...) custom-call(s32[1]{0:T(128)} %bitcast.12.at_dp, bf16[3,64,512]{2,1,0:T(8,128)(2,1)S(1)} %get-tuple-element.31.own, ...), custom_call_target="tpu_custom_call" | custom-call | flops 2147483648 | bytes 10485760 | tf_op jit(solution)/shard_map/products/pallas_call | solution.py:283
  88.6 2.3 %collective-permute-done.17 = f32[2,2304]{1,0:T(2,128)S(1)} collective-permute-done((f32[2,2304]{1,0:T(2,128)S(1)}, f32[2,2304]{1,0:T(2,128)S(1)}, u32[]{:S(2)}, u32[]{:S(2)}) %collective-permute-start.17) | collective-permute-done | bytes 18464 | tf_op jit(solution)/shard_map/ppermute | solution.py:25
  91.6 2.8 %collective-permute-start.16 = (bf16[8,2,128,128]{3,2,1,0:T(8,128)(2,1)S(1)}, bf16[8,2,128,128]{3,2,1,0:T(8,128)(2,1)S(1)}, u32[]{:S(2)}, u32[]{:S(2)}) collective-permute-start(bf16[8,2,128,128]{3,2,1,0:T(8,128)(2,1)S(1)} %fusion.8), channel_id=1, source_target_pairs={{0,2},{2,0},{1,3},{3,1},{4,6},{6,4},{5,7},{7,5},{8,10},{10,8},{9,1... | collective-permute-start | bytes 1572872 | tf_op jit(solution)/shard_map/ppermute | solution.py:25
  94.4 2.2 %convolution_convert_fusion.1 = bf16[2048,512]{1,0:T(8,128)(2,1)} fusion(bf16[128,2048]{1,0:T(8,128)(2,1)S(1)} %get-tuple-element.58, bf16[128,2048]{1,0:T(8,128)(2,1)S(1)} %bitcast.117, f32[2048]{0:T(1024)S(1)} %bitcast.109, f32[2048]{0:T(1024)S(1)} %bitcast.108, f32[256]{0:T(256)S(1)} %get-tuple-element.53, f32[256]{0:T(256)S(1)} %get-tuple-element.52, ...), kind=kOutput, calls=%fused_computation.1 | convolution fusion | flops 542638080 | bytes 3426304 | tf_op jit(solution)/shard_map/dot_general | solution.py:364
  97.8 2.1 %convolution_convert_fusion = bf16[512,2048]{1,0:T(8,128)(2,1)} fusion(bf16[128,2048]{1,0:T(8,128)(2,1)S(1)} %get-tuple-element.57, bf16[128,2048]{1,0:T(8,128)(2,1)S(1)} %bitcast.110, bf16[3,256,512]{2,1,0:T(8,128)(2,1)S(1)} %get-tuple-element.35), kind=kOutput, calls=%fused_computation | convolution fusion | flops 540016640 | bytes 3407872 | tf_op jit(solution)/shard_map/dot_general | solution.py:360
  99.8 3.4 %collective-permute-done.19 = f32[2,2304]{1,0:T(2,128)S(1)} collective-permute-done((f32[2,2304]{1,0:T(2,128)S(1)}, f32[2,2304]{1,0:T(2,128)S(1)}, u32[]{:S(2)}, u32[]{:S(2)}) %collective-permute-start.19) | collective-permute-done | bytes 18464 | tf_op jit(solution)/shard_map/ppermute | solution.py:25
  103.3 2.7 %collective-permute-start.20 = (f32[2,2176]{1,0:T(2,128)S(1)}, f32[2,2176]{1,0:T(2,128)S(1)}, u32[]{:S(2)}, u32[]{:S(2)}) collective-permute-start(f32[2,2176]{1,0:T(2,128)S(1)} %slice.125), channel_id=1, source_target_pairs={{0,1},{1,0},{2,3},{3,2},{4,5},{5,4},{6,7},{7,6},{8,9},{9,8},{10,11... | collective-permute-start | bytes 52232 | tf_op jit(solution)/shard_map/ppermute | solution.py:25
  106.9 3.9 %all-to-all-start = ((bf16[8,2,128,128]{3,2,1,0:T(8,128)(2,1)}), bf16[8,2,128,128]{3,2,1,0:T(8,128)(2,1)S(1)}, u32[]{:S(2)}, u32[]{:S(2)}) async-start(bf16[8,2,128,128]{3,2,1,0:T(8,128)(2,1)} %fusion.3), calls=%async_computation | async-start | bytes 1048576 | tf_op jit(solution)/shard_map/all_to_all | solution.py:370
  110.9 1.8 %collective-permute-start.21 = (f32[2,2176]{1,0:T(2,128)S(1)}, f32[2,2176]{1,0:T(2,128)S(1)}, u32[]{:S(2)}, u32[]{:S(2)}) collective-permute-start(f32[2,2176]{1,0:T(2,128)S(1)} %maximum_add_fusion), channel_id=1, source_target_pairs={{0,2},{2,0},{1,3},{3,1},{4,6},{6,4},{5,7},{7,5},{8,10},{10,8},{9,1... | collective-permute-start | bytes 52232 | tf_op jit(solution)/shard_map/ppermute | solution.py:25
  117.9 1.9 %collective-permute-done.23 = f32[2,128]{1,0:T(2,128)S(1)} collective-permute-done((f32[2,128]{1,0:T(2,128)S(1)}, f32[2,128]{1,0:T(2,128)S(1)}, u32[]{:S(2)}, u32[]{:S(2)}) %collective-permute-start.23) | collective-permute-done | bytes 1056 | tf_op jit(solution)/shard_map/ppermute | solution.py:20
  120.9 6.3 %all-to-all-done = bf16[8,2,128,128]{3,2,1,0:T(8,128)(2,1)S(1)} async-done(((bf16[8,2,128,128]{3,2,1,0:T(8,128)(2,1)}), bf16[8,2,128,128]{3,2,1,0:T(8,128)(2,1)S(1)}, u32[]{:S(2)}, u32[]{:S(2)}) %all-to-all-start) | async-done | bytes 524320 | tf_op jit(solution)/shard_map/all_to_all | solution.py:370
  128.3 2.3 %collective-permute-start.26 = (bf16[2,128,64]{2,1,0:T(8,128)(2,1)S(1)}, bf16[2,128,64]{2,1,0:T(8,128)(2,1)S(1)}, u32[]{:S(2)}, u32[]{:S(2)}) collective-permute-start(bf16[2,128,64]{2,1,0:T(8,128)(2,1)S(1)} %get-tuple-element.64), channel_id=1, source_target_pairs={{0,129},{1,128},{128,1},{129,0},{2,131},{3,130},{130,3},{131,2},{4... | collective-permute-start | bytes 98312 | tf_op jit(solution)/shard_map/ppermute | solution.py:316
  132.6 2.5 %collective-permute-done.25 = bf16[2,128,64]{2,1,0:T(8,128)(2,1)S(1)} collective-permute-done((bf16[2,128,64]{2,1,0:T(8,128)(2,1)S(1)}, bf16[2,128,64]{2,1,0:T(8,128)(2,1)S(1)}, u32[]{:S(2)}, u32[]{:S(2)}) %collective-permute-start.25) | collective-permute-done | bytes 32800 | tf_op jit(solution)/shard_map/ppermute | solution.py:25
  (89 shorter events, 24.2 us)
Async XLA Ops:
  2.1 12.9 %copy-start.7 = (bf16[3,8,2048]{2,1,0:T(8,128)(2,1)S(1)}, bf16[3,8,2048]{2,1,0:T(8,128)(2,1)}, u32[]{:S(2)}) copy-start(bf16[3,8,2048]{2,1,0:T(8,128)(2,1)} %together.1) | copy-start | bytes 294916
  2.1 5.9 %collective-permute-start = (bf16[3,8,2048]{2,1,0:T(8,128)(2,1)}, bf16[3,8,2048]{2,1,0:T(8,128)(2,1)S(1)}, u32[]{:S(2)}, u32[]{:S(2)}) collective-permute-start(bf16[3,8,2048]{2,1,0:T(8,128)(2,1)} %together.1), channel_id=1, source_target_pairs={{0,2},{2,0},{1,3},{3,1},{4,6},{6,4},{5,7},{7,5},{8,10},{10,8},{9,1... | collective-permute-start | bytes 294920 | tf_op jit(solution)/shard_map/ppermute | solution.py:25
  8.9 8.4 %collective-permute-start.1 = (bf16[3,2,8,2048]{3,2,0,1:T(8,128)(2,1)S(1)}, bf16[3,2,8,2048]{3,2,0,1:T(8,128)(2,1)S(1)}, u32[]{:S(2)}, u32[]{:S(2)}) collective-permute-start(bf16[3,2,8,2048]{3,2,0,1:T(8,128)(2,1)S(1)} %maximum_select_fusion.1), channel_id=1, source_target_pairs={{0,28},{4,0},{8,4},{12,8},{16,12},{20,16},{24,20},{28,24},{1,29},{... | collective-permute-start | bytes 589832 | tf_op jit(solution)/shard_map/ppermute | solution.py:20
  14.7 5.7 %collective-permute-start.2 = (bf16[3,2,8,2048]{3,2,0,1:T(8,128)(2,1)S(1)}, bf16[3,2,8,2048]{3,2,0,1:T(8,128)(2,1)S(1)}, u32[]{:S(2)}, u32[]{:S(2)}) collective-permute-start(bf16[3,2,8,2048]{3,2,0,1:T(8,128)(2,1)S(1)} %maximum_select_fusion.1), channel_id=1, source_target_pairs={{0,4},{4,8},{8,12},{12,16},{16,20},{20,24},{24,28},{28,0},{1,5},{5... | collective-permute-start | bytes 589832 | tf_op jit(solution)/shard_map/ppermute | solution.py:20
  17.4 5.7 %collective-permute-start.3 = (bf16[3,2,8,2048]{3,2,0,1:T(8,128)(2,1)S(1)}, bf16[3,2,8,2048]{3,2,0,1:T(8,128)(2,1)S(1)}, u32[]{:S(2)}, u32[]{:S(2)}) collective-permute-start(bf16[3,2,8,2048]{3,2,0,1:T(8,128)(2,1)S(1)} %collective-permute-done.1), channel_id=1, source_target_pairs={{0,28},{4,0},{8,4},{12,8},{16,12},{20,16},{24,20},{28,24},{1,29},{... | collective-permute-start | bytes 589832 | tf_op jit(solution)/shard_map/ppermute | solution.py:20
  20.5 5.7 %collective-permute-start.4 = (bf16[3,2,8,2048]{3,2,0,1:T(8,128)(2,1)S(1)}, bf16[3,2,8,2048]{3,2,0,1:T(8,128)(2,1)S(1)}, u32[]{:S(2)}, u32[]{:S(2)}) collective-permute-start(bf16[3,2,8,2048]{3,2,0,1:T(8,128)(2,1)S(1)} %collective-permute-done.2), channel_id=1, source_target_pairs={{0,4},{4,8},{8,12},{12,16},{16,20},{20,24},{24,28},{28,0},{1,5},{5... | collective-permute-start | bytes 589832 | tf_op jit(solution)/shard_map/ppermute | solution.py:20
  23.1 8.9 %collective-permute-start.5 = (bf16[3,2,8,2048]{3,2,0,1:T(8,128)(2,1)S(1)}, bf16[3,2,8,2048]{3,2,0,1:T(8,128)(2,1)S(1)}, u32[]{:S(2)}, u32[]{:S(2)}) collective-permute-start(bf16[3,2,8,2048]{3,2,0,1:T(8,128)(2,1)S(1)} %collective-permute-done.3), channel_id=1, source_target_pairs={{0,28},{4,0},{8,4},{12,8},{16,12},{20,16},{24,20},{28,24},{1,29},{... | collective-permute-start | bytes 589832 | tf_op jit(solution)/shard_map/ppermute | solution.py:20
  26.2 5.8 %collective-permute-start.6 = (bf16[3,2,8,2048]{3,2,0,1:T(8,128)(2,1)S(1)}, bf16[3,2,8,2048]{3,2,0,1:T(8,128)(2,1)S(1)}, u32[]{:S(2)}, u32[]{:S(2)}) collective-permute-start(bf16[3,2,8,2048]{3,2,0,1:T(8,128)(2,1)S(1)} %collective-permute-done.4), channel_id=1, source_target_pairs={{0,4},{4,8},{8,12},{12,16},{16,20},{20,24},{24,28},{28,0},{1,5},{5... | collective-permute-start | bytes 589832 | tf_op jit(solution)/shard_map/ppermute | solution.py:20
  32.0 6.9 %collective-permute-start.7 = (bf16[3,2,8,2048]{3,2,0,1:T(8,128)(2,1)S(1)}, bf16[3,2,8,2048]{3,2,0,1:T(8,128)(2,1)S(1)}, u32[]{:S(2)}, u32[]{:S(2)}) collective-permute-start(bf16[3,2,8,2048]{3,2,0,1:T(8,128)(2,1)S(1)} %collective-permute-done.6), channel_id=1, source_target_pairs={{0,4},{4,8},{8,12},{12,16},{16,20},{20,24},{24,28},{28,0},{1,5},{5... | collective-permute-start | bytes 589832 | tf_op jit(solution)/shard_map/ppermute | solution.py:20
  38.9 10.2 %collective-permute-start.8 = (bf16[3,128,2048]{2,1,0:T(8,128)(2,1)S(1)}, bf16[3,128,2048]{2,1,0:T(8,128)(2,1)S(1)}, u32[]{:S(2)}, u32[]{:S(2)}) collective-permute-start(bf16[3,128,2048]{2,1,0:T(8,128)(2,1)S(1)} %bitcast.101), channel_id=1, source_target_pairs={{0,1},{1,0},{2,3},{3,2},{4,5},{5,4},{6,7},{7,6},{8,9},{9,8},{10,11... | collective-permute-start | bytes 4718600 | tf_op jit(solution)/shard_map/ppermute | solution.py:25
  49.6 16.6 %copy-start.3 = (f32[1,512]{1,0:T(1,128)S(1)}, f32[1,512]{1,0:T(1,128)}, u32[]{:S(2)}) copy-start(f32[1,512]{1,0:T(1,128)} %bias.1) | copy-start | bytes 6148
  52.2 8.3 %collective-permute-start.9 = (bf16[208,512]{1,0:T(8,128)(2,1)S(1)}, bf16[208,512]{1,0:T(8,128)(2,1)S(1)}, u32[]{:S(2)}, u32[]{:S(2)}) collective-permute-start(bf16[208,512]{1,0:T(8,128)(2,1)S(1)} %get-tuple-element.28), channel_id=1, source_target_pairs={{0,32},{32,64},{64,96},{96,0},{1,33},{33,65},{65,97},{97,1},{2,34}... | collective-permute-start | bytes 638984 | tf_op jit(solution)/shard_map/ppermute | solution.py:20
  53.6 12.6 %collective-permute-start.10 = (bf16[208,512]{1,0:T(8,128)(2,1)S(1)}, bf16[208,512]{1,0:T(8,128)(2,1)S(1)}, u32[]{:S(2)}, u32[]{:S(2)}) collective-permute-start(bf16[208,512]{1,0:T(8,128)(2,1)S(1)} %get-tuple-element.29), channel_id=1, source_target_pairs={{0,64},{32,96},{64,0},{96,32},{1,65},{33,97},{65,1},{97,33},{2,66}... | collective-permute-start | bytes 638984 | tf_op jit(solution)/shard_map/ppermute | solution.py:20
  56.2 10.0 %collective-permute-start.11 = (bf16[208,512]{1,0:T(8,128)(2,1)S(1)}, bf16[208,512]{1,0:T(8,128)(2,1)S(1)}, u32[]{:S(2)}, u32[]{:S(2)}) collective-permute-start(bf16[208,512]{1,0:T(8,128)(2,1)S(1)} %get-tuple-element.30), channel_id=1, source_target_pairs={{0,96},{32,0},{64,32},{96,64},{1,97},{33,1},{65,33},{97,65},{2,98}... | collective-permute-start | bytes 638984 | tf_op jit(solution)/shard_map/ppermute | solution.py:20
  66.7 7.1 %collective-permute-start.12 = (bf16[3,64,512]{2,1,0:T(8,128)(2,1)S(1)}, bf16[3,64,512]{2,1,0:T(8,128)(2,1)}, u32[]{:S(2)}, u32[]{:S(2)}) collective-permute-start(bf16[3,64,512]{2,1,0:T(8,128)(2,1)S(1)} %get-tuple-element.31.own), channel_id=1, source_target_pairs={{0,96},{32,0},{64,32},{96,64},{1,97},{33,1},{65,33},{97,65},{2,98}... | collective-permute-start | bytes 589832 | tf_op jit(solution)/shard_map/ppermute | solution.py:20
  69.2 7.4 %collective-permute-start.13 = (bf16[3,64,512]{2,1,0:T(8,128)(2,1)S(1)}, bf16[3,64,512]{2,1,0:T(8,128)(2,1)}, u32[]{:S(2)}, u32[]{:S(2)}) collective-permute-start(bf16[3,64,512]{2,1,0:T(8,128)(2,1)S(1)} %get-tuple-element.31.own), channel_id=1, source_target_pairs={{0,64},{32,96},{64,0},{96,32},{1,65},{33,97},{65,1},{97,33},{2,66}... | collective-permute-start | bytes 589832 | tf_op jit(solution)/shard_map/ppermute | solution.py:20
  69.4 12.2 %collective-permute-start.14 = (bf16[3,64,512]{2,1,0:T(8,128)(2,1)S(1)}, bf16[3,64,512]{2,1,0:T(8,128)(2,1)}, u32[]{:S(2)}, u32[]{:S(2)}) collective-permute-start(bf16[3,64,512]{2,1,0:T(8,128)(2,1)S(1)} %get-tuple-element.31.own), channel_id=1, source_target_pairs={{0,32},{32,64},{64,96},{96,0},{1,33},{33,65},{65,97},{97,1},{2,34}... | collective-permute-start | bytes 589832 | tf_op jit(solution)/shard_map/ppermute | solution.py:20
  86.6 4.5 %collective-permute-start.15 = (bf16[8,2,2,128,128]{4,3,2,1,0:T(8,128)(2,1)S(1)}, bf16[8,2,2,128,128]{4,3,2,1,0:T(8,128)(2,1)S(1)}, u32[]{:S(2)}, u32[]{:S(2)}) collective-permute-start(bf16[8,2,2,128,128]{4,3,2,1,0:T(8,128)(2,1)S(1)} %get-tuple-element.34), channel_id=1, source_target_pairs={{0,1},{1,0},{2,3},{3,2},{4,5},{5,4},{6,7},{7,6},{8,9},{9,8},{10,11... | collective-permute-start | bytes 3145736 | tf_op jit(solution)/shard_map/ppermute | solution.py:25
  88.2 9.6 %copy-start.5 = (bf16[1,8,2,8,2048]{4,3,2,1,0:T(8,128)(2,1)}, bf16[1,8,2,8,2048]{4,3,2,1,0:T(8,128)(2,1)S(1)}, u32[]{:S(2)}) copy-start(bf16[1,8,2,8,2048]{4,3,2,1,0:T(8,128)(2,1)S(1)} %get-tuple-element.55) | copy-start | bytes 1572868
  88.3 2.7 %collective-permute-start.17 = (f32[2,2304]{1,0:T(2,128)S(1)}, f32[2,2304]{1,0:T(2,128)S(1)}, u32[]{:S(2)}, u32[]{:S(2)}) collective-permute-start(f32[2,2304]{1,0:T(2,128)S(1)} %constant_dynamic-update-slice_fusion), channel_id=1, source_target_pairs={{0,4},{4,0},{8,12},{12,8},{16,20},{20,16},{24,28},{28,24},{1,5},{5... | collective-permute-start | bytes 55304 | tf_op jit(solution)/shard_map/ppermute | solution.py:25
  91.0 5.7 %collective-permute-start.18 = (f32[2,2304]{1,0:T(2,128)S(1)}, f32[2,2304]{1,0:T(2,128)S(1)}, u32[]{:S(2)}, u32[]{:S(2)}) collective-permute-start(f32[2,2304]{1,0:T(2,128)S(1)} %add.177), channel_id=1, source_target_pairs={{0,8},{4,12},{8,0},{12,4},{16,24},{20,28},{24,16},{28,20},{1,9},{5... | collective-permute-start | bytes 55304 | tf_op jit(solution)/shard_map/ppermute | solution.py:25
  91.6 14.4 %collective-permute-start.16 = (bf16[8,2,128,128]{3,2,1,0:T(8,128)(2,1)S(1)}, bf16[8,2,128,128]{3,2,1,0:T(8,128)(2,1)S(1)}, u32[]{:S(2)}, u32[]{:S(2)}) collective-permute-start(bf16[8,2,128,128]{3,2,1,0:T(8,128)(2,1)S(1)} %fusion.8), channel_id=1, source_target_pairs={{0,2},{2,0},{1,3},{3,1},{4,6},{6,4},{5,7},{7,5},{8,10},{10,8},{9,1... | collective-permute-start | bytes 1572872 | tf_op jit(solution)/shard_map/ppermute | solution.py:25
  96.7 6.6 %collective-permute-start.19 = (f32[2,2304]{1,0:T(2,128)S(1)}, f32[2,2304]{1,0:T(2,128)S(1)}, u32[]{:S(2)}, u32[]{:S(2)}) collective-permute-start(f32[2,2304]{1,0:T(2,128)S(1)} %add.178), channel_id=1, source_target_pairs={{0,16},{4,20},{8,24},{12,28},{16,0},{20,4},{24,8},{28,12},{1,17},{... | collective-permute-start | bytes 55304 | tf_op jit(solution)/shard_map/ppermute | solution.py:25
  99.8 12.9 %copy-start.6 = (bf16[1,8,2,8,2048]{4,3,2,1,0:T(8,128)(2,1)S(1)}, bf16[1,8,2,8,2048]{4,3,2,1,0:T(8,128)(2,1)}, u32[]{:S(2)}) copy-start(bf16[1,8,2,8,2048]{4,3,2,1,0:T(8,128)(2,1)} %copy-done.5) | copy-start | bytes 1572868
  103.3 7.5 %collective-permute-start.20 = (f32[2,2176]{1,0:T(2,128)S(1)}, f32[2,2176]{1,0:T(2,128)S(1)}, u32[]{:S(2)}, u32[]{:S(2)}) collective-permute-start(f32[2,2176]{1,0:T(2,128)S(1)} %slice.125), channel_id=1, source_target_pairs={{0,1},{1,0},{2,3},{3,2},{4,5},{5,4},{6,7},{7,6},{8,9},{9,8},{10,11... | collective-permute-start | bytes 52232 | tf_op jit(solution)/shard_map/ppermute | solution.py:25
  106.9 20.3 %all-to-all-start = ((bf16[8,2,128,128]{3,2,1,0:T(8,128)(2,1)}), bf16[8,2,128,128]{3,2,1,0:T(8,128)(2,1)S(1)}, u32[]{:S(2)}, u32[]{:S(2)}) async-start(bf16[8,2,128,128]{3,2,1,0:T(8,128)(2,1)} %fusion.3), calls=%async_computation | async-start | bytes 1048576 | tf_op jit(solution)/shard_map/all_to_all | solution.py:370
  110.9 4.2 %collective-permute-start.21 = (f32[2,2176]{1,0:T(2,128)S(1)}, f32[2,2176]{1,0:T(2,128)S(1)}, u32[]{:S(2)}, u32[]{:S(2)}) collective-permute-start(f32[2,2176]{1,0:T(2,128)S(1)} %maximum_add_fusion), channel_id=1, source_target_pairs={{0,2},{2,0},{1,3},{3,1},{4,6},{6,4},{5,7},{7,5},{8,10},{10,8},{9,1... | collective-permute-start | bytes 52232 | tf_op jit(solution)/shard_map/ppermute | solution.py:25
  115.1 2.8 %collective-permute-start.24 = (f32[2,128]{1,0:T(2,128)S(1)}, f32[2,128]{1,0:T(2,128)S(1)}, u32[]{:S(2)}, u32[]{:S(2)}) collective-permute-start(f32[2,128]{1,0:T(2,128)S(1)} %slice.126), channel_id=1, source_target_pairs={{0,96},{32,0},{64,32},{96,64},{1,97},{33,1},{65,33},{97,65},{2,98}... | collective-permute-start | bytes 3080 | tf_op jit(solution)/shard_map/ppermute | solution.py:20
  115.6 4.2 %collective-permute-start.23 = (f32[2,128]{1,0:T(2,128)S(1)}, f32[2,128]{1,0:T(2,128)S(1)}, u32[]{:S(2)}, u32[]{:S(2)}) collective-permute-start(f32[2,128]{1,0:T(2,128)S(1)} %slice.126), channel_id=1, source_target_pairs={{0,64},{32,96},{64,0},{96,32},{1,65},{33,97},{65,1},{97,33},{2,66}... | collective-permute-start | bytes 3080 | tf_op jit(solution)/shard_map/ppermute | solution.py:20
  115.7 4.5 %collective-permute-start.22 = (f32[2,128]{1,0:T(2,128)S(1)}, f32[2,128]{1,0:T(2,128)S(1)}, u32[]{:S(2)}, u32[]{:S(2)}) collective-permute-start(f32[2,128]{1,0:T(2,128)S(1)} %slice.126), channel_id=1, source_target_pairs={{0,32},{32,64},{64,96},{96,0},{1,33},{33,65},{65,97},{97,1},{2,34}... | collective-permute-start | bytes 3080 | tf_op jit(solution)/shard_map/ppermute | solution.py:20
  128.3 4.3 %collective-permute-start.26 = (bf16[2,128,64]{2,1,0:T(8,128)(2,1)S(1)}, bf16[2,128,64]{2,1,0:T(8,128)(2,1)S(1)}, u32[]{:S(2)}, u32[]{:S(2)}) collective-permute-start(bf16[2,128,64]{2,1,0:T(8,128)(2,1)S(1)} %get-tuple-element.64), channel_id=1, source_target_pairs={{0,129},{1,128},{128,1},{129,0},{2,131},{3,130},{130,3},{131,2},{4... | collective-permute-start | bytes 98312 | tf_op jit(solution)/shard_map/ppermute | solution.py:316
  130.7 4.4 %collective-permute-start.25 = (bf16[2,128,64]{2,1,0:T(8,128)(2,1)S(1)}, bf16[2,128,64]{2,1,0:T(8,128)(2,1)S(1)}, u32[]{:S(2)}, u32[]{:S(2)}) collective-permute-start(bf16[2,128,64]{2,1,0:T(8,128)(2,1)S(1)} %get-tuple-element.63), channel_id=1, source_target_pairs={{0,128},{128,0},{1,129},{129,1},{2,130},{130,2},{3,131},{131,3},{4... | collective-permute-start | bytes 98312 | tf_op jit(solution)/shard_map/ppermute | solution.py:25
  (5 other events, 10.8 us)

commit v4 on v3

--- a/solution.py
+++ b/solution.py
@@ -74,30 +74,6 @@
     )(a, b, c)
 
 
-def fetched_kernel(far_up, far_down, near_up, near_down, arrived):
-    copies = [
-        pltpu.make_async_copy(far_up, near_up, arrived.at[0]),
-        pltpu.make_async_copy(far_down, near_down, arrived.at[1]),
-    ]
-    for copy in copies:
-        copy.start()
-    for copy in copies:
-        copy.wait()
-
-
-def fetched(w_up, w_down):
-    return pl.pallas_call(
-        fetched_kernel,
-        in_specs=[pl.BlockSpec(memory_space=pltpu.HBM)] * 2,
-        out_specs=[pl.BlockSpec(memory_space=pltpu.VMEM)] * 2,
-        out_shape=[jax.ShapeDtypeStruct(w.shape, w.dtype) for w in (w_up, w_down)],
-        scratch_shapes=[pltpu.SemaphoreType.DMA((2,))],
-        compiler_params=pltpu.CompilerParams(vmem_limit_bytes=8 * 2**20),
-        cost_estimate=pl.CostEstimate(flops=0, bytes_accessed=8 * 2**20, transcendentals=0),
-        name="fetched",
-    )(w_up, w_down)
-
-
 def in_thirds(value):
     high = value.astype(BF).astype(F32)
     rest = value - high
@@ -105,42 +81,61 @@
     return high, middle, rest - middle
 
 
-def entry_kernel(
-    at_dp, mine, other, gain, shift, w_up, w_down,
-    sent0, sent1, sent2, sent3, scaled, grads, rows, extra, turned, found,
+def half_products(half, tokens, gain, w_up, w_down, found, scaled, extra, turned):
+    width = tokens.shape[2]
+    lane = lax.broadcasted_iota(jnp.int32, (128, 128), 1)
+    columns = jnp.zeros((128, 128), F32)
+    for i in range(2):
+        value = tokens[i].astype(F32)
+        total = jnp.sum(value, 1, keepdims=True)
+        square = jnp.sum(value * value, 1, keepdims=True)
+        columns = jnp.where(lane == 2 * i, total, columns)
+        columns = jnp.where(lane == 2 * i + 1, square, columns)
+        scaled[i * 128 : i * 128 + 128, :] = ((value - total / width) * gain[...]).astype(BF)
+    turned[...] = columns.T
+    for k, third in enumerate(in_thirds(turned[0:4, :])):
+        extra[6 + 4 * half : 10 + 4 * half, k * 128 : k * 128 + 128] = third
+    rows = slice(half * 128, half * 128 + 128)
+    product = jnp.dot(scaled[...], w_up[...], preferred_element_type=F32).astype(BF)
+    for i in range(2):
+        found[i, rows, :] = product[i * 128 : i * 128 + 128]
+    found[2, rows, :] = lax.dot_general(
+        tokens[2], w_down[...], (((1,), (1,)), ((), ())), preferred_element_type=F32
+    ).astype(BF)
+
+
+def first_kernel(
+    mine, gain, shift, far_up, far_down, found, extra, w_up, w_down, scaled, rows, turned, arrived
 ):
-    width = mine.shape[2]
+    copies = [
+        pltpu.make_async_copy(far_up, w_up, arrived.at[0]),
+        pltpu.make_async_copy(far_down, w_down, arrived.at[1]),
+    ]
+    for copy in copies:
+        copy.start()
     extra[...] = jnp.zeros_like(extra)
     rows[...] = jnp.zeros_like(rows)
-    lane = lax.broadcasted_iota(jnp.int32, (128, 128), 1)
-    for half, tokens in enumerate((mine, other)):
-        columns = jnp.zeros((128, 128), F32)
-        for i in range(2):
-            value = tokens[i].astype(F32)
-            total = jnp.sum(value, 1, keepdims=True)
-            square = jnp.sum(value * value, 1, keepdims=True)
-            columns = jnp.where(lane == 2 * i, total, columns)
-            columns = jnp.where(lane == 2 * i + 1, square, columns)
-            scaled[i, half * 128 : half * 128 + 128, :] = (
-                (value - total / width) * gain[...]
-            ).astype(BF)
-        turned[...] = columns.T
-        grads[half * 128 : half * 128 + 128, :] = tokens[2]
-        for k, third in enumerate(in_thirds(turned[0:4, :])):
-            extra[6 + 4 * half : 10 + 4 * half, k * 128 : k * 128 + 128] = third
     for j, vector in enumerate((gain, shift)):
         for k, third in enumerate(in_thirds(vector[...])):
             rows[3 * j + k : 3 * j + k + 1, :] = third
+    for copy in copies:
+        copy.wait()
     sums = jnp.dot(rows[...].astype(BF), w_up[...], preferred_element_type=F32)
     for j in range(2):
         vector = sums[3 * j : 3 * j + 1] + sums[3 * j + 1 : 3 * j + 2] + sums[3 * j + 2 : 3 * j + 3]
         for k, third in enumerate(in_thirds(vector)):
             extra[3 * j + k : 3 * j + k + 1, :] = third
-    for i in range(2):
-        found[i] = jnp.dot(scaled[i], w_up[...], preferred_element_type=F32).astype(BF)
-    found[2] = lax.dot_general(
-        grads[...], w_down[...], (((1,), (1,)), ((), ())), preferred_element_type=F32
-    ).astype(BF)
+    half_products(0, mine, gain, w_up, w_down, found, scaled, extra, turned)
+
+
+def second_kernel(
+    at_dp, found0, extra0, other, gain, w_up, w_down,
+    sent0, sent1, sent2, sent3, scaled, extra, turned, found,
+):
+    extra[...] = extra0[...]
+    for i in range(3):
+        found[i, 0:128, :] = found0[i]
+    half_products(1, other, gain, w_up, w_down, found, scaled, extra, turned)
     for k, sent in enumerate((sent0, sent1, sent2, sent3)):
         row = pl.multiple_of(((at_dp[0] + k) % 4) * 64, 64)
         for i in range(3):
@@ -149,26 +144,44 @@
 
 
 def entry(mine, other, gain, shift, w_up, w_down):
+    held = pl.BlockSpec(memory_space=pltpu.VMEM)
+    params = pltpu.CompilerParams(vmem_limit_bytes=20 * 2**20)
+    cost = pl.CostEstimate(flops=2**30, bytes_accessed=4 * 2**20, transcendentals=0)
+    found, extra, w_up, w_down = pl.pallas_call(
+        first_kernel,
+        in_specs=[held] * 3 + [pl.BlockSpec(memory_space=pltpu.HBM)] * 2,
+        out_specs=[held] * 4,
+        out_shape=[
+            jax.ShapeDtypeStruct((3, 128, 512), BF),
+            jax.ShapeDtypeStruct((16, 512), F32),
+            jax.ShapeDtypeStruct((2048, 512), BF),
+            jax.ShapeDtypeStruct((512, 2048), BF),
+        ],
+        scratch_shapes=[
+            pltpu.VMEM((256, 2048), BF),
+            pltpu.VMEM((8, 2048), F32),
+            pltpu.VMEM((128, 128), F32),
+            pltpu.SemaphoreType.DMA((2,)),
+        ],
+        compiler_params=pltpu.CompilerParams(vmem_limit_bytes=50 * 2**20),
+        cost_estimate=cost,
+        name="first_half",
+    )(mine, gain, shift, w_up, w_down)
     return pl.pallas_call(
-        entry_kernel,
-        in_specs=[pl.BlockSpec(memory_space=pltpu.SMEM)]
-        + [pl.BlockSpec(memory_space=pltpu.VMEM)] * 6,
-        out_specs=[pl.BlockSpec(memory_space=pltpu.VMEM)] * 4,
+        second_kernel,
+        in_specs=[pl.BlockSpec(memory_space=pltpu.SMEM)] + [held] * 6,
+        out_specs=[held] * 4,
         out_shape=[jax.ShapeDtypeStruct((208, 512), BF)] * 4,
         scratch_shapes=[
-            pltpu.VMEM((2, 256, 2048), BF),
             pltpu.VMEM((256, 2048), BF),
-            pltpu.VMEM((8, 2048), F32),
             pltpu.VMEM((16, 512), F32),
             pltpu.VMEM((128, 128), F32),
             pltpu.VMEM((3, 256, 512), BF),
         ],
-        compiler_params=pltpu.CompilerParams(vmem_limit_bytes=28 * 2**20),
-        cost_estimate=pl.CostEstimate(
-            flops=2**31, bytes_accessed=8 * 2**20, transcendentals=0
-        ),
-        name="entry",
-    )(lax.axis_index("dp").reshape(1), mine, other, gain, shift, w_up, w_down)
+        compiler_params=params,
+        cost_estimate=cost,
+        name="second_half",
+    )(lax.axis_index("dp").reshape(1), found, extra, other, gain, w_up, w_down)
 
 
 def middle_kernel(at_dp, part0, part1, part2, part3, bias, quarter, stats, rows):
@@ -339,8 +352,7 @@
     mine = gather_half(together(section_input, saved_input, cotangent))
     other = swapped(mine, "core", 1)
 
-    near_up, near_down = fetched(w_up, w_down)
-    parts = entry(mine, other, gain[None], shift[None], near_up, near_down)
+    parts = entry(mine, other, gain[None], shift[None], w_up, w_down)
     parts = [parts[0]] + [shifted(parts[k], "dp", k) for k in (1, 2, 3)]
     quarter, stats = middle(parts, bias_up[None])
     quarters = [quarter] + [shifted(quarter, "dp", -k) for k in (1, 2, 3)]

time: 137 us -> 139 us (1.015)
  Pallas kernels: 9.87 us -> 13.7 us
  local copies, waits for them, and re-layouts: 7.44 us -> 5.59 us
    pallas_call x2, Pallas kernels: 2.95 us -> 6.79 us  [the longest x1 5.15 us: entry(): pl.pallas_call(first_kernel, in_specs=[held] * 3 + [pl.BlockSpec(memory_s...]
    unnamed x21 -> x19, local copies, waits for them, and re-layouts: 5.02 us -> 3.04 us
  transfers between devices with their start and end apart: 28 -> 28, of which waited for: 19 -> 19; matrix products, arithmetic and copies ran while one was open for 7% -> 7% of each run, Pallas kernels for 0% -> 4%
where the time goes in v4:
time: 139 us; the launch traced here: 138 us
  waiting for transfers between devices  60.3 us (43%)
  starting transfers between devices  48.6 us (35%)
  Pallas kernels  13.7 us (10%)
  local copies, waits for them, and re-layouts  5.59 us (4%)
  other arithmetic  4.97 us (4%)
  matrix products  4.3 us (3%)
    ppermute x16, waiting for transfers between devices, shifted(): lax.ppermute(value, axis, [(i, (i + steps) % count) for i in range(count)])  41.6 us
    ppermute x16, starting transfers between devices, shifted(): lax.ppermute(value, axis, [(i, (i + steps) % count) for i in range(count)])  21.6 us
    ppermute x10, starting transfers between devices, swapped(): return lax.ppermute(value, axis, [(i, i ^ bit) for i in range(count)])  20.8 us
    ppermute x10, waiting for transfers between devices, swapped(): return lax.ppermute(value, axis, [(i, i ^ bit) for i in range(count)])  12.1 us
    all_to_all x1, waiting for transfers between devices, local(): tiles = jnp.sum(lax.all_to_all(kept, 'z', 0, 0, tiled=False).astype(F32), 0)  6.32 us
    pallas_call x1, Pallas kernels, entry(): pl.pallas_call(first_kernel, in_specs=[held] * 3 + [pl.BlockSpec(memory_s...  5.15 us
    pallas_call x1, Pallas kernels, products(): pl.pallas_call(products_kernel, in_specs=[pl.BlockSpec(memory_space=pltpu...  4.97 us
    all_to_all x1, starting transfers between devices, local(): tiles = jnp.sum(lax.all_to_all(kept, 'z', 0, 0, tiled=False).astype(F32), 0)  3.9 us
  transfers between devices with their start and end apart: 28, of which 19 were waited for; matrix products, arithmetic and copies ran while one was open for 7% of the time, Pallas kernels for 4%

profile of v4, /device:TPU:1, one launch (start us, length us, event | category | flops | bytes accessed | tf_op | source)
XLA Modules:
  0.0 138.4 jit_solution(9093668042977875126)
XLA Ops:
  2.1 3.6 %collective-permute-start = (bf16[3,8,2048]{2,1,0:T(8,128)(2,1)}, bf16[3,8,2048]{2,1,0:T(8,128)(2,1)S(1)}, u32[]{:S(2)}, u32[]{:S(2)}) collective-permute-start(bf16[3,8,2048]{2,1,0:T(8,128)(2,1)} %together.1), channel_id=1, source_target_pairs={{0,2},{2,0},{1,3},{3,1},{4,6},{6,4},{5,7},{7,5},{8,10},{10,8},{9,1... | collective-permute-start | bytes 294920 | tf_op jit(solution)/shard_map/ppermute | solution.py:25
  5.6 2.3 %collective-permute-done = bf16[3,8,2048]{2,1,0:T(8,128)(2,1)S(1)} collective-permute-done((bf16[3,8,2048]{2,1,0:T(8,128)(2,1)}, bf16[3,8,2048]{2,1,0:T(8,128)(2,1)S(1)}, u32[]{:S(2)}, u32[]{:S(2)}) %collective-permute-start) | collective-permute-done | bytes 98336 | tf_op jit(solution)/shard_map/ppermute | solution.py:25
  8.9 5.8 %collective-permute-start.1 = (bf16[3,2,8,2048]{3,2,0,1:T(8,128)(2,1)S(1)}, bf16[3,2,8,2048]{3,2,0,1:T(8,128)(2,1)S(1)}, u32[]{:S(2)}, u32[]{:S(2)}) collective-permute-start(bf16[3,2,8,2048]{3,2,0,1:T(8,128)(2,1)S(1)} %maximum_select_fusion.1), channel_id=1, source_target_pairs={{0,28},{4,0},{8,4},{12,8},{16,12},{20,16},{24,20},{28,24},{1,29},{... | collective-permute-start | bytes 589832 | tf_op jit(solution)/shard_map/ppermute | solution.py:20
  15.0 2.4 %collective-permute-done.1 = bf16[3,2,8,2048]{3,2,0,1:T(8,128)(2,1)S(1)} collective-permute-done((bf16[3,2,8,2048]{3,2,0,1:T(8,128)(2,1)S(1)}, bf16[3,2,8,2048]{3,2,0,1:T(8,128)(2,1)S(1)}, u32[]{:S(2)}, u32[]{:S(2)}) %collective-permute-start.1) | collective-permute-done | bytes 196640 | tf_op jit(solution)/shard_map/ppermute | solution.py:20
  17.4 3.1 %collective-permute-start.3 = (bf16[3,2,8,2048]{3,2,0,1:T(8,128)(2,1)S(1)}, bf16[3,2,8,2048]{3,2,0,1:T(8,128)(2,1)S(1)}, u32[]{:S(2)}, u32[]{:S(2)}) collective-permute-start(bf16[3,2,8,2048]{3,2,0,1:T(8,128)(2,1)S(1)} %collective-permute-done.1), channel_id=1, source_target_pairs={{0,28},{4,0},{8,4},{12,8},{16,12},{20,16},{24,20},{28,24},{1,29},{... | collective-permute-start | bytes 589832 | tf_op jit(solution)/shard_map/ppermute | solution.py:20
  20.5 2.6 %collective-permute-done.3 = bf16[3,2,8,2048]{3,2,0,1:T(8,128)(2,1)S(1)} collective-permute-done((bf16[3,2,8,2048]{3,2,0,1:T(8,128)(2,1)S(1)}, bf16[3,2,8,2048]{3,2,0,1:T(8,128)(2,1)S(1)}, u32[]{:S(2)}, u32[]{:S(2)}) %collective-permute-start.3) | collective-permute-done | bytes 196640 | tf_op jit(solution)/shard_map/ppermute | solution.py:20
  23.1 3.1 %collective-permute-start.5 = (bf16[3,2,8,2048]{3,2,0,1:T(8,128)(2,1)S(1)}, bf16[3,2,8,2048]{3,2,0,1:T(8,128)(2,1)S(1)}, u32[]{:S(2)}, u32[]{:S(2)}) collective-permute-start(bf16[3,2,8,2048]{3,2,0,1:T(8,128)(2,1)S(1)} %collective-permute-done.3), channel_id=1, source_target_pairs={{0,28},{4,0},{8,4},{12,8},{16,12},{20,16},{24,20},{28,24},{1,29},{... | collective-permute-start | bytes 589832 | tf_op jit(solution)/shard_map/ppermute | solution.py:20
  26.3 5.8 %collective-permute-done.6 = bf16[3,2,8,2048]{3,2,0,1:T(8,128)(2,1)S(1)} collective-permute-done((bf16[3,2,8,2048]{3,2,0,1:T(8,128)(2,1)S(1)}, bf16[3,2,8,2048]{3,2,0,1:T(8,128)(2,1)S(1)}, u32[]{:S(2)}, u32[]{:S(2)}) %collective-permute-start.6) | collective-permute-done | bytes 196640 | tf_op jit(solution)/shard_map/ppermute | solution.py:20
  32.1 6.8 %collective-permute-done.7 = bf16[3,2,8,2048]{3,2,0,1:T(8,128)(2,1)S(1)} collective-permute-done((bf16[3,2,8,2048]{3,2,0,1:T(8,128)(2,1)S(1)}, bf16[3,2,8,2048]{3,2,0,1:T(8,128)(2,1)S(1)}, u32[]{:S(2)}, u32[]{:S(2)}) %collective-permute-start.7) | collective-permute-done | bytes 196640 | tf_op jit(solution)/shard_map/ppermute | solution.py:20
  38.9 6.7 %collective-permute-start.8 = (bf16[3,128,2048]{2,1,0:T(8,128)(2,1)S(1)}, bf16[3,128,2048]{2,1,0:T(8,128)(2,1)S(1)}, u32[]{:S(2)}, u32[]{:S(2)}) collective-permute-start(bf16[3,128,2048]{2,1,0:T(8,128)(2,1)S(1)} %bitcast.101), channel_id=1, source_target_pairs={{0,1},{1,0},{2,3},{3,2},{4,5},{5,4},{6,7},{7,6},{8,9},{9,8},{10,11... | collective-permute-start | bytes 4718600 | tf_op jit(solution)/shard_map/ppermute | solution.py:25
  45.7 5.1 %first_half.1 = (bf16[3,128,512]{2,1,0:T(8,128)(2,1)S(1)}, f32[16,512]{1,0:T(8,128)S(1)}, bf16[2048,512]{1,0:T(8,128)(2,1)S(1)}, bf16[512,2048]{1,0:T(8,128)(2,1)}) custom-call(bf16[3,128,2048]{2,1,0:T(8,128)(2,1)S(1)} %bitcast.102, f32[1,2048]{1,0:T(1,128)S(1)} %copy-done.1, f32[1,2048]{1,0:T(1,128)S(1)} %copy-done.2, bf16[2048,512]{1,0:T(8,128)(2,1)} %bitcast.106, ...), custom_call_target="tpu_custom_call" | custom-call | flops 1073741824 | bytes 4194304 | tf_op jit(solution)/shard_map/first_half/pallas_call | solution.py:150
  52.4 1.6 %second_half.1 = (bf16[208,512]{1,0:T(8,128)(2,1)S(1)}, bf16[208,512]{1,0:T(8,128)(2,1)S(1)}, bf16[208,512]{1,0:T(8,128)(2,1)S(1)}, bf16[208,512]{1,0:T(8,128)(2,1)S(1)}) custom-call(s32[1]{0:T(128)} %bitcast.12.at_dp, bf16[3,128,512]{2,1,0:T(8,128)(2,1)S(1)} %get-tuple-element.27.found0, f32[16,512]{1,0:T(8,128)S(1)} %get-tuple-element.28.extra0, ...), custom_call_target="tpu_custom_call" | custom-call | flops 1073741824 | bytes 4194304 | tf_op jit(solution)/shard_map/second_half/pallas_call | solution.py:170
  55.5 2.6 %collective-permute-start.10 = (bf16[208,512]{1,0:T(8,128)(2,1)S(1)}, bf16[208,512]{1,0:T(8,128)(2,1)S(1)}, u32[]{:S(2)}, u32[]{:S(2)}) collective-permute-start(bf16[208,512]{1,0:T(8,128)(2,1)S(1)} %get-tuple-element.33), channel_id=1, source_target_pairs={{0,64},{32,96},{64,0},{96,32},{1,65},{33,97},{65,1},{97,33},{2,66}... | collective-permute-start | bytes 638984 | tf_op jit(solution)/shard_map/ppermute | solution.py:20
  59.2 3.2 %collective-permute-done.9.part1 = bf16[208,512]{1,0:T(8,128)(2,1)S(1)} collective-permute-done((bf16[208,512]{1,0:T(8,128)(2,1)S(1)}, bf16[208,512]{1,0:T(8,128)(2,1)S(1)}, u32[]{:S(2)}, u32[]{:S(2)}) %collective-permute-start.9) | collective-permute-done | bytes 213024 | tf_op jit(solution)/shard_map/ppermute | solution.py:20
  62.4 5.7 %collective-permute-done.10.part2 = bf16[208,512]{1,0:T(8,128)(2,1)S(1)} collective-permute-done((bf16[208,512]{1,0:T(8,128)(2,1)S(1)}, bf16[208,512]{1,0:T(8,128)(2,1)S(1)}, u32[]{:S(2)}, u32[]{:S(2)}) %collective-permute-start.10) | collective-permute-done | bytes 213024 | tf_op jit(solution)/shard_map/ppermute | solution.py:20
  68.5 2.3 %collective-permute-start.12 = (bf16[3,64,512]{2,1,0:T(8,128)(2,1)S(1)}, bf16[3,64,512]{2,1,0:T(8,128)(2,1)}, u32[]{:S(2)}, u32[]{:S(2)}) collective-permute-start(bf16[3,64,512]{2,1,0:T(8,128)(2,1)S(1)} %get-tuple-element.35.own), channel_id=1, source_target_pairs={{0,96},{32,0},{64,32},{96,64},{1,97},{33,1},{65,33},{97,65},{2,98}... | collective-permute-start | bytes 589832 | tf_op jit(solution)/shard_map/ppermute | solution.py:20
  71.5 4.0 %collective-permute-done.12.next1 = bf16[3,64,512]{2,1,0:T(8,128)(2,1)} collective-permute-done((bf16[3,64,512]{2,1,0:T(8,128)(2,1)S(1)}, bf16[3,64,512]{2,1,0:T(8,128)(2,1)}, u32[]{:S(2)}, u32[]{:S(2)}) %collective-permute-start.12) | collective-permute-done | bytes 196640 | tf_op jit(solution)/shard_map/ppermute | solution.py:20
  75.6 2.6 %collective-permute-done.13.next2 = bf16[3,64,512]{2,1,0:T(8,128)(2,1)} collective-permute-done((bf16[3,64,512]{2,1,0:T(8,128)(2,1)S(1)}, bf16[3,64,512]{2,1,0:T(8,128)(2,1)}, u32[]{:S(2)}, u32[]{:S(2)}) %collective-permute-start.13) | collective-permute-done | bytes 196640 | tf_op jit(solution)/shard_map/ppermute | solution.py:20
  78.2 5.1 %collective-permute-done.14.next3 = bf16[3,64,512]{2,1,0:T(8,128)(2,1)} collective-permute-done((bf16[3,64,512]{2,1,0:T(8,128)(2,1)S(1)}, bf16[3,64,512]{2,1,0:T(8,128)(2,1)}, u32[]{:S(2)}, u32[]{:S(2)}) %collective-permute-start.14) | collective-permute-done | bytes 196640 | tf_op jit(solution)/shard_map/ppermute | solution.py:20
  83.3 5.0 %products.1 = (f32[8,2,2,128,128]{4,3,2,1,0:T(8,128)S(1)}, bf16[8,2,2,128,128]{4,3,2,1,0:T(8,128)(2,1)S(1)}, bf16[3,256,512]{2,1,0:T(8,128)(2,1)S(1)}, f32[1,512...) custom-call(s32[1]{0:T(128)} %bitcast.12.at_dp, bf16[3,64,512]{2,1,0:T(8,128)(2,1)S(1)} %get-tuple-element.35.own, ...), custom_call_target="tpu_custom_call" | custom-call | flops 2147483648 | bytes 10485760 | tf_op jit(solution)/shard_map/products/pallas_call | solution.py:296
  90.4 2.3 %collective-permute-done.17 = f32[2,2304]{1,0:T(2,128)S(1)} collective-permute-done((f32[2,2304]{1,0:T(2,128)S(1)}, f32[2,2304]{1,0:T(2,128)S(1)}, u32[]{:S(2)}, u32[]{:S(2)}) %collective-permute-start.17) | collective-permute-done | bytes 18464 | tf_op jit(solution)/shard_map/ppermute | solution.py:25
  93.4 2.8 %collective-permute-start.16 = (bf16[8,2,128,128]{3,2,1,0:T(8,128)(2,1)S(1)}, bf16[8,2,128,128]{3,2,1,0:T(8,128)(2,1)S(1)}, u32[]{:S(2)}, u32[]{:S(2)}) collective-permute-start(bf16[8,2,128,128]{3,2,1,0:T(8,128)(2,1)S(1)} %fusion.8), channel_id=1, source_target_pairs={{0,2},{2,0},{1,3},{3,1},{4,6},{6,4},{5,7},{7,5},{8,10},{10,8},{9,1... | collective-permute-start | bytes 1572872 | tf_op jit(solution)/shard_map/ppermute | solution.py:25
  96.2 2.3 %convolution_convert_fusion.1 = bf16[2048,512]{1,0:T(8,128)(2,1)} fusion(bf16[128,2048]{1,0:T(8,128)(2,1)S(1)} %get-tuple-element.62, bf16[128,2048]{1,0:T(8,128)(2,1)S(1)} %bitcast.117, f32[2048]{0:T(1024)S(1)} %bitcast.105, f32[2048]{0:T(1024)S(1)} %bitcast.104, f32[256]{0:T(256)S(1)} %get-tuple-element.57, f32[256]{0:T(256)S(1)} %get-tuple-element.56, ...), kind=kOutput, calls=%fused_computation.1 | convolution fusion | flops 542638080 | bytes 3426304 | tf_op jit(solution)/shard_map/dot_general | solution.py:376
  99.6 2.1 %convolution_convert_fusion = bf16[512,2048]{1,0:T(8,128)(2,1)} fusion(bf16[128,2048]{1,0:T(8,128)(2,1)S(1)} %get-tuple-element.61, bf16[128,2048]{1,0:T(8,128)(2,1)S(1)} %bitcast.110, bf16[3,256,512]{2,1,0:T(8,128)(2,1)S(1)} %get-tuple-element.39), kind=kOutput, calls=%fused_computation | convolution fusion | flops 540016640 | bytes 3407872 | tf_op jit(solution)/shard_map/dot_general | solution.py:372
  101.7 3.4 %collective-permute-done.19 = f32[2,2304]{1,0:T(2,128)S(1)} collective-permute-done((f32[2,2304]{1,0:T(2,128)S(1)}, f32[2,2304]{1,0:T(2,128)S(1)}, u32[]{:S(2)}, u32[]{:S(2)}) %collective-permute-start.19) | collective-permute-done | bytes 18464 | tf_op jit(solution)/shard_map/ppermute | solution.py:25
  105.1 2.7 %collective-permute-start.20 = (f32[2,2176]{1,0:T(2,128)S(1)}, f32[2,2176]{1,0:T(2,128)S(1)}, u32[]{:S(2)}, u32[]{:S(2)}) collective-permute-start(f32[2,2176]{1,0:T(2,128)S(1)} %slice.125), channel_id=1, source_target_pairs={{0,1},{1,0},{2,3},{3,2},{4,5},{5,4},{6,7},{7,6},{8,9},{9,8},{10,11... | collective-permute-start | bytes 52232 | tf_op jit(solution)/shard_map/ppermute | solution.py:25
  108.7 3.9 %all-to-all-start = ((bf16[8,2,128,128]{3,2,1,0:T(8,128)(2,1)}), bf16[8,2,128,128]{3,2,1,0:T(8,128)(2,1)S(1)}, u32[]{:S(2)}, u32[]{:S(2)}) async-start(bf16[8,2,128,128]{3,2,1,0:T(8,128)(2,1)} %fusion.3), calls=%async_computation | async-start | bytes 1048576 | tf_op jit(solution)/shard_map/all_to_all | solution.py:382
  112.7 1.8 %collective-permute-start.21 = (f32[2,2176]{1,0:T(2,128)S(1)}, f32[2,2176]{1,0:T(2,128)S(1)}, u32[]{:S(2)}, u32[]{:S(2)}) collective-permute-start(f32[2,2176]{1,0:T(2,128)S(1)} %maximum_add_fusion), channel_id=1, source_target_pairs={{0,2},{2,0},{1,3},{3,1},{4,6},{6,4},{5,7},{7,5},{8,10},{10,8},{9,1... | collective-permute-start | bytes 52232 | tf_op jit(solution)/shard_map/ppermute | solution.py:25
  119.7 1.9 %collective-permute-done.23 = f32[2,128]{1,0:T(2,128)S(1)} collective-permute-done((f32[2,128]{1,0:T(2,128)S(1)}, f32[2,128]{1,0:T(2,128)S(1)}, u32[]{:S(2)}, u32[]{:S(2)}) %collective-permute-start.23) | collective-permute-done | bytes 1056 | tf_op jit(solution)/shard_map/ppermute | solution.py:20
  122.7 6.3 %all-to-all-done = bf16[8,2,128,128]{3,2,1,0:T(8,128)(2,1)S(1)} async-done(((bf16[8,2,128,128]{3,2,1,0:T(8,128)(2,1)}), bf16[8,2,128,128]{3,2,1,0:T(8,128)(2,1)S(1)}, u32[]{:S(2)}, u32[]{:S(2)}) %all-to-all-start) | async-done | bytes 524320 | tf_op jit(solution)/shard_map/all_to_all | solution.py:382
  130.2 2.3 %collective-permute-start.26 = (bf16[2,128,64]{2,1,0:T(8,128)(2,1)S(1)}, bf16[2,128,64]{2,1,0:T(8,128)(2,1)S(1)}, u32[]{:S(2)}, u32[]{:S(2)}) collective-permute-start(bf16[2,128,64]{2,1,0:T(8,128)(2,1)S(1)} %get-tuple-element.68), channel_id=1, source_target_pairs={{0,129},{1,128},{128,1},{129,0},{2,131},{3,130},{130,3},{131,2},{4... | collective-permute-start | bytes 98312 | tf_op jit(solution)/shard_map/ppermute | solution.py:329
  134.4 2.5 %collective-permute-done.25 = bf16[2,128,64]{2,1,0:T(8,128)(2,1)S(1)} collective-permute-done((bf16[2,128,64]{2,1,0:T(8,128)(2,1)S(1)}, bf16[2,128,64]{2,1,0:T(8,128)(2,1)S(1)}, u32[]{:S(2)}, u32[]{:S(2)}) %collective-permute-start.25) | collective-permute-done | bytes 32800 | tf_op jit(solution)/shard_map/ppermute | solution.py:25
  (87 shorter events, 23.6 us)
Async XLA Ops:
  2.1 5.9 %collective-permute-start = (bf16[3,8,2048]{2,1,0:T(8,128)(2,1)}, bf16[3,8,2048]{2,1,0:T(8,128)(2,1)S(1)}, u32[]{:S(2)}, u32[]{:S(2)}) collective-permute-start(bf16[3,8,2048]{2,1,0:T(8,128)(2,1)} %together.1), channel_id=1, source_target_pairs={{0,2},{2,0},{1,3},{3,1},{4,6},{6,4},{5,7},{7,5},{8,10},{10,8},{9,1... | collective-permute-start | bytes 294920 | tf_op jit(solution)/shard_map/ppermute | solution.py:25
  8.9 8.4 %collective-permute-start.1 = (bf16[3,2,8,2048]{3,2,0,1:T(8,128)(2,1)S(1)}, bf16[3,2,8,2048]{3,2,0,1:T(8,128)(2,1)S(1)}, u32[]{:S(2)}, u32[]{:S(2)}) collective-permute-start(bf16[3,2,8,2048]{3,2,0,1:T(8,128)(2,1)S(1)} %maximum_select_fusion.1), channel_id=1, source_target_pairs={{0,28},{4,0},{8,4},{12,8},{16,12},{20,16},{24,20},{28,24},{1,29},{... | collective-permute-start | bytes 589832 | tf_op jit(solution)/shard_map/ppermute | solution.py:20
  14.7 5.7 %collective-permute-start.2 = (bf16[3,2,8,2048]{3,2,0,1:T(8,128)(2,1)S(1)}, bf16[3,2,8,2048]{3,2,0,1:T(8,128)(2,1)S(1)}, u32[]{:S(2)}, u32[]{:S(2)}) collective-permute-start(bf16[3,2,8,2048]{3,2,0,1:T(8,128)(2,1)S(1)} %maximum_select_fusion.1), channel_id=1, source_target_pairs={{0,4},{4,8},{8,12},{12,16},{16,20},{20,24},{24,28},{28,0},{1,5},{5... | collective-permute-start | bytes 589832 | tf_op jit(solution)/shard_map/ppermute | solution.py:20
  14.7 30.9 %copy-start.1 = (f32[1,2048]{1,0:T(1,128)S(1)}, f32[1,2048]{1,0:T(1,128)}, u32[]{:S(2)}) copy-start(f32[1,2048]{1,0:T(1,128)} %gain.5) | copy-start | bytes 24580
  14.7 30.9 %copy-start.2 = (f32[1,2048]{1,0:T(1,128)S(1)}, f32[1,2048]{1,0:T(1,128)}, u32[]{:S(2)}) copy-start(f32[1,2048]{1,0:T(1,128)} %shift.1) | copy-start | bytes 24580
  17.4 5.7 %collective-permute-start.3 = (bf16[3,2,8,2048]{3,2,0,1:T(8,128)(2,1)S(1)}, bf16[3,2,8,2048]{3,2,0,1:T(8,128)(2,1)S(1)}, u32[]{:S(2)}, u32[]{:S(2)}) collective-permute-start(bf16[3,2,8,2048]{3,2,0,1:T(8,128)(2,1)S(1)} %collective-permute-done.1), channel_id=1, source_target_pairs={{0,28},{4,0},{8,4},{12,8},{16,12},{20,16},{24,20},{28,24},{1,29},{... | collective-permute-start | bytes 589832 | tf_op jit(solution)/shard_map/ppermute | solution.py:20
  20.5 5.7 %collective-permute-start.4 = (bf16[3,2,8,2048]{3,2,0,1:T(8,128)(2,1)S(1)}, bf16[3,2,8,2048]{3,2,0,1:T(8,128)(2,1)S(1)}, u32[]{:S(2)}, u32[]{:S(2)}) collective-permute-start(bf16[3,2,8,2048]{3,2,0,1:T(8,128)(2,1)S(1)} %collective-permute-done.2), channel_id=1, source_target_pairs={{0,4},{4,8},{8,12},{12,16},{16,20},{20,24},{24,28},{28,0},{1,5},{5... | collective-permute-start | bytes 589832 | tf_op jit(solution)/shard_map/ppermute | solution.py:20
  23.1 8.9 %collective-permute-start.5 = (bf16[3,2,8,2048]{3,2,0,1:T(8,128)(2,1)S(1)}, bf16[3,2,8,2048]{3,2,0,1:T(8,128)(2,1)S(1)}, u32[]{:S(2)}, u32[]{:S(2)}) collective-permute-start(bf16[3,2,8,2048]{3,2,0,1:T(8,128)(2,1)S(1)} %collective-permute-done.3), channel_id=1, source_target_pairs={{0,28},{4,0},{8,4},{12,8},{16,12},{20,16},{24,20},{28,24},{1,29},{... | collective-permute-start | bytes 589832 | tf_op jit(solution)/shard_map/ppermute | solution.py:20
  26.2 5.8 %collective-permute-start.6 = (bf16[3,2,8,2048]{3,2,0,1:T(8,128)(2,1)S(1)}, bf16[3,2,8,2048]{3,2,0,1:T(8,128)(2,1)S(1)}, u32[]{:S(2)}, u32[]{:S(2)}) collective-permute-start(bf16[3,2,8,2048]{3,2,0,1:T(8,128)(2,1)S(1)} %collective-permute-done.4), channel_id=1, source_target_pairs={{0,4},{4,8},{8,12},{12,16},{16,20},{20,24},{24,28},{28,0},{1,5},{5... | collective-permute-start | bytes 589832 | tf_op jit(solution)/shard_map/ppermute | solution.py:20
  32.0 6.9 %collective-permute-start.7 = (bf16[3,2,8,2048]{3,2,0,1:T(8,128)(2,1)S(1)}, bf16[3,2,8,2048]{3,2,0,1:T(8,128)(2,1)S(1)}, u32[]{:S(2)}, u32[]{:S(2)}) collective-permute-start(bf16[3,2,8,2048]{3,2,0,1:T(8,128)(2,1)S(1)} %collective-permute-done.6), channel_id=1, source_target_pairs={{0,4},{4,8},{8,12},{12,16},{16,20},{20,24},{24,28},{28,0},{1,5},{5... | collective-permute-start | bytes 589832 | tf_op jit(solution)/shard_map/ppermute | solution.py:20
  38.9 11.9 %collective-permute-start.8 = (bf16[3,128,2048]{2,1,0:T(8,128)(2,1)S(1)}, bf16[3,128,2048]{2,1,0:T(8,128)(2,1)S(1)}, u32[]{:S(2)}, u32[]{:S(2)}) collective-permute-start(bf16[3,128,2048]{2,1,0:T(8,128)(2,1)S(1)} %bitcast.101), channel_id=1, source_target_pairs={{0,1},{1,0},{2,3},{3,2},{4,5},{5,4},{6,7},{7,6},{8,9},{9,8},{10,11... | collective-permute-start | bytes 4718600 | tf_op jit(solution)/shard_map/ppermute | solution.py:25
  52.4 15.6 %copy-start.3 = (f32[1,512]{1,0:T(1,128)S(1)}, f32[1,512]{1,0:T(1,128)}, u32[]{:S(2)}) copy-start(f32[1,512]{1,0:T(1,128)} %bias.1) | copy-start | bytes 6148
  54.1 8.3 %collective-permute-start.9 = (bf16[208,512]{1,0:T(8,128)(2,1)S(1)}, bf16[208,512]{1,0:T(8,128)(2,1)S(1)}, u32[]{:S(2)}, u32[]{:S(2)}) collective-permute-start(bf16[208,512]{1,0:T(8,128)(2,1)S(1)} %get-tuple-element.32), channel_id=1, source_target_pairs={{0,32},{32,64},{64,96},{96,0},{1,33},{33,65},{65,97},{97,1},{2,34}... | collective-permute-start | bytes 638984 | tf_op jit(solution)/shard_map/ppermute | solution.py:20
  55.5 12.6 %collective-permute-start.10 = (bf16[208,512]{1,0:T(8,128)(2,1)S(1)}, bf16[208,512]{1,0:T(8,128)(2,1)S(1)}, u32[]{:S(2)}, u32[]{:S(2)}) collective-permute-start(bf16[208,512]{1,0:T(8,128)(2,1)S(1)} %get-tuple-element.33), channel_id=1, source_target_pairs={{0,64},{32,96},{64,0},{96,32},{1,65},{33,97},{65,1},{97,33},{2,66}... | collective-permute-start | bytes 638984 | tf_op jit(solution)/shard_map/ppermute | solution.py:20
  58.1 9.9 %collective-permute-start.11 = (bf16[208,512]{1,0:T(8,128)(2,1)S(1)}, bf16[208,512]{1,0:T(8,128)(2,1)S(1)}, u32[]{:S(2)}, u32[]{:S(2)}) collective-permute-start(bf16[208,512]{1,0:T(8,128)(2,1)S(1)} %get-tuple-element.34), channel_id=1, source_target_pairs={{0,96},{32,0},{64,32},{96,64},{1,97},{33,1},{65,33},{97,65},{2,98}... | collective-permute-start | bytes 638984 | tf_op jit(solution)/shard_map/ppermute | solution.py:20
  68.5 7.0 %collective-permute-start.12 = (bf16[3,64,512]{2,1,0:T(8,128)(2,1)S(1)}, bf16[3,64,512]{2,1,0:T(8,128)(2,1)}, u32[]{:S(2)}, u32[]{:S(2)}) collective-permute-start(bf16[3,64,512]{2,1,0:T(8,128)(2,1)S(1)} %get-tuple-element.35.own), channel_id=1, source_target_pairs={{0,96},{32,0},{64,32},{96,64},{1,97},{33,1},{65,33},{97,65},{2,98}... | collective-permute-start | bytes 589832 | tf_op jit(solution)/shard_map/ppermute | solution.py:20
  70.8 7.4 %collective-permute-start.13 = (bf16[3,64,512]{2,1,0:T(8,128)(2,1)S(1)}, bf16[3,64,512]{2,1,0:T(8,128)(2,1)}, u32[]{:S(2)}, u32[]{:S(2)}) collective-permute-start(bf16[3,64,512]{2,1,0:T(8,128)(2,1)S(1)} %get-tuple-element.35.own), channel_id=1, source_target_pairs={{0,64},{32,96},{64,0},{96,32},{1,65},{33,97},{65,1},{97,33},{2,66}... | collective-permute-start | bytes 589832 | tf_op jit(solution)/shard_map/ppermute | solution.py:20
  71.0 12.2 %collective-permute-start.14 = (bf16[3,64,512]{2,1,0:T(8,128)(2,1)S(1)}, bf16[3,64,512]{2,1,0:T(8,128)(2,1)}, u32[]{:S(2)}, u32[]{:S(2)}) collective-permute-start(bf16[3,64,512]{2,1,0:T(8,128)(2,1)S(1)} %get-tuple-element.35.own), channel_id=1, source_target_pairs={{0,32},{32,64},{64,96},{96,0},{1,33},{33,65},{65,97},{97,1},{2,34}... | collective-permute-start | bytes 589832 | tf_op jit(solution)/shard_map/ppermute | solution.py:20
  88.3 4.6 %collective-permute-start.15 = (bf16[8,2,2,128,128]{4,3,2,1,0:T(8,128)(2,1)S(1)}, bf16[8,2,2,128,128]{4,3,2,1,0:T(8,128)(2,1)S(1)}, u32[]{:S(2)}, u32[]{:S(2)}) collective-permute-start(bf16[8,2,2,128,128]{4,3,2,1,0:T(8,128)(2,1)S(1)} %get-tuple-element.38), channel_id=1, source_target_pairs={{0,1},{1,0},{2,3},{3,2},{4,5},{5,4},{6,7},{7,6},{8,9},{9,8},{10,11... | collective-permute-start | bytes 3145736 | tf_op jit(solution)/shard_map/ppermute | solution.py:25
  90.1 2.7 %collective-permute-start.17 = (f32[2,2304]{1,0:T(2,128)S(1)}, f32[2,2304]{1,0:T(2,128)S(1)}, u32[]{:S(2)}, u32[]{:S(2)}) collective-permute-start(f32[2,2304]{1,0:T(2,128)S(1)} %constant_dynamic-update-slice_fusion), channel_id=1, source_target_pairs={{0,4},{4,0},{8,12},{12,8},{16,20},{20,16},{24,28},{28,24},{1,5},{5... | collective-permute-start | bytes 55304 | tf_op jit(solution)/shard_map/ppermute | solution.py:25
  92.8 5.7 %collective-permute-start.18 = (f32[2,2304]{1,0:T(2,128)S(1)}, f32[2,2304]{1,0:T(2,128)S(1)}, u32[]{:S(2)}, u32[]{:S(2)}) collective-permute-start(f32[2,2304]{1,0:T(2,128)S(1)} %add.177), channel_id=1, source_target_pairs={{0,8},{4,12},{8,0},{12,4},{16,24},{20,28},{24,16},{28,20},{1,9},{5... | collective-permute-start | bytes 55304 | tf_op jit(solution)/shard_map/ppermute | solution.py:25
  93.4 14.4 %collective-permute-start.16 = (bf16[8,2,128,128]{3,2,1,0:T(8,128)(2,1)S(1)}, bf16[8,2,128,128]{3,2,1,0:T(8,128)(2,1)S(1)}, u32[]{:S(2)}, u32[]{:S(2)}) collective-permute-start(bf16[8,2,128,128]{3,2,1,0:T(8,128)(2,1)S(1)} %fusion.8), channel_id=1, source_target_pairs={{0,2},{2,0},{1,3},{3,1},{4,6},{6,4},{5,7},{7,5},{8,10},{10,8},{9,1... | collective-permute-start | bytes 1572872 | tf_op jit(solution)/shard_map/ppermute | solution.py:25
  98.5 6.6 %collective-permute-start.19 = (f32[2,2304]{1,0:T(2,128)S(1)}, f32[2,2304]{1,0:T(2,128)S(1)}, u32[]{:S(2)}, u32[]{:S(2)}) collective-permute-start(f32[2,2304]{1,0:T(2,128)S(1)} %add.178), channel_id=1, source_target_pairs={{0,16},{4,20},{8,24},{12,28},{16,0},{20,4},{24,8},{28,12},{1,17},{... | collective-permute-start | bytes 55304 | tf_op jit(solution)/shard_map/ppermute | solution.py:25
  101.7 12.9 %copy-start.5 = (bf16[1,8,2,8,2048]{4,3,2,1,0:T(8,128)(2,1)S(1)}, bf16[1,8,2,8,2048]{4,3,2,1,0:T(8,128)(2,1)}, u32[]{:S(2)}) copy-start(bf16[1,8,2,8,2048]{4,3,2,1,0:T(8,128)(2,1)} %copy-done.4) | copy-start | bytes 1572868
  105.1 7.5 %collective-permute-start.20 = (f32[2,2176]{1,0:T(2,128)S(1)}, f32[2,2176]{1,0:T(2,128)S(1)}, u32[]{:S(2)}, u32[]{:S(2)}) collective-permute-start(f32[2,2176]{1,0:T(2,128)S(1)} %slice.125), channel_id=1, source_target_pairs={{0,1},{1,0},{2,3},{3,2},{4,5},{5,4},{6,7},{7,6},{8,9},{9,8},{10,11... | collective-permute-start | bytes 52232 | tf_op jit(solution)/shard_map/ppermute | solution.py:25
  108.7 20.3 %all-to-all-start = ((bf16[8,2,128,128]{3,2,1,0:T(8,128)(2,1)}), bf16[8,2,128,128]{3,2,1,0:T(8,128)(2,1)S(1)}, u32[]{:S(2)}, u32[]{:S(2)}) async-start(bf16[8,2,128,128]{3,2,1,0:T(8,128)(2,1)} %fusion.3), calls=%async_computation | async-start | bytes 1048576 | tf_op jit(solution)/shard_map/all_to_all | solution.py:382
  112.7 4.2 %collective-permute-start.21 = (f32[2,2176]{1,0:T(2,128)S(1)}, f32[2,2176]{1,0:T(2,128)S(1)}, u32[]{:S(2)}, u32[]{:S(2)}) collective-permute-start(f32[2,2176]{1,0:T(2,128)S(1)} %maximum_add_fusion), channel_id=1, source_target_pairs={{0,2},{2,0},{1,3},{3,1},{4,6},{6,4},{5,7},{7,5},{8,10},{10,8},{9,1... | collective-permute-start | bytes 52232 | tf_op jit(solution)/shard_map/ppermute | solution.py:25
  116.9 2.8 %collective-permute-start.24 = (f32[2,128]{1,0:T(2,128)S(1)}, f32[2,128]{1,0:T(2,128)S(1)}, u32[]{:S(2)}, u32[]{:S(2)}) collective-permute-start(f32[2,128]{1,0:T(2,128)S(1)} %slice.126), channel_id=1, source_target_pairs={{0,96},{32,0},{64,32},{96,64},{1,97},{33,1},{65,33},{97,65},{2,98}... | collective-permute-start | bytes 3080 | tf_op jit(solution)/shard_map/ppermute | solution.py:20
  117.4 4.2 %collective-permute-start.23 = (f32[2,128]{1,0:T(2,128)S(1)}, f32[2,128]{1,0:T(2,128)S(1)}, u32[]{:S(2)}, u32[]{:S(2)}) collective-permute-start(f32[2,128]{1,0:T(2,128)S(1)} %slice.126), channel_id=1, source_target_pairs={{0,64},{32,96},{64,0},{96,32},{1,65},{33,97},{65,1},{97,33},{2,66}... | collective-permute-start | bytes 3080 | tf_op jit(solution)/shard_map/ppermute | solution.py:20
  117.6 4.5 %collective-permute-start.22 = (f32[2,128]{1,0:T(2,128)S(1)}, f32[2,128]{1,0:T(2,128)S(1)}, u32[]{:S(2)}, u32[]{:S(2)}) collective-permute-start(f32[2,128]{1,0:T(2,128)S(1)} %slice.126), channel_id=1, source_target_pairs={{0,32},{32,64},{64,96},{96,0},{1,33},{33,65},{65,97},{97,1},{2,34}... | collective-permute-start | bytes 3080 | tf_op jit(solution)/shard_map/ppermute | solution.py:20
  130.2 4.3 %collective-permute-start.26 = (bf16[2,128,64]{2,1,0:T(8,128)(2,1)S(1)}, bf16[2,128,64]{2,1,0:T(8,128)(2,1)S(1)}, u32[]{:S(2)}, u32[]{:S(2)}) collective-permute-start(bf16[2,128,64]{2,1,0:T(8,128)(2,1)S(1)} %get-tuple-element.68), channel_id=1, source_target_pairs={{0,129},{1,128},{128,1},{129,0},{2,131},{3,130},{130,3},{131,2},{4... | collective-permute-start | bytes 98312 | tf_op jit(solution)/shard_map/ppermute | solution.py:329
  132.5 4.4 %collective-permute-start.25 = (bf16[2,128,64]{2,1,0:T(8,128)(2,1)S(1)}, bf16[2,128,64]{2,1,0:T(8,128)(2,1)S(1)}, u32[]{:S(2)}, u32[]{:S(2)}) collective-permute-start(bf16[2,128,64]{2,1,0:T(8,128)(2,1)S(1)} %get-tuple-element.67), channel_id=1, source_target_pairs={{0,128},{128,0},{1,129},{129,1},{2,130},{130,2},{3,131},{131,3},{4... | collective-permute-start | bytes 98312 | tf_op jit(solution)/shard_map/ppermute | solution.py:25
  (4 other events, 30.4 us)
